TPU v7x, 128 devices: a whole 4x4x4 slice. The times are simulated.
128 devices in a mesh: slide: 8 (over z, core), tile: 16 (over y, x).
Axes of the slice: x: 4, y: 4, z: 4, core: 2. Of those that a mesh axis runs over, the one named last changes fastest.
Arguments:
- tile_features: bfloat16 [49152, 1536], P(('slide', 'tile')), may hold values from -8 to 8
- embed_weight: bfloat16 [1536, 768], replicated, may hold values from -0.15625 to 0.15625
- qkv_weight: bfloat16 [768, 2304], replicated, may hold values from -0.21875 to 0.21875
- positions: int32 [49152], P(('slide', 'tile')), may hold values from -1 to 16383, as said below
- out_grad: bfloat16 [4, 4096, 768], P(None, 'slide', 'tile'), may hold values from -48 to 48
Outputs:
- feature_grad: bfloat16 [49152, 1536], P(('slide', 'tile'))
- embed_grad: float32 [1536, 768], P('slide', 'tile')
- qkv_grad: float32 [768, 2304], P('slide', 'tile')
Inputs may be any that keep to these rules, and one draw needn't show every extreme that they name: Every position 0 to 16383 is held by exactly one slot; -1 marks an empty slot. A device's live slots come first. A device holds 384, 128 or 64 live tiles, some devices 384 in every draw, and sends the same number to each segment row r (positions whose offset in their slide lies in [r * 512, (r + 1) * 512)), so at most 48 tiles, exactly 48 from the fullest devices.
All inputs are finite; a program needn't handle non-finite values.
Results may differ from a plain program's by a relative error of at most 0.025.
The roundings to bfloat16 on the way count: a program that leaves them out, or rounds other values in their place, can miss the bound.
Values may be sent and summed in bfloat16 or wider, within the bound.
No kernel may reach another device: no remote copies, remote signals or barrier semaphores. Data moves between devices by JAX's collectives and lax.ppermute only.
A program may use at most 128 MiB of HBM per device.

v0:
```python
import jax
import jax.numpy as jnp
from jax import lax
from jax.sharding import PartitionSpec as P

HEAD_SIZE = 48


def pick_sparse(values, phase_col, stride):
    shape = values.shape
    grouped = values.reshape((shape[0], shape[1] // stride, stride) + shape[2:])
    return lax.dynamic_index_in_dim(grouped, phase_col, 2, False)


def put_sparse(full, sparse, phase_col, stride):
    shape = full.shape
    grouped = full.reshape(shape[0], shape[1] // stride, stride)
    column = jnp.arange(stride, dtype=jnp.int32) == phase_col
    return jnp.where(column[None, None, :], sparse[:, :, None], grouped).reshape(shape)


def add_sparse(full, sparse, phase_col, stride):
    shape = full.shape
    grouped = full.reshape(shape[0], shape[1] // stride, stride, shape[2])
    column = (jnp.arange(stride, dtype=jnp.int32) == phase_col)[None, None, :, None]
    return (grouped + jnp.where(column, sparse[:, :, None, :], jnp.float32(0.0))).reshape(shape)


def attend(queries, key_rows, value_rows, cotangent, far_keys, far_values, phase_col, stride):
    floats = jnp.float32
    score_scale = queries.shape[-1] ** (-0.5)
    sparse_queries = pick_sparse(queries, phase_col, stride)
    sparse_grad = pick_sparse(cotangent, phase_col, stride)
    nearby_window = (
        jnp.einsum("sqd,skd->sqk", queries, key_rows, preferred_element_type=floats) * score_scale
    )
    far = (
        jnp.einsum("sqd,skd->sqk", sparse_queries, far_keys, preferred_element_type=floats)
        * score_scale
    )
    near_max = jnp.max(nearby_window, axis=-1)
    far_max = jnp.maximum(pick_sparse(near_max, phase_col, stride), jnp.max(far, axis=-1))
    row_max = put_sparse(near_max, far_max, phase_col, stride)
    exp_near = jnp.exp(nearby_window - row_max[..., None])
    exp_far = jnp.exp(far - far_max[..., None])
    near_total = jnp.sum(exp_near, axis=-1)
    far_total = pick_sparse(near_total, phase_col, stride) + jnp.sum(exp_far, axis=-1)
    row_total = put_sparse(near_total, far_total, phase_col, stride)
    prob_near = exp_near / row_total[..., None]
    prob_far = exp_far / far_total[..., None]
    nearby_weight = prob_near.astype(jnp.bfloat16)
    weight_far = prob_far.astype(jnp.bfloat16)
    near_prob_gradient = jnp.einsum(
        "sqd,skd->sqk", cotangent, value_rows, preferred_element_type=floats
    )
    dprob_far = jnp.einsum("sqd,skd->sqk", sparse_grad, far_values, preferred_element_type=floats)
    near_delta = jnp.sum(prob_near * near_prob_gradient, axis=-1)
    far_delta = pick_sparse(near_delta, phase_col, stride) + jnp.sum(prob_far * dprob_far, axis=-1)
    row_delta = put_sparse(near_delta, far_delta, phase_col, stride)
    near_score_gradient = (prob_near * (near_prob_gradient - row_delta[..., None])).astype(
        jnp.bfloat16
    )
    dscore_far = (prob_far * (dprob_far - far_delta[..., None])).astype(jnp.bfloat16)
    query_gradient = (
        jnp.einsum("sqk,skd->sqd", near_score_gradient, key_rows, preferred_element_type=floats)
        * score_scale
    )
    far_query = (
        jnp.einsum("sqk,skd->sqd", dscore_far, far_keys, preferred_element_type=floats)
        * score_scale
    )
    query_gradient = add_sparse(query_gradient, far_query, phase_col, stride)
    key_gradient = (
        jnp.einsum("sqk,sqd->skd", near_score_gradient, queries, preferred_element_type=floats)
        * score_scale
    )
    value_gradient = jnp.einsum(
        "sqk,sqd->skd", nearby_weight, cotangent, preferred_element_type=floats
    )
    far_key_grad = (
        jnp.einsum("sqk,sqd->skd", dscore_far, sparse_queries, preferred_element_type=floats)
        * score_scale
    )
    far_value_grad = jnp.einsum(
        "sqk,sqd->skd", weight_far, sparse_grad, preferred_element_type=floats
    )
    return (query_gradient, key_gradient, value_gradient, far_key_grad, far_value_grad)


def per_device(tile_features, embed_weight, qkv_weight, positions, out_grad):
    n_slide = lax.axis_size("slide")
    n_tile = lax.axis_size("tile")
    devices = n_slide * n_tile
    tile_dev = tile_features.shape[0]
    slides = out_grad.shape[0]
    segment = out_grad.shape[1]
    heads_dev = out_grad.shape[2] // HEAD_SIZE
    width = qkv_weight.shape[1] // n_tile
    capacity = tile_dev // n_slide
    span_len = segment * n_slide
    row_here = lax.axis_index("slide")
    embedded = jnp.dot(tile_features, embed_weight, preferred_element_type=jnp.float32).astype(
        jnp.bfloat16
    )
    projected = jnp.dot(embedded, qkv_weight, preferred_element_type=jnp.float32).astype(
        jnp.bfloat16
    )
    is_live = positions >= 0
    offset = jnp.where(is_live, positions % span_len, 0)
    dest_row = offset // segment
    onehot = (
        (dest_row[:, None] == jnp.arange(n_slide, dtype=jnp.int32)[None, :]) & is_live[:, None]
    ).astype(jnp.int32)
    rank_in_row = jnp.sum(jnp.cumsum(onehot, axis=0) * onehot, axis=1) - 1
    send_slot = jnp.where(is_live, dest_row * capacity + rank_in_row, n_slide * capacity)
    outgoing = (
        jnp.zeros((n_slide * capacity, projected.shape[1]), jnp.bfloat16)
        .at[send_slot]
        .set(projected, mode="drop")
    )
    outgoing_pos = (
        jnp.full((n_slide * capacity,), -1, jnp.int32).at[send_slot].set(positions, mode="drop")
    )
    outgoing = outgoing.reshape(n_slide, capacity, n_tile, width)
    outgoing_pos = jnp.broadcast_to(
        outgoing_pos.reshape(n_slide, capacity, 1, 1), (n_slide, capacity, n_tile, 1)
    )
    flat_rows = outgoing.transpose(0, 2, 1, 3).reshape(devices, capacity, width)
    flat_pos = outgoing_pos.transpose(0, 2, 1, 3).reshape(devices, capacity, 1)
    arrived, arrived_pos = (
        lax.all_to_all(flat_rows, ("slide", "tile"), split_axis=0, concat_axis=0, tiled=True),
        lax.all_to_all(flat_pos, ("slide", "tile"), split_axis=0, concat_axis=0, tiled=True),
    )
    arrived_shape = arrived.shape
    arrived_rows = arrived.reshape(-1, width)
    arrived_pos = arrived_pos.reshape(-1)
    present = arrived_pos >= 0
    local_index = jnp.where(
        present,
        arrived_pos // span_len * segment + arrived_pos % span_len - row_here * segment,
        slides * segment,
    ).astype(jnp.int32)
    by_position = (
        jnp.zeros((slides * segment, width), jnp.bfloat16)
        .at[local_index]
        .set(arrived_rows, mode="drop")
    )
    by_position = by_position.reshape(slides, segment, heads_dev, 3, HEAD_SIZE)
    cotangent = out_grad.reshape(slides, segment, heads_dev, HEAD_SIZE)
    phases = [(lax.axis_index("tile") * heads_dev + 0) % n_slide]
    local_keys = jnp.stack([pick_sparse(by_position[:, :, 0, 1], phases[0], n_slide)], axis=2)
    local_values = jnp.stack([pick_sparse(by_position[:, :, 0, 2], phases[0], n_slide)], axis=2)
    all_keys, all_values = (
        lax.all_gather(local_keys, "slide", axis=1, tiled=True),
        lax.all_gather(local_values, "slide", axis=1, tiled=True),
    )
    head_local = 0
    results = [
        attend(
            by_position[:, :, head_local, 0],
            by_position[:, :, head_local, 1],
            by_position[:, :, head_local, 2],
            cotangent[:, :, head_local],
            all_keys[:, :, head_local],
            all_values[:, :, head_local],
            phases[head_local],
            n_slide,
        )
    ]
    far_key_all = jnp.stack([entry[3] for entry in results], axis=2)
    far_value_all = jnp.stack([entry[4] for entry in results], axis=2)
    summed_keys, summed_values = (
        lax.psum_scatter(far_key_all, "slide", scatter_dimension=1, tiled=True),
        lax.psum_scatter(far_value_all, "slide", scatter_dimension=1, tiled=True),
    )
    head_local = 0
    query_gradient = results[head_local][0]
    key_gradient = results[head_local][1]
    value_gradient = results[head_local][2]
    key_gradient = add_sparse(
        key_gradient, summed_keys[:, :, head_local], phases[head_local], n_slide
    )
    value_gradient = add_sparse(
        value_gradient, summed_values[:, :, head_local], phases[head_local], n_slide
    )
    head_grads = [
        jnp.stack([query_gradient, key_gradient, value_gradient], axis=2).astype(jnp.bfloat16)
    ]
    d_position = jnp.stack(head_grads, axis=2).reshape(slides * segment, width)
    safe_local = jnp.clip(local_index, 0, slides * segment - 1)
    going_back = jnp.where(
        present[:, None], d_position[safe_local], jnp.zeros((), jnp.bfloat16)
    ).reshape(arrived_shape)
    came_back = lax.all_to_all(
        going_back, ("slide", "tile"), split_axis=0, concat_axis=0, tiled=True
    )
    slot_rows = (
        came_back.reshape(n_slide, n_tile, capacity, width)
        .transpose(0, 2, 1, 3)
        .reshape(n_slide * capacity, n_tile * width)
    )
    safe_slot = jnp.clip(send_slot, 0, n_slide * capacity - 1)
    d_slots = jnp.where(is_live[:, None], slot_rows[safe_slot], jnp.zeros((), jnp.bfloat16))
    qkv_partial = jnp.einsum("td,tf->df", embedded, d_slots, preferred_element_type=jnp.float32)
    d_embedded = jnp.einsum(
        "tf,df->td", d_slots, qkv_weight, preferred_element_type=jnp.float32
    ).astype(jnp.bfloat16)
    embed_partial = jnp.einsum(
        "tc,td->cd", tile_features, d_embedded, preferred_element_type=jnp.float32
    )
    feature_grad = jnp.einsum(
        "td,cd->tc", d_embedded, embed_weight, preferred_element_type=jnp.float32
    ).astype(jnp.bfloat16)
    embed_half, qkv_half = (
        lax.psum_scatter(embed_partial, "tile", scatter_dimension=1, tiled=True),
        lax.psum_scatter(qkv_partial, "tile", scatter_dimension=1, tiled=True),
    )
    embed_grad, qkv_grad = (
        lax.psum_scatter(embed_half, "slide", scatter_dimension=0, tiled=True),
        lax.psum_scatter(qkv_half, "slide", scatter_dimension=0, tiled=True),
    )
    return (feature_grad, embed_grad, qkv_grad)


def solution(mesh):
    placed = (P(("slide", "tile"), None), P(), P(), P(("slide", "tile")), P(None, "slide", "tile"))
    return jax.shard_map(
        per_device,
        mesh=mesh,
        in_specs=placed,
        out_specs=(P(("slide", "tile"), None), P("slide", "tile"), P("slide", "tile")),
        check_vma=False,
    )
```

profile of v0, /device:TPU:0, one launch (start us, length us, event | category | flops | bytes accessed | tf_op | source)
XLA Modules:
  0.0 649.2 jit_solution(1049379997082727459)
XLA Ops:
  15.1 3.1 scatter_custom_fusion
  18.9 11.7 %all-to-all-start = ((s32[128,48,1]{1,2,0:T(1,128)}), s32[128,48,1]{1,2,0:T(1,128)}, u32[]{:S(2)}, u32[]{:S(2)}) async-start(s32[128,48,1]{1,2,0:T(1,128)} %bitcast.160), calls=%async_computation | async-start | bytes 131072 | tf_op jit(solution)/shard_map/all_to_all | solution.py:132
  30.6 3.1 convolution_convert_fusion.2
  39.2 5.4 scatter_custom_fusion.1
  44.6 7.0 %reshape.330 = bf16[8,48,16,144]{3,2,1,0:T(8,128)(2,1)} reshape(bf16[384,2304]{1,0:T(8,128)(2,1)} %scatter_custom_fusion.1) | data formatting | bytes 3538944 | tf_op jit(solution)/shard_map/reshape | solution.py:124
  51.6 4.8 copy.103
  56.4 10.2 %all-to-all-start.1 = ((bf16[128,48,144]{2,1,0:T(8,128)(2,1)}), bf16[128,48,144]{2,1,0:T(8,128)(2,1)}, u32[]{:S(2)}, u32[]{:S(2)}) async-start(bf16[128,48,144]{2,1,0:T(8,128)(2,1)} %bitcast.146), calls=%async_computation.1 | async-start | bytes 6291456 | tf_op jit(solution)/shard_map/all_to_all | solution.py:131
  78.7 27.9 %all-to-all-done.1 = bf16[128,48,144]{2,1,0:T(8,128)(2,1)} async-done(((bf16[128,48,144]{2,1,0:T(8,128)(2,1)}), bf16[128,48,144]{2,1,0:T(8,128)(2,1)}, u32[]{:S(2)}, u32[]{:S(2)}) %all-to-all-start.1) | async-done | bytes 1769504 | tf_op jit(solution)/shard_map/all_to_all | solution.py:131
  106.6 27.7 %scatter_custom_fusion.2 = bf16[2048,144]{1,0:T(8,128)(2,1)} fusion(s32[6144]{0:T(1024)} %bitcast.163, bf16[6144,144]{1,0:T(8,128)(2,1)} %bitcast.9, bf16[]{:T(256)} %constant.111.clone.1), kind=kCustom, calls=%fused_computation.50 | custom fusion | bytes 590336 | tf_op jit(solution)/shard_map/scatter | solution.py:146
  145.1 3.7 multiply_reduce_fusion
  152.1 14.2 %all_gather.7 = bf16[4,512,1,48]{3,0,2,1:T(4,128)(2,1)} all-gather(bf16[4,64,1,48]{3,0,2,1:T(4,128)(2,1)S(1)} %copy.118), channel_id=1, replica_groups=mesh['slide'=8,'tile'=16] {'slide'}, dimensions={1}, use_global_device_ids=true | all-gather | bytes 221184 | tf_op jit(solution)/shard_map/all_gather | solution.py:155
  174.9 14.4 %all_gather.6 = bf16[4,512,1,48]{3,0,2,1:T(4,128)(2,1)} all-gather(bf16[4,64,1,48]{3,0,2,1:T(4,128)(2,1)S(1)} %copy.110), channel_id=1, replica_groups=mesh['slide'=8,'tile'=16] {'slide'}, dimensions={1}, use_global_device_ids=true | all-gather | bytes 221184 | tf_op jit(solution)/shard_map/all_gather | solution.py:154
  215.4 6.1 fusion
  249.7 5.9 fusion.2
  258.5 4.7 reduce-scatter.21.cloned.1.call-done
  269.0 4.0 fusion.20
  273.0 22.4 %reduce-scatter.19.cloned.1.call-done = f32[64,192]{1,0:T(8,128)} async-done(((f32[512,192]{1,0:T(8,128)}), f32[64,192]{1,0:T(8,128)}) %reduce-scatter.19.cloned.1.call-update) | async-done | bytes 49168
  308.5 26.7 %gather_fusion = bf16[6144,144]{1,0:T(8,128)(2,1)} fusion(bf16[2048,144]{1,0:T(8,128)(2,1)} %copy.131, s32[6144]{0:T(1024)} %broadcast_clamp_fusion), kind=kCustom, calls=%fused_computation | custom fusion | bytes 3563520 | tf_op jit(solution)/shard_map/gather | solution.py:192
  335.2 5.0 broadcast_select_fusion
  340.2 7.8 %all-to-all-start.2 = ((bf16[128,48,144]{2,1,0:T(8,128)(2,1)}), bf16[128,48,144]{2,1,0:T(8,128)(2,1)}, u32[]{:S(2)}, u32[]{:S(2)}) async-start(bf16[128,48,144]{2,1,0:T(8,128)(2,1)} %broadcast_select_fusion), calls=%async_computation.2 | async-start | bytes 6291456 | tf_op jit(solution)/shard_map/all_to_all | solution.py:194
  348.1 40.0 %all-to-all-done.2 = bf16[128,48,144]{2,1,0:T(8,128)(2,1)} async-done(((bf16[128,48,144]{2,1,0:T(8,128)(2,1)}), bf16[128,48,144]{2,1,0:T(8,128)(2,1)}, u32[]{:S(2)}, u32[]{:S(2)}) %all-to-all-start.2) | async-done | bytes 1769504 | tf_op jit(solution)/shard_map/all_to_all | solution.py:194
  388.1 4.8 copy.170
  392.9 6.3 reshape.338
  399.2 7.3 %gather_fusion.1 = bf16[384,2304]{1,0:T(8,128)(2,1)} fusion(bf16[384,2304]{1,0:T(8,128)(2,1)} %reshape.338, s32[1024]{0:T(1024)S(1)} %pad_clamp_fusion), kind=kCustom, calls=%fused_computation.1 | custom fusion | bytes 3540480 | tf_op jit(solution)/shard_map/gather | solution.py:203
  406.5 3.2 convolution_convert_fusion.3
  410.5 3.6 convolution_bitcast_fusion
  414.2 6.7 %fusion.25 = f32[768,2304]{0,1:T(8,128)} fusion(bf16[384,768]{1,0:T(8,128)(2,1)} %copy-done.3, bf16[384,2304]{1,0:T(8,128)(2,1)} %gather_fusion.1, pred[384]{0:T(512)(128)(4,1)S(1)} %copy-done.12), kind=kOutput, calls=%fused_computation.42 | convolution fusion | flops 1359839232 | bytes 9437568 | tf_op jit(solution)/shard_map/td,tf->df/dot_general | solution.py:204
  421.0 68.3 %reduce-scatter.15.cloned.1.call-done = f32[1536,48]{0,1:T(8,128)} async-done(((f32[1536,768]{0,1:T(8,128)}), f32[1536,48]{0,1:T(8,128)}) %reduce-scatter.15.cloned.1.call-update) | async-done | bytes 294928 | tf_op jit(solution)/shard_map/reduce_scatter | solution.py:215
  491.5 83.1 %reduce-scatter.17.cloned.1.call-done = f32[768,144]{0,1:T(8,128)} async-done(((f32[768,2304]{0,1:T(8,128)}), f32[768,144]{0,1:T(8,128)}) %reduce-scatter.17.cloned.1.call-update) | async-done | bytes 442384 | tf_op jit(solution)/shard_map/reduce_scatter | solution.py:216
  576.8 4.0 convolution_convert_fusion.1
  580.8 27.2 %reduce-scatter.23.cloned.1.call-done = f32[192,48]{1,0:T(8,128)} async-done(((f32[1536,48]{1,0:T(8,128)}), f32[192,48]{1,0:T(8,128)}) %reduce-scatter.23.cloned.1.call-update) | async-done | bytes 36880
  609.6 30.9 %reduce-scatter.25.cloned.1.call-done = f32[96,144]{1,0:T(8,128)} async-done(((f32[768,144]{1,0:T(8,128)}), f32[96,144]{1,0:T(8,128)}) %reduce-scatter.25.cloned.1.call-update) | async-done | bytes 55312
  (131 shorter events, 133.3 us)
Async XLA Ops:
  7.2 26.6 %copy-start = (bf16[768,2304]{1,0:T(8,128)(2,1)S(1)}, bf16[768,2304]{1,0:T(8,128)(2,1)}, u32[]{:S(2)}) copy-start(bf16[768,2304]{1,0:T(8,128)(2,1)} %param.7) | copy-start | bytes 10616836
  8.0 0.5 copy-start.11
  18.9 37.4 %all-to-all-start = ((s32[128,48,1]{1,2,0:T(1,128)}), s32[128,48,1]{1,2,0:T(1,128)}, u32[]{:S(2)}, u32[]{:S(2)}) async-start(s32[128,48,1]{1,2,0:T(1,128)} %bitcast.160), calls=%async_computation | async-start | bytes 131072 | tf_op jit(solution)/shard_map/all_to_all | solution.py:132
  33.8 2.8 copy-start.3
  56.4 50.3 %all-to-all-start.1 = ((bf16[128,48,144]{2,1,0:T(8,128)(2,1)}), bf16[128,48,144]{2,1,0:T(8,128)(2,1)}, u32[]{:S(2)}, u32[]{:S(2)}) async-start(bf16[128,48,144]{2,1,0:T(8,128)(2,1)} %bitcast.146), calls=%async_computation.1 | async-start | bytes 6291456 | tf_op jit(solution)/shard_map/all_to_all | solution.py:131
  66.5 196.6 %reduce-scatter.21.cloned.1.call-start = ((), (), s32[]{:S(2)}) async-start(), calls=%async_computation.12 | async-start | bytes 589824
  196.0 2.8 copy-start.5
  205.9 0.6 copy-start.10
  215.4 9.3 %copy-start.6 = (f32[4,64]{1,0:T(4,128)S(1)}, f32[4,64]{1,0:T(4,128)}, u32[]{:S(2)}) copy-start(f32[4,64]{1,0:T(4,128)} %copy-done.5) | copy-start | bytes 3076
  224.1 0.6 copy-start.9
  226.1 13.2 %copy-start.7 = (f32[4,512]{1,0:T(4,128)S(1)}, f32[4,512]{1,0:T(4,128)}, u32[]{:S(2)}) copy-start(f32[4,512]{1,0:T(4,128)} %get-tuple-element.18) | copy-start | bytes 24580
  234.5 60.9 %reduce-scatter.19.cloned.1.call-start = ((), (), s32[]{:S(2)}) async-start(), calls=%async_computation.11 | async-start | bytes 589824
  240.6 9.1 %copy-start.8 = (f32[4,512]{1,0:T(4,128)S(1)}, f32[4,512]{1,0:T(4,128)}, u32[]{:S(2)}) copy-start(f32[4,512]{1,0:T(4,128)} %broadcast_select_fusion.5) | copy-start | bytes 24580
  308.5 26.7 %copy-start.4 = (pred[128,48]{1,0:T(8,128)(4,1)S(1)}, pred[128,48]{1,0:T(8,128)(4,1)}, u32[]{:S(2)}) copy-start(pred[128,48]{1,0:T(8,128)(4,1)} %copy.102) | copy-start | bytes 18436
  340.2 7.9 %copy-start.13 = (s32[384]{0:T(512)S(1)}, s32[384]{0:T(512)}, u32[]{:S(2)}) copy-start(s32[384]{0:T(512)} %get-tuple-element.10) | copy-start | bytes 4612
  340.2 47.9 %all-to-all-start.2 = ((bf16[128,48,144]{2,1,0:T(8,128)(2,1)}), bf16[128,48,144]{2,1,0:T(8,128)(2,1)}, u32[]{:S(2)}, u32[]{:S(2)}) async-start(bf16[128,48,144]{2,1,0:T(8,128)(2,1)} %broadcast_select_fusion), calls=%async_computation.2 | async-start | bytes 6291456 | tf_op jit(solution)/shard_map/all_to_all | solution.py:194
  348.0 141.3 %reduce-scatter.15.cloned.1.call-start = ((), (), s32[]{:S(2)}) async-start(), calls=%async_computation.9 | async-start | bytes 5013504 | tf_op jit(solution)/shard_map/reduce_scatter | solution.py:215
  399.2 7.3 %copy-start.12 = (pred[384]{0:T(512)(128)(4,1)S(1)}, pred[384]{0:T(512)(128)(4,1)}, u32[]{:S(2)}) copy-start(pred[384]{0:T(512)(128)(4,1)} %copy-done.11) | copy-start | bytes 1156
  406.5 4.0 copy-start.1
  409.7 0.8 copy-start.2
  414.2 160.5 %reduce-scatter.17.cloned.1.call-start = ((), (), s32[]{:S(2)}) async-start(), calls=%async_computation.10 | async-start | bytes 7520256 | tf_op jit(solution)/shard_map/reduce_scatter | solution.py:216
  421.0 187.0 %reduce-scatter.23.cloned.1.call-start = ((), (), s32[]{:S(2)}) async-start(), calls=%async_computation.13 | async-start | bytes 884736
  491.4 149.0 %reduce-scatter.25.cloned.1.call-start = ((), (), s32[]{:S(2)}) async-start(), calls=%async_computation.14 | async-start | bytes 884736
Sparse Core Ops, SparseCore 0:
  234.7 28.4 reduce-scatter.20
  265.7 29.7 reduce-scatter.18
  414.3 74.9 reduce-scatter.14
  492.6 81.9 reduce-scatter.16
  577.0 30.9 reduce-scatter.22
  610.2 30.2 reduce-scatter.24
where the time goes:
time: 661 us; the launch traced here: 649 us
  waiting for transfers between devices  305 us (46%)
  local copies, waits for them, and re-layouts  180 us (27%)
  matrix products  52.6 us (8%)
  other arithmetic  38.3 us (6%)
  starting transfers between devices  30.4 us (5%)
  blocking collectives  28.6 us (4%)
  between operations  14.6 us (2%)
    unnamed x10, waiting for transfers between devices  85.3 us
    reduce_scatter x1, waiting for transfers between devices, per_device(): lax.psum_scatter(qkv_partial, 'tile', scatter_dimension=1, tiled=True)  83.1 us
    reduce_scatter x1, waiting for transfers between devices, per_device(): lax.psum_scatter(embed_partial, 'tile', scatter_dimension=1, tiled=True)  68.3 us
    all_to_all x1, waiting for transfers between devices, per_device(): lax.all_to_all(going_back, ('slide', 'tile'), split_axis=0, concat_axis=0...  40 us
    scatter x2, local copies, waits for them, and re-layouts, per_device(): by_position = jnp.zeros((slides * segment, width), jnp.bfloat16).at[local...  29.8 us
    all_to_all x1, waiting for transfers between devices, per_device(): lax.all_to_all(flat_rows, ('slide', 'tile'), split_axis=0, concat_axis=0,...  27.9 us
    gather x1, local copies, waits for them, and re-layouts, per_device(): d_position[safe_local]  26.7 us
    unnamed x40, local copies, waits for them, and re-layouts  25.8 us
  transfers between devices with their start and end apart: 9, of which 8 were waited for; matrix products, arithmetic and copies ran while one was open for 13% of the time, Pallas kernels for 0%

commit v1 on v0

v1 whole, which is shorter than its diff:
```python
import functools

import jax
import jax.numpy as jnp
from jax import lax
from jax.experimental import pallas as pl
from jax.experimental.pallas import tpu as pltpu
from jax.sharding import PartitionSpec as P

HEAD_SIZE = 48
WIDTH = 3 * HEAD_SIZE
CHUNK_ROWS = 160
FLOATS = jnp.float32
HALFS = jnp.bfloat16
SCALE = HEAD_SIZE ** (-0.5)
VMEM = pltpu.CompilerParams(vmem_limit_bytes=56 * 1024 * 1024)


def iota(shape, dim):
    return lax.broadcasted_iota(jnp.int32, shape, dim)


def hot(cond):
    return jnp.where(cond, 1.0, 0.0).astype(HALFS)


def dot(a, b, dims="nn"):
    contract = (0 if dims[0] == "t" else 1, 1 if dims[1] == "t" else 0)
    return lax.dot_general(
        a, b, (((contract[0],), (contract[1],)), ((), ())), preferred_element_type=FLOATS
    )


def whole(memory=pltpu.VMEM):
    return pl.BlockSpec(memory_space=memory)


def call(body, outs, args, smem=(), **kw):
    specs = [whole(pltpu.SMEM if i in smem else pltpu.VMEM) for i in range(len(args))]
    return pl.pallas_call(
        body,
        out_shape=outs,
        in_specs=specs,
        out_specs=jax.tree.map(lambda _: whole(), outs),
        compiler_params=VMEM,
        **kw,
    )(*args)


def shaped(shape, dtype=HALFS):
    return jax.ShapeDtypeStruct(shape, dtype)


def place(pos, rank, off):
    row = (pos & 4095) >> 9
    dest = row * 16 + ((rank + off) & 15)
    return dest * 8, rank >> 4


def dispatch_body(me_ref, counts_ref, pos_row_ref, pos_col_ref, emb_ref, send_ref, base_ref):
    slots = emb_ref.shape[0]
    half = emb_ref.shape[1] // 2
    counts = counts_ref[...]
    before = (iota(counts.shape, 0) < me_ref[0]) & (iota(counts.shape, 1) == 0)
    off = jnp.sum(
        jnp.sum(jnp.where(before, counts, 0), axis=0, keepdims=True), axis=1, keepdims=True
    )
    pos = pos_row_ref[...]
    live = pos >= 0
    pos = jnp.where(live, pos, 0)
    member = ((pos & 4095) >> 9 == iota((8, slots), 0)) & live
    upper = hot(iota((slots, slots), 0) < iota((slots, slots), 1))
    ranks = dot(hot(member), upper)
    rank = jnp.sum(jnp.where(member, ranks, 0.0), axis=0, keepdims=True).astype(jnp.int32)
    dest, sub = place(pos, rank, off)
    base = jnp.where(live, dest + 2 * sub, -16)
    note = jnp.where(live, dest + 6, -16)
    local = ((pos >> 12) << 9) + (pos & 511)
    lane = iota((128, slots), 0)
    notes = jnp.where(
        lane == 4 * sub, (local >> 7) + 1, jnp.where(lane == 4 * sub + 1, local & 127, 0)
    )
    notes = notes.astype(FLOATS).astype(HALFS)
    step = 256
    for start in range(0, send_ref.shape[0], step):
        rows = iota((step, slots), 0) + start
        out = dot(hot(rows == base), emb_ref[:, :half])
        out = out + dot(hot(rows == base + 1), emb_ref[:, half:])
        send_ref[start : start + step, :] = out.astype(HALFS)
        info = dot(hot(rows == note), notes, "nt")
        send_ref[start : start + step, :128] = (out[:, :128] + info).astype(HALFS)
    pos = pos_col_ref[...]
    live = pos >= 0
    pos = jnp.where(live, pos, 0)
    member = ((pos & 4095) >> 9 == iota((slots, 128), 1)) & live
    lower = hot(iota((slots, slots), 0) > iota((slots, slots), 1))
    ranks = dot(lower, hot(member))
    rank = jnp.sum(jnp.where(member, ranks, 0.0), axis=1, keepdims=True).astype(jnp.int32)
    dest, sub = place(pos, rank, off)
    base_ref[...] = jnp.broadcast_to(jnp.where(live, dest + 2 * sub, -16), base_ref.shape)


def project_body(recv_ref, weight_ref, emb_ref, chunk_ref, pick0_ref, pick1_ref):
    total = recv_ref.shape[0]
    senders = total // 8
    sel = hot(iota((senders, total), 1) == 8 * iota((senders, total), 0) + 6)
    notes = dot(sel, recv_ref[:, :128])
    lane = iota((senders, 128), 1)
    valid = (notes > 0.5) & ((lane & 3) == 0) & (lane < 12)
    lower = hot(iota((senders, senders), 0) > iota((senders, senders), 1))
    cum = dot(lower, hot(valid))
    ones = jnp.where(valid, 1.0, 0.0)
    first = jnp.sum(jnp.where(lane == 0, ones, 0.0), axis=0, keepdims=True)
    first = jnp.sum(first, axis=1, keepdims=True)
    second = jnp.sum(jnp.where(lane == 4, ones, 0.0), axis=0, keepdims=True)
    second = jnp.sum(second, axis=1, keepdims=True)
    shift = jnp.where(lane >= 4, first, 0.0) + jnp.where(lane >= 8, second, 0.0)
    index = jnp.where(valid, cum + shift, -1.0)
    repeat = hot(iota((total, senders), 0) >> 3 == iota((total, senders), 1))
    index_all = dot(repeat, index.astype(HALFS))
    notes_all = dot(repeat, notes.astype(HALFS))
    turn = iota((total, 128), 0) & 7
    lanes = iota((total, 128), 1)
    mine = (lanes == 4 * (turn >> 1)) & (turn < 6)
    mine_low = (lanes == 4 * (turn >> 1) + 1) & (turn < 6)
    spot = jnp.sum(jnp.where(mine, index_all + 1.0, 0.0), axis=1, keepdims=True) - 1.0
    high = jnp.sum(jnp.where(mine, notes_all, 0.0), axis=1, keepdims=True)
    low = jnp.sum(jnp.where(mine_low, notes_all, 0.0), axis=1, keepdims=True)
    match = spot.astype(jnp.int32) == lanes
    pick0 = hot(match & ((turn & 1) == 0))
    pick1 = hot(match & ((turn & 1) == 1))
    pick0_ref[...] = pick0
    pick1_ref[...] = pick1
    half = recv_ref.shape[1]
    emb_ref[:, :half] = dot(pick0, recv_ref[...], "tn").astype(HALFS)
    emb_ref[:, half:] = dot(pick1, recv_ref[...], "tn").astype(HALFS)
    info = jnp.where(lanes == 0, high, jnp.where(lanes == 1, low, 0.0)).astype(HALFS)
    info = dot(info, pick0, "tn")[:16].astype(HALFS)
    heads = chunk_ref.shape[0] // CHUNK_ROWS
    for head in range(heads):
        columns = slice(head * WIDTH, (head + 1) * WIDTH)
        top = head * CHUNK_ROWS
        if head % 8 == 0:
            wide = slice(head * WIDTH, (head + 8) * WIDTH)
            part = dot(emb_ref[...], weight_ref[:, wide]).T
        columns = slice((head % 8) * WIDTH, (head % 8 + 1) * WIDTH)
        chunk_ref[top : top + WIDTH, :] = part[columns].astype(HALFS)
        chunk_ref[top + WIDTH : top + CHUNK_ROWS, :] = info


def dilated_body(phase_ref, chunk_ref, query_ref, far_ref, rows_ref, local_ref):
    blocks = chunk_ref.shape[0] // CHUNK_ROWS
    total = jnp.zeros((WIDTH, query_ref.shape[1]), FLOATS)
    target = 8 * iota((query_ref.shape[1], 128), 0) + phase_ref[0]
    for block in range(blocks):
        top = block * CHUNK_ROWS
        lanes = slice(block * 128, (block + 1) * 128)
        part = chunk_ref[top : top + WIDTH, :]
        info = chunk_ref[top + WIDTH : top + CHUNK_ROWS, :].astype(FLOATS)
        local = ((info[0:1] - 1.0) * 128.0 + info[1:2]).astype(jnp.int32)
        rows_ref[:, lanes] = part
        local_ref[:, lanes] = jnp.broadcast_to(local, (8, 128))
        total = total + dot(part, hot(target == local), "nt")
    query_ref[...] = total[:HEAD_SIZE].astype(HALFS)
    far_ref[...] = total[HEAD_SIZE:].astype(HALFS)


def near_body(phase_ref, rows_ref, local_ref, grad_ref, place_ref, near_ref):
    seg = grad_ref.shape[2]
    slide = pl.program_id(0)
    local = local_ref[0:1, :]
    order = hot(local == iota((seg, local.shape[1]), 0) + slide * seg)
    parts = dot(rows_ref[...], order, "nt").astype(HALFS)
    place_ref[...] = parts
    query = parts[:HEAD_SIZE]
    key = parts[HEAD_SIZE : 2 * HEAD_SIZE]
    value = parts[2 * HEAD_SIZE :]
    grad = grad_ref[0]
    score = dot(key, query, "tn") * SCALE
    top = jnp.max(score, axis=0, keepdims=True)
    prob = jnp.exp(score - top)
    norm = 1.0 / jnp.sum(prob, axis=0, keepdims=True)
    dilated = (iota((1, seg), 1) & 7) == phase_ref[0]
    prob = prob * jnp.where(dilated, 0.0, norm)
    dprob = dot(value, grad, "tn")
    delta = jnp.sum(prob * dprob, axis=0, keepdims=True)
    dscore = (prob * (dprob - delta)).astype(HALFS)
    near_ref[:HEAD_SIZE, :] = dot(key, dscore) * SCALE
    near_ref[HEAD_SIZE : 2 * HEAD_SIZE, :] = dot(query, dscore, "nt") * SCALE
    near_ref[2 * HEAD_SIZE :, :] = dot(grad, prob.astype(HALFS), "nt")


def far_body(phase_ref, query_ref, place_ref, grad_ref, *refs):
    n = (len(refs) - 2) // 2
    far_refs, dquery_ref, near_ref, out_refs = refs[:n], refs[n], refs[n + 1], refs[n + 2 :]
    seg = grad_ref.shape[2]
    for pair in range(grad_ref.shape[0] // 2):
        lanes = slice(pair * 128, (pair + 1) * 128)
        spots = slice(pair * 2 * seg, (pair + 1) * 2 * seg)
        query = query_ref[:, lanes]
        grad = jnp.zeros((HEAD_SIZE, 128), FLOATS)
        for b in range(2):
            target = 8 * (iota((seg, 128), 1) - 64 * b) + phase_ref[0]
            grad = grad + dot(grad_ref[2 * pair + b], hot(iota((seg, 128), 0) == target))
        grad = grad.astype(HALFS)
        key = jnp.concatenate(
            [place_ref[HEAD_SIZE : 2 * HEAD_SIZE, spots]]
            + [ref[:HEAD_SIZE, lanes] for ref in far_refs],
            axis=1,
        )
        value = jnp.concatenate(
            [place_ref[2 * HEAD_SIZE :, spots]] + [ref[HEAD_SIZE:, lanes] for ref in far_refs],
            axis=1,
        )
        size = key.shape[1]
        row = iota((size, 128), 0)
        slide_of_key = jnp.where(row < 2 * seg, row // seg, (row & 127) >> 6)
        same = slide_of_key == iota((size, 128), 1) >> 6
        score = jnp.where(same, dot(key, query, "tn") * SCALE, -1e30)
        top = jnp.max(score, axis=0, keepdims=True)
        prob = jnp.exp(score - top)
        prob = prob * (1.0 / jnp.sum(prob, axis=0, keepdims=True))
        dprob = dot(value, grad, "tn")
        delta = jnp.sum(prob * dprob, axis=0, keepdims=True)
        dscore = (prob * (dprob - delta)).astype(HALFS)
        dquery_ref[:, lanes] = (dot(key, dscore) * SCALE).astype(HALFS)
        dkey = dot(query, dscore, "nt") * SCALE
        dvalue = dot(grad, prob.astype(HALFS), "nt")
        near_ref[:HEAD_SIZE, spots] = dkey[:, : 2 * seg]
        near_ref[HEAD_SIZE:, spots] = dvalue[:, : 2 * seg]
        for k, ref in enumerate(out_refs):
            part = slice(2 * seg + k * 128, 2 * seg + (k + 1) * 128)
            ref[:HEAD_SIZE, lanes] = dkey[:, part].astype(HALFS)
            ref[HEAD_SIZE:, lanes] = dvalue[:, part].astype(HALFS)


def unplace_body(local_ref, near_ref, extra_ref, out_ref):
    places = near_ref.shape[1]
    block = out_ref.shape[1]
    local = local_ref[0:1, :]
    order = hot(local == iota((places, block), 0))
    query = near_ref[:HEAD_SIZE, :].astype(HALFS)
    rest = (near_ref[HEAD_SIZE:, :] + extra_ref[...]).astype(HALFS)
    out_ref[...] = dot(jnp.concatenate([query, rest], axis=0), order)


def finish_body(phase_ref, local_ref, main_ref, dquery_ref, *refs):
    far_refs, chunk_ref, rows_ref = refs[:-2], refs[-2], refs[-1]
    far = far_refs[0][...].astype(FLOATS)
    for ref in far_refs[1:]:
        far = far + ref[...].astype(FLOATS)
    sparse = jnp.concatenate([dquery_ref[...], far.astype(HALFS)], axis=0)
    local = local_ref[0:1, :]
    count = dquery_ref.shape[1]
    order = hot(local == 8 * iota((count, local.shape[1]), 0) + phase_ref[0])
    rows = (main_ref[...] + dot(sparse, order)).astype(HALFS)
    rows_ref[...] = rows
    for block in range(chunk_ref.shape[0] // WIDTH):
        chunk_ref[block * WIDTH : (block + 1) * WIDTH, :] = rows[
            :, block * 128 : (block + 1) * 128
        ]


def back_body(rows_ref, weight_ref, pick0_ref, pick1_ref, back_ref):
    half = back_ref.shape[1]
    grad = dot(weight_ref[...], rows_ref[...]).astype(HALFS)
    back = dot(pick0_ref[...], grad[:half], "nt") + dot(pick1_ref[...], grad[half:], "nt")
    back_ref[...] = back.astype(HALFS)


def collect_body(recv_ref, base_ref, out_ref):
    total, half = recv_ref.shape
    base = base_ref[:, 0:1]
    rows = iota((base.shape[0], total), 1)
    out_ref[:, :half] = dot(hot(rows == base), recv_ref[...]).astype(HALFS)
    out_ref[:, half:] = dot(hot(rows == base + 1), recv_ref[...]).astype(HALFS)


def per_device(tile_features, embed_weight, qkv_weight, positions, out_grad):
    n_slide = lax.axis_size("slide")
    n_tile = lax.axis_size("tile")
    devices = n_slide * n_tile
    every = ("slide", "tile")
    slots = tile_features.shape[0]
    slides, seg = out_grad.shape[0], out_grad.shape[1]
    wide = embed_weight.shape[1]
    half = wide // 2
    rows = slides * seg
    share = rows // n_tile
    row_here = lax.axis_index("slide")
    col_here = lax.axis_index("tile")
    me = (row_here * n_tile + col_here).astype(jnp.int32).reshape(1)
    phase = (col_here % n_slide).astype(jnp.int32).reshape(1)
    core = row_here % 2

    with jax.named_scope("counts"):
        count = jnp.sum((positions >= 0).astype(jnp.int32)) // n_slide
        counts = lax.all_to_all(
            jnp.broadcast_to(count, (devices, 1, 128)), every, 0, 0, tiled=True
        ).reshape(devices, 128)
    with jax.named_scope("embed"):
        embedded = jnp.dot(tile_features, embed_weight, preferred_element_type=FLOATS).astype(HALFS)
    with jax.named_scope("dispatch"):
        sent, base = call(
            dispatch_body,
            [shaped((devices * 8, half)), shaped((slots, 128), jnp.int32)],
            [me, counts, positions.reshape(1, slots), positions.reshape(slots, 1), embedded],
            smem=(0,),
        )
        arrived = lax.all_to_all(
            sent.reshape(devices, 8, half), every, 0, 0, tiled=True
        ).reshape(devices * 8, half)
    with jax.named_scope("project"):
        emb_rows, chunks, pick0, pick1 = call(
            project_body,
            [
                shaped((share, wide)),
                shaped((n_tile * CHUNK_ROWS, 128)),
                shaped((devices * 8, 128)),
                shaped((devices * 8, 128)),
            ],
            [arrived, qkv_weight],
        )
        chunks = lax.all_to_all(
            chunks.reshape(n_tile, CHUNK_ROWS, 128), "tile", 0, 0, tiled=True
        ).reshape(n_tile * CHUNK_ROWS, 128)
    with jax.named_scope("dilated"):
        few = rows // n_slide
        query, far, head_rows, local = call(
            dilated_body,
            [
                shaped((HEAD_SIZE, few)),
                shaped((2 * HEAD_SIZE, few)),
                shaped((WIDTH, rows)),
                shaped((8, rows), jnp.int32),
            ],
            [phase, chunks],
            smem=(0,),
        )
        fars = [far] + [
            lax.ppermute(far, "slide", [(i, (i + k) % n_slide) for i in range(n_slide)])
            for k in range(1, n_slide)
        ]
    with jax.named_scope("near"):
        grads = out_grad.transpose(0, 2, 1)
        placed, near = pl.pallas_call(
            near_body,
            grid=(slides,),
            out_shape=[shaped((WIDTH, rows)), shaped((WIDTH, rows), FLOATS)],
            in_specs=[
                whole(pltpu.SMEM),
                pl.BlockSpec((WIDTH, rows), lambda i: (0, 0)),
                pl.BlockSpec((8, rows), lambda i: (0, 0)),
                pl.BlockSpec((1, HEAD_SIZE, seg), lambda i: (i, 0, 0)),
            ],
            out_specs=[
                pl.BlockSpec((WIDTH, seg), lambda i: (0, i)),
                pl.BlockSpec((WIDTH, seg), lambda i: (0, i)),
            ],
            compiler_params=VMEM,
            cost_estimate=pl.CostEstimate(
                flops=8_000_000_000, bytes_accessed=8_000_000, transcendentals=1 << 20
            ),
        )(phase, head_rows, local, grads)
    with jax.named_scope("far"):
        results = call(
            far_body,
            [shaped((HEAD_SIZE, few)), shaped((2 * HEAD_SIZE, rows), FLOATS)]
            + [shaped((2 * HEAD_SIZE, few))] * n_slide,
            [phase, query, placed, grads] + fars,
            smem=(0,),
        )
        dquery, extra, outs = results[0], results[1], results[2:]
        returned = [outs[0]] + [
            lax.ppermute(outs[k], "slide", [((i + k) % n_slide, i) for i in range(n_slide)])
            for k in range(1, n_slide)
        ]
    with jax.named_scope("unplace"):
        block = rows // 4
        main = pl.pallas_call(
            unplace_body,
            grid=(rows // block,),
            out_shape=shaped((WIDTH, rows), FLOATS),
            in_specs=[
                pl.BlockSpec((8, block), lambda i: (0, i)),
                pl.BlockSpec((WIDTH, rows), lambda i: (0, 0)),
                pl.BlockSpec((2 * HEAD_SIZE, rows), lambda i: (0, 0)),
            ],
            out_specs=pl.BlockSpec((WIDTH, block), lambda i: (0, i)),
            compiler_params=VMEM,
            cost_estimate=pl.CostEstimate(
                flops=4_000_000_000, bytes_accessed=4_000_000, transcendentals=0
            ),
        )(local, near, extra)
        back_chunks, d_rows = call(
            finish_body,
            [shaped((n_tile * WIDTH, 128)), shaped((WIDTH, rows))],
            [phase, local, main, dquery] + returned,
            smem=(0,),
        )
        back_rows = lax.all_to_all(
            back_chunks.reshape(n_tile, WIDTH, 128), "tile", 0, 0, tiled=True
        ).reshape(n_tile * WIDTH, 128)
    with jax.named_scope("back"):
        back = call(
            back_body, shaped((devices * 8, half)), [back_rows, qkv_weight, pick0, pick1]
        )
        back = lax.all_to_all(
            back.reshape(devices, 8, half), every, 0, 0, tiled=True
        ).reshape(devices * 8, half)
        d_embedded = call(collect_body, shaped((slots, wide)), [back, base])
    with jax.named_scope("qkv_grad"):
        all_rows = lax.all_gather(emb_rows, "tile", axis=0, tiled=True)
        qkv_part = lax.dot_general(
            all_rows, d_rows, (((0,), (1,)), ((), ())), preferred_element_type=FLOATS
        ).astype(HALFS)
        qkv_parts = lax.all_to_all(
            qkv_part.reshape(n_slide, wide // n_slide, WIDTH), "slide", 0, 0, tiled=True
        )
        qkv_grad = jnp.sum(qkv_parts.astype(FLOATS), axis=0)
    with jax.named_scope("embed_grad"):
        tiles = tile_features.shape[1]
        narrow = tiles // n_slide
        split = tile_features.reshape(slots, n_slide // 2, 2, narrow)
        keep_cols = lax.dynamic_index_in_dim(split, core, 2, False).reshape(slots, tiles // 2)
        give_cols = lax.dynamic_index_in_dim(split, 1 - core, 2, False).reshape(slots, tiles // 2)
        given = lax.dot_general(
            d_embedded, give_cols, (((0,), (0,)), ((), ())), preferred_element_type=FLOATS
        ).astype(HALFS)
        given = lax.ppermute(given, "slide", [(i, i ^ 1) for i in range(n_slide)])
        kept = lax.dot_general(
            d_embedded, keep_cols, (((0,), (0,)), ((), ())), preferred_element_type=FLOATS
        )
        kept = (kept + given.astype(FLOATS)).astype(HALFS)
        parts = lax.all_to_all(
            kept.reshape(n_tile, wide // n_tile, tiles // 2), "tile", 0, 0, tiled=True
        )
        part = jnp.sum(parts.astype(FLOATS), axis=0)
        part = part.reshape(wide // n_tile, n_slide // 2, narrow).transpose(1, 0, 2)
        same_core = [list(range(c, n_slide, 2)) for c in range(2)]
        part = lax.all_to_all(part, "slide", 0, 0, axis_index_groups=same_core, tiled=True)
        embed_grad = jnp.sum(part, axis=0).T
    with jax.named_scope("feature_grad"):
        feature_grad = lax.dot_general(
            d_embedded, embed_weight, (((1,), (1,)), ((), ())), preferred_element_type=FLOATS
        ).astype(HALFS)
    return feature_grad, embed_grad, qkv_grad


def solution(mesh):
    placed = (P(("slide", "tile"), None), P(), P(), P(("slide", "tile")), P(None, "slide", "tile"))
    return jax.shard_map(
        per_device,
        mesh=mesh,
        in_specs=placed,
        out_specs=(P(("slide", "tile"), None), P("slide", "tile"), P("slide", "tile")),
        check_vma=False,
    )
```

time: 661 us -> 233 us (0.35); the launches traced: 649 us -> 231 us
  waiting for transfers between devices: 305 us -> 40.9 us
  local copies, waits for them, and re-layouts: 180 us -> 9.57 us
  Pallas kernels: 0 us -> 43.8 us
  matrix products: 52.6 us -> 10.8 us
  other arithmetic: 38.3 us -> 3.88 us
  blocking collectives: 28.6 us -> 61.5 us
  starting transfers between devices: 30.4 us -> 43.5 us
    reduce_scatter x2 -> x0, waiting for transfers between devices: 151 us -> none  [the longest x1 83.1 us: per_device(): lax.psum_scatter(qkv_partial, 'tile', scatter_dimension=1, tiled=True)]
    unnamed x10 -> x1, waiting for transfers between devices: 85.3 us -> 0.68 us
    all_to_all x0 -> x3, blocking collectives: none -> 61.5 us  [the longest x1 22 us: per_device(): lax.all_to_all(kept.reshape(n_tile, wide // n_tile, tiles // 2), 'tile',...]
    pallas_call x0 -> x9, Pallas kernels: none -> 43.8 us  [the longest x7 28.5 us: call(): pl.pallas_call(body, out_shape=outs, in_specs=specs, out_specs=jax.tree.m...]
    dot_general x16 -> x5, matrix products: 52.6 us -> 10.8 us  [the longest x1 3.2 us: per_device(): jnp.dot(tile_features, embed_weight, preferred_element_type=FLOATS)]
    scatter x4 -> x0, local copies, waits for them, and re-layouts: 38.3 us -> none  [the longest x2 29.8 us: per_device(): by_position = jnp.zeros((slides * segment, width), jnp.bfloat16).at[local...]
    gather x2 -> x0, local copies, waits for them, and re-layouts: 34 us -> none  [the longest x1 26.7 us: per_device(): d_position[safe_local]]
    all_to_all x3 -> x5, waiting for transfers between devices: 68 us -> 36.9 us  [the longest x1 13.1 us: per_device(): lax.all_to_all(back.reshape(devices, 8, half), every, 0, 0, tiled=True)]
  transfers between devices with their start and end apart: 9 -> 21, of which waited for: 8 -> 7; matrix products, arithmetic and copies ran while one was open for 13% -> 8% of each run, Pallas kernels for 0% -> 15%
where the time goes in v1:
time: 233 us; the launch traced here: 231 us
  blocking collectives  61.5 us (26%)
  Pallas kernels  43.8 us (19%)
  starting transfers between devices  43.5 us (19%)
  waiting for transfers between devices  40.9 us (18%)
  between operations  17 us (7%)
  matrix products  10.8 us (5%)
  local copies, waits for them, and re-layouts  9.57 us (4%)
  other arithmetic  3.88 us (2%)
    pallas_call x7, Pallas kernels, call(): pl.pallas_call(body, out_shape=outs, in_specs=specs, out_specs=jax.tree.m...  28.5 us
    all_to_all x1, blocking collectives, per_device(): lax.all_to_all(kept.reshape(n_tile, wide // n_tile, tiles // 2), 'tile',...  22 us
    all_to_all x1, blocking collectives, per_device(): lax.all_to_all(sent.reshape(devices, 8, half), every, 0, 0, tiled=True)  21.9 us
    all_to_all x1, blocking collectives, per_device(): lax.all_to_all(back_chunks.reshape(n_tile, WIDTH, 128), 'tile', 0, 0, til...  17.6 us
    all_to_all x1, waiting for transfers between devices, per_device(): lax.all_to_all(back.reshape(devices, 8, half), every, 0, 0, tiled=True)  13.1 us
    all_to_all x1, waiting for transfers between devices, per_device(): lax.all_to_all(chunks.reshape(n_tile, CHUNK_ROWS, 128), 'tile', 0, 0, til...  12.3 us
    all_to_all x1, starting transfers between devices, per_device(): lax.all_to_all(jnp.broadcast_to(count, (devices, 1, 128)), every, 0, 0, t...  11.1 us
    pallas_call x1, Pallas kernels, per_device(): pl.pallas_call(near_body, grid=(slides,), out_shape=[shaped((WIDTH, rows)...  10.6 us
  transfers between devices with their start and end apart: 21, of which 7 were waited for; matrix products, arithmetic and copies ran while one was open for 8% of the time, Pallas kernels for 15%

profile of v1, /device:TPU:0, one launch (start us, length us, event | category | flops | bytes accessed | tf_op | source)
XLA Modules:
  0.0 231.0 jit_solution(4225022965677741534)
XLA Ops:
  11.9 11.1 %all-to-all-start = ((s32[128,1,128]{2,1,0:T(1,128)}), s32[128,1,128]{2,1,0:T(1,128)S(1)}, u32[]{:S(2)}, u32[]{:S(2)}) async-start(s32[128,1,128]{2,1,0:T(1,128)} %broadcast_in_dim.3), calls=%async_computation | async-start | bytes 131072 | tf_op jit(solution)/shard_map/counts/all_to_all | solution.py:298
  23.1 3.2 %convolution_convert_fusion.2.emb_ref = bf16[384,768]{1,0:T(8,128)(2,1)} fusion(bf16[384,1536]{1,0:T(8,128)(2,1)} %param.5, bf16[1536,768]{1,0:T(8,128)(2,1)S(1)} %copy-done), kind=kOutput, calls=%fused_computation.4 | convolution fusion | flops 906264576 | bytes 4128768 | tf_op jit(solution)/shard_map/embed/dot_general | solution.py:302
  27.6 4.8 %all-to-all-done = s32[128,1,128]{2,1,0:T(1,128)S(1)} async-done(((s32[128,1,128]{2,1,0:T(1,128)}), s32[128,1,128]{2,1,0:T(1,128)S(1)}, u32[]{:S(2)}, u32[]{:S(2)}) %all-to-all-start) | async-done | bytes 65568 | tf_op jit(solution)/shard_map/counts/all_to_all | solution.py:298
  33.1 3.8 %dispatch.1 = (bf16[1024,384]{1,0:T(8,128)(2,1)}, s32[384,128]{1,0:T(8,128)}) custom-call(s32[1]{0:T(128)} %bitcast.1.me_ref, s32[128,128]{1,0:T(8,128)} %bitcast.42, s32[1,384]{1,0:T(1,128)} %reshape.68.pos_row_ref, s32[384,1]{1,0:T(8,128)} %reshape.84.pos_col_ref, bf16[384,768]{1,0:T(8,128)(2,1)} %convolution_convert_fusion.2.emb_ref), custom_call_target="tpu_custom_call" | custom-call | tf_op jit(solution)/shard_map/dispatch/pallas_call | solution.py:40
  36.9 21.9 %all_to_all.40 = bf16[128,8,384]{2,1,0:T(8,128)(2,1)} all-to-all(bf16[128,8,384]{2,1,0:T(8,128)(2,1)} %bitcast.38), channel_id=1, replica_groups=mesh['slide'=8,'tile'=16] {'slide','tile'}, dimensions={0} | all-to-all | bytes 1572864 | tf_op jit(solution)/shard_map/dispatch/all_to_all | solution.py:310
  58.8 5.2 %project.1 = (bf16[128,768]{1,0:T(8,128)(2,1)}, bf16[2560,128]{1,0:T(8,128)(2,1)}, bf16[1024,128]{1,0:T(8,128)(2,1)}, bf16[1024,128]{1,0:T(8,128)(2,1)}) custom-call(bf16[1024,384]{1,0:T(8,128)(2,1)} %bitcast.33, bf16[768,2304]{1,0:T(8,128)(2,1)} %weight_ref.3), custom_call_target="tpu_custom_call" | custom-call | tf_op jit(solution)/shard_map/project/pallas_call | solution.py:40
  64.0 3.6 %all-to-all-start.2 = ((bf16[16,160,128]{2,1,0:T(8,128)(2,1)}), bf16[16,160,128]{2,1,0:T(8,128)(2,1)S(1)}, u32[]{:S(2)}, u32[]{:S(2)}) async-start(bf16[16,160,128]{2,1,0:T(8,128)(2,1)} %bitcast.40), calls=%async_computation.2 | async-start | bytes 1310720 | tf_op jit(solution)/shard_map/project/all_to_all | solution.py:324
  68.3 12.3 %all-to-all-done.2 = bf16[16,160,128]{2,1,0:T(8,128)(2,1)S(1)} async-done(((bf16[16,160,128]{2,1,0:T(8,128)(2,1)}), bf16[16,160,128]{2,1,0:T(8,128)(2,1)S(1)}, u32[]{:S(2)}, u32[]{:S(2)}) %all-to-all-start.2) | async-done | bytes 655392 | tf_op jit(solution)/shard_map/project/all_to_all | solution.py:324
  81.5 2.4 %dilated.1 = (bf16[48,256]{1,0:T(8,128)(2,1)}, bf16[96,256]{1,0:T(8,128)(2,1)}, bf16[144,2048]{1,0:T(8,128)(2,1)}, s32[8,2048]{1,0:T(8,128)}) custom-call(s32[1]{0:T(128)} %bitcast.phase_ref, bf16[2560,128]{1,0:T(8,128)(2,1)} %bitcast.34), custom_call_target="tpu_custom_call" | custom-call | tf_op jit(solution)/shard_map/dilated/pallas_call | solution.py:40
  85.7 3.2 %collective-permute-start.3 = (bf16[96,256]{1,0:T(8,128)(2,1)}, bf16[96,256]{1,0:T(8,128)(2,1)S(1)}, u32[]{:S(2)}, u32[]{:S(2)}) collective-permute-start(bf16[96,256]{1,0:T(8,128)(2,1)} %get-tuple-element.34.refs_0_), channel_id=1, source_target_pairs={{0,64},{16,80},{32,96},{48,112},{64,0},{80,16},{96,32},{112,48},{1... | collective-permute-start | bytes 147464 | tf_op jit(solution)/shard_map/dilated/ppermute | solution.py:341
  89.3 1.7 collective-permute-start.5
  91.0 10.6 %near.1 = (bf16[144,2048]{1,0:T(8,128)(2,1)}, f32[144,2048]{1,0:T(8,128)}) custom-call(s32[1]{0:T(128)} %bitcast.phase_ref, bf16[144,2048]{1,0:T(8,128)(2,1)} %get-tuple-element.30.rows_ref, s32[8,2048]{1,0:T(8,128)} %get-tuple-element.29.local_ref, bf16[4,48,512]{2,1,0:T(8,128)(2,1)} %bitcast.43), custom_call_target="tpu_custom_call" | custom-call | flops 8000000000 | bytes 8000000 | tf_op jit(solution)/shard_map/near/pallas_call | solution.py:346
  102.3 5.8 %far.1 = (bf16[48,256]{1,0:T(8,128)(2,1)}, f32[96,2048]{1,0:T(8,128)}, bf16[96,256]{1,0:T(8,128)(2,1)}, bf16[96,256]{1,0:T(8,128)(2,1)}, bf16[96,256]{1,0:T(8,12...) custom-call(s32[1]{0:T(128)} %bitcast.phase_ref, ...), custom_call_target="tpu_custom_call" | custom-call | tf_op jit(solution)/shard_map/far/pallas_call | solution.py:40
  108.1 3.3 %collective-permute-start.10 = (bf16[96,256]{1,0:T(8,128)(2,1)}, bf16[96,256]{1,0:T(8,128)(2,1)S(1)}, u32[]{:S(2)}, u32[]{:S(2)}) collective-permute-start(bf16[96,256]{1,0:T(8,128)(2,1)} %get-tuple-element.41), channel_id=1, source_target_pairs={{64,0},{80,16},{96,32},{112,48},{0,64},{16,80},{32,96},{48,112},{6... | collective-permute-start | bytes 147464 | tf_op jit(solution)/shard_map/far/ppermute | solution.py:375
  114.4 2.0 collective-permute-start.8
  116.9 4.7 %unplace.2.main_ref = f32[144,2048]{1,0:T(8,128)} custom-call(s32[8,2048]{1,0:T(8,128)} %get-tuple-element.29.local_ref, f32[144,2048]{1,0:T(8,128)} %get-tuple-element.31.near_ref, f32[96,2048]{1,0:T(8,128)} %get-tuple-element.35.extra_ref), custom_call_target="tpu_custom_call" | custom-call | flops 4000000000 | bytes 4000000 | tf_op jit(solution)/shard_map/unplace/pallas_call | solution.py:380
  122.3 2.7 %unplace.3 = (bf16[2304,128]{1,0:T(8,128)(2,1)}, bf16[144,2048]{1,0:T(8,128)(2,1)}) custom-call(s32[1]{0:T(128)} %bitcast.phase_ref, s32[8,2048]{1,0:T(8,128)} %get-tuple-element.29.local_ref, f32[144,2048]{1,0:T(8,128)} %unplace.2.main_ref, bf16[48,256]{1,0:T(8,128)(2,1)} %get-tuple-element.36.dquery_ref, bf16[96,256]{1,0:T(8,128)(2,1)} %get-tuple-element.37.refs_0_, ...), custom_call_target="tpu_custom_call" | custom-call | tf_op jit(solution)/shard_map/unplace/pallas_call | solution.py:40
  125.0 17.6 %all_to_all.41 = bf16[16,144,128]{2,1,0:T(8,128)(2,1)} all-to-all(bf16[16,144,128]{2,1,0:T(8,128)(2,1)} %bitcast.41), channel_id=1, replica_groups=mesh['slide'=8,'tile'=16] {'tile'}, dimensions={0} | all-to-all | bytes 1179648 | tf_op jit(solution)/shard_map/unplace/all_to_all | solution.py:401
  142.6 5.5 %back.2 = bf16[1024,384]{1,0:T(8,128)(2,1)} custom-call(bf16[2304,128]{1,0:T(8,128)(2,1)} %bitcast.36, bf16[768,2304]{1,0:T(8,128)(2,1)} %weight_ref.3, bf16[1024,128]{1,0:T(8,128)(2,1)} %get-tuple-element.46.pick0_ref, bf16[1024,128]{1,0:T(8,128)(2,1)} %get-tuple-element.47.pick1_ref), custom_call_target="tpu_custom_call" | custom-call | tf_op jit(solution)/shard_map/back/pallas_call | solution.py:40
  148.1 5.7 %all-to-all-start.4 = ((bf16[128,8,384]{2,1,0:T(8,128)(2,1)}), bf16[128,8,384]{2,1,0:T(8,128)(2,1)}, u32[]{:S(2)}, u32[]{:S(2)}) async-start(bf16[128,8,384]{2,1,0:T(8,128)(2,1)} %bitcast.32), calls=%async_computation.4 | async-start | bytes 1572864 | tf_op jit(solution)/shard_map/back/all_to_all | solution.py:408
  153.8 1.7 copy.14
  156.7 13.1 %all-to-all-done.4 = bf16[128,8,384]{2,1,0:T(8,128)(2,1)} async-done(((bf16[128,8,384]{2,1,0:T(8,128)(2,1)}), bf16[128,8,384]{2,1,0:T(8,128)(2,1)}, u32[]{:S(2)}, u32[]{:S(2)}) %all-to-all-start.4) | async-done | bytes 786464 | tf_op jit(solution)/shard_map/back/all_to_all | solution.py:408
  169.8 3.1 %back.3 = bf16[384,768]{1,0:T(8,128)(2,1)} custom-call(bf16[1024,384]{1,0:T(8,128)(2,1)} %bitcast.11.recv_ref, s32[384,128]{1,0:T(8,128)} %get-tuple-element.48.base_ref), custom_call_target="tpu_custom_call" | custom-call | tf_op jit(solution)/shard_map/back/pallas_call | solution.py:40
  172.8 2.0 convolution_convert_fusion.1
  175.1 2.8 %collective-permute-done.14 = bf16[768,768]{1,0:T(8,128)(2,1)S(1)} collective-permute-done((bf16[768,768]{1,0:T(8,128)(2,1)S(1)}, bf16[768,768]{1,0:T(8,128)(2,1)S(1)}, u32[]{:S(2)}, u32[]{:S(2)}) %collective-permute-start.14) | collective-permute-done | bytes 1179680 | tf_op jit(solution)/shard_map/embed_grad/ppermute | solution.py:430
  178.8 22.0 %all_to_all.42 = bf16[16,48,768]{2,1,0:T(8,128)(2,1)S(1)} all-to-all(bf16[16,48,768]{2,1,0:T(8,128)(2,1)S(1)} %bitcast.30), channel_id=1, replica_groups=mesh['slide'=8,'tile'=16] {'tile'}, dimensions={0} | all-to-all | bytes 2359296 | tf_op jit(solution)/shard_map/embed_grad/all_to_all | solution.py:435
  201.8 4.0 %all-to-all-start.6 = ((f32[4,48,192]{2,1,0:T(8,128)}), f32[4,48,192]{2,1,0:T(8,128)}, u32[]{:S(2)}, u32[]{:S(2)}) async-start(f32[4,48,192]{2,1,0:T(8,128)} %copy.15), calls=%async_computation.6 | async-start | bytes 393216 | tf_op jit(solution)/shard_map/embed_grad/all_to_all | solution.py:441
  205.8 2.7 %convolution_convert_fusion.3 = bf16[768,144]{0,1:T(8,128)(2,1)S(1)} fusion(bf16[144,2048]{1,0:T(8,128)(2,1)} %get-tuple-element.50, bf16[2048,768]{1,0:T(8,128)(2,1)} %all-gather.2.cloned.1.call-done), kind=kOutput, calls=%fused_computation.5 | convolution fusion | flops 453095424 | bytes 3956736 | tf_op jit(solution)/shard_map/qkv_grad/dot_general | solution.py:414
  209.6 2.6 %all-to-all-done.6 = f32[4,48,192]{2,1,0:T(8,128)} async-done(((f32[4,48,192]{2,1,0:T(8,128)}), f32[4,48,192]{2,1,0:T(8,128)}, u32[]{:S(2)}, u32[]{:S(2)}) %all-to-all-start.6) | async-done | bytes 147488 | tf_op jit(solution)/shard_map/embed_grad/all_to_all | solution.py:441
  212.2 3.4 %all-to-all-start.7 = ((bf16[8,96,144]{1,2,0:T(8,128)(2,1)}), bf16[8,96,144]{1,2,0:T(8,128)(2,1)S(1)}, u32[]{:S(2)}, u32[]{:S(2)}) async-start(bf16[8,96,144]{1,2,0:T(8,128)(2,1)} %copy.16), calls=%async_computation.7 | async-start | bytes 589824 | tf_op jit(solution)/shard_map/qkv_grad/all_to_all | solution.py:417
  215.6 2.1 convolution_convert_fusion
  219.3 4.1 %all-to-all-done.7 = bf16[8,96,144]{1,2,0:T(8,128)(2,1)S(1)} async-done(((bf16[8,96,144]{1,2,0:T(8,128)(2,1)}), bf16[8,96,144]{1,2,0:T(8,128)(2,1)S(1)}, u32[]{:S(2)}, u32[]{:S(2)}) %all-to-all-start.7) | async-done | bytes 221216 | tf_op jit(solution)/shard_map/qkv_grad/all_to_all | solution.py:417
  (83 shorter events, 19.3 us)
Async XLA Ops:
  7.2 15.9 %copy-start = (bf16[1536,768]{1,0:T(8,128)(2,1)S(1)}, bf16[1536,768]{1,0:T(8,128)(2,1)}, u32[]{:S(2)}) copy-start(bf16[1536,768]{1,0:T(8,128)(2,1)} %param.6) | copy-start | bytes 7077892
  11.9 20.6 %all-to-all-start = ((s32[128,1,128]{2,1,0:T(1,128)}), s32[128,1,128]{2,1,0:T(1,128)S(1)}, u32[]{:S(2)}, u32[]{:S(2)}) async-start(s32[128,1,128]{2,1,0:T(1,128)} %broadcast_in_dim.3), calls=%async_computation | async-start | bytes 131072 | tf_op jit(solution)/shard_map/counts/all_to_all | solution.py:298
  23.1 3.2 %copy-start.20 = (s32[384]{0:T(512)S(1)}, s32[384]{0:T(512)}, u32[]{:S(2)}) copy-start(s32[384]{0:T(512)} %param.8) | copy-start | bytes 4612
  32.5 0.6 copy-start.5
  64.0 16.6 %all-to-all-start.2 = ((bf16[16,160,128]{2,1,0:T(8,128)(2,1)}), bf16[16,160,128]{2,1,0:T(8,128)(2,1)S(1)}, u32[]{:S(2)}, u32[]{:S(2)}) async-start(bf16[16,160,128]{2,1,0:T(8,128)(2,1)} %bitcast.40), calls=%async_computation.2 | async-start | bytes 1310720 | tf_op jit(solution)/shard_map/project/all_to_all | solution.py:324
  67.6 138.2 %all-gather.2.cloned.1.call-start = ((), (), s32[]{:S(2)}) async-start(), calls=%async_computation.8 | async-start | bytes 3342336 | tf_op jit(solution)/shard_map/qkv_grad/all_gather | solution.py:413
  80.6 0.8 copy-start.2
  83.9 5.4 %collective-permute-start = (bf16[96,256]{1,0:T(8,128)(2,1)}, bf16[96,256]{1,0:T(8,128)(2,1)S(1)}, u32[]{:S(2)}, u32[]{:S(2)}) collective-permute-start(bf16[96,256]{1,0:T(8,128)(2,1)} %get-tuple-element.34.refs_0_), channel_id=1, source_target_pairs={{0,16},{16,32},{32,48},{48,64},{64,80},{80,96},{96,112},{112,0},{1... | collective-permute-start | bytes 147464 | tf_op jit(solution)/shard_map/dilated/ppermute | solution.py:341
  83.9 7.1 %collective-permute-start.1 = (bf16[96,256]{1,0:T(8,128)(2,1)}, bf16[96,256]{1,0:T(8,128)(2,1)S(1)}, u32[]{:S(2)}, u32[]{:S(2)}) collective-permute-start(bf16[96,256]{1,0:T(8,128)(2,1)} %get-tuple-element.34.refs_0_), channel_id=1, source_target_pairs={{0,32},{16,48},{32,64},{48,80},{64,96},{80,112},{96,0},{112,16},{1... | collective-permute-start | bytes 147464 | tf_op jit(solution)/shard_map/dilated/ppermute | solution.py:341
  84.8 16.8 %collective-permute-start.2 = (bf16[96,256]{1,0:T(8,128)(2,1)}, bf16[96,256]{1,0:T(8,128)(2,1)S(1)}, u32[]{:S(2)}, u32[]{:S(2)}) collective-permute-start(bf16[96,256]{1,0:T(8,128)(2,1)} %get-tuple-element.34.refs_0_), channel_id=1, source_target_pairs={{0,48},{16,64},{32,80},{48,96},{64,112},{80,0},{96,16},{112,32},{1... | collective-permute-start | bytes 147464 | tf_op jit(solution)/shard_map/dilated/ppermute | solution.py:341
  85.7 15.9 %collective-permute-start.3 = (bf16[96,256]{1,0:T(8,128)(2,1)}, bf16[96,256]{1,0:T(8,128)(2,1)S(1)}, u32[]{:S(2)}, u32[]{:S(2)}) collective-permute-start(bf16[96,256]{1,0:T(8,128)(2,1)} %get-tuple-element.34.refs_0_), channel_id=1, source_target_pairs={{0,64},{16,80},{32,96},{48,112},{64,0},{80,16},{96,32},{112,48},{1... | collective-permute-start | bytes 147464 | tf_op jit(solution)/shard_map/dilated/ppermute | solution.py:341
  88.9 12.8 %collective-permute-start.4 = (bf16[96,256]{1,0:T(8,128)(2,1)}, bf16[96,256]{1,0:T(8,128)(2,1)S(1)}, u32[]{:S(2)}, u32[]{:S(2)}) collective-permute-start(bf16[96,256]{1,0:T(8,128)(2,1)} %get-tuple-element.34.refs_0_), channel_id=1, source_target_pairs={{0,80},{16,96},{32,112},{48,0},{64,16},{80,32},{96,48},{112,64},{1... | collective-permute-start | bytes 147464 | tf_op jit(solution)/shard_map/dilated/ppermute | solution.py:341
  89.3 12.3 %copy-start.7 = (bf16[96,256]{1,0:T(8,128)(2,1)}, bf16[96,256]{1,0:T(8,128)(2,1)S(1)}, u32[]{:S(2)}) copy-start(bf16[96,256]{1,0:T(8,128)(2,1)S(1)} %collective-permute-done.refs_1_) | copy-start | bytes 147460
  89.3 12.4 %collective-permute-start.5 = (bf16[96,256]{1,0:T(8,128)(2,1)}, bf16[96,256]{1,0:T(8,128)(2,1)S(1)}, u32[]{:S(2)}, u32[]{:S(2)}) collective-permute-start(bf16[96,256]{1,0:T(8,128)(2,1)} %get-tuple-element.34.refs_0_), channel_id=1, source_target_pairs={{0,96},{16,112},{32,0},{48,16},{64,32},{80,48},{96,64},{112,80},{1... | collective-permute-start | bytes 147464 | tf_op jit(solution)/shard_map/dilated/ppermute | solution.py:341
  91.0 10.6 %copy-start.9 = (bf16[96,256]{1,0:T(8,128)(2,1)}, bf16[96,256]{1,0:T(8,128)(2,1)S(1)}, u32[]{:S(2)}) copy-start(bf16[96,256]{1,0:T(8,128)(2,1)S(1)} %collective-permute-done.1.refs_2_) | copy-start | bytes 147460
  91.0 10.7 %collective-permute-start.6 = (bf16[96,256]{1,0:T(8,128)(2,1)}, bf16[96,256]{1,0:T(8,128)(2,1)S(1)}, u32[]{:S(2)}, u32[]{:S(2)}) collective-permute-start(bf16[96,256]{1,0:T(8,128)(2,1)} %get-tuple-element.34.refs_0_), channel_id=1, source_target_pairs={{0,112},{16,0},{32,16},{48,32},{64,48},{80,64},{96,80},{112,96},{1... | collective-permute-start | bytes 147464 | tf_op jit(solution)/shard_map/dilated/ppermute | solution.py:341
  108.1 6.3 %collective-permute-start.10 = (bf16[96,256]{1,0:T(8,128)(2,1)}, bf16[96,256]{1,0:T(8,128)(2,1)S(1)}, u32[]{:S(2)}, u32[]{:S(2)}) collective-permute-start(bf16[96,256]{1,0:T(8,128)(2,1)} %get-tuple-element.41), channel_id=1, source_target_pairs={{64,0},{80,16},{96,32},{112,48},{0,64},{16,80},{32,96},{48,112},{6... | collective-permute-start | bytes 147464 | tf_op jit(solution)/shard_map/far/ppermute | solution.py:375
  111.4 5.5 %collective-permute-start.11 = (bf16[96,256]{1,0:T(8,128)(2,1)}, bf16[96,256]{1,0:T(8,128)(2,1)S(1)}, u32[]{:S(2)}, u32[]{:S(2)}) collective-permute-start(bf16[96,256]{1,0:T(8,128)(2,1)} %get-tuple-element.42), channel_id=1, source_target_pairs={{80,0},{96,16},{112,32},{0,48},{16,64},{32,80},{48,96},{64,112},{8... | collective-permute-start | bytes 147464 | tf_op jit(solution)/shard_map/far/ppermute | solution.py:375
  111.4 10.2 %collective-permute-start.12 = (bf16[96,256]{1,0:T(8,128)(2,1)}, bf16[96,256]{1,0:T(8,128)(2,1)S(1)}, u32[]{:S(2)}, u32[]{:S(2)}) collective-permute-start(bf16[96,256]{1,0:T(8,128)(2,1)} %get-tuple-element.43), channel_id=1, source_target_pairs={{96,0},{112,16},{0,32},{16,48},{32,64},{48,80},{64,96},{80,112},{9... | collective-permute-start | bytes 147464 | tf_op jit(solution)/shard_map/far/ppermute | solution.py:375
  111.4 10.1 %collective-permute-start.13 = (bf16[96,256]{1,0:T(8,128)(2,1)}, bf16[96,256]{1,0:T(8,128)(2,1)S(1)}, u32[]{:S(2)}, u32[]{:S(2)}) collective-permute-start(bf16[96,256]{1,0:T(8,128)(2,1)} %get-tuple-element.44), channel_id=1, source_target_pairs={{112,0},{0,16},{16,32},{32,48},{48,64},{64,80},{80,96},{96,112},{1... | collective-permute-start | bytes 147464 | tf_op jit(solution)/shard_map/far/ppermute | solution.py:375
  113.0 8.6 %collective-permute-start.7 = (bf16[96,256]{1,0:T(8,128)(2,1)}, bf16[96,256]{1,0:T(8,128)(2,1)S(1)}, u32[]{:S(2)}, u32[]{:S(2)}) collective-permute-start(bf16[96,256]{1,0:T(8,128)(2,1)} %get-tuple-element.38), channel_id=1, source_target_pairs={{16,0},{32,16},{48,32},{64,48},{80,64},{96,80},{112,96},{0,112},{1... | collective-permute-start | bytes 147464 | tf_op jit(solution)/shard_map/far/ppermute | solution.py:375
  114.4 7.2 %copy-start.6 = (bf16[96,256]{1,0:T(8,128)(2,1)}, bf16[96,256]{1,0:T(8,128)(2,1)S(1)}, u32[]{:S(2)}) copy-start(bf16[96,256]{1,0:T(8,128)(2,1)S(1)} %collective-permute-done.10.refs_4_) | copy-start | bytes 147460
  114.4 7.2 %collective-permute-start.8 = (bf16[96,256]{1,0:T(8,128)(2,1)}, bf16[96,256]{1,0:T(8,128)(2,1)S(1)}, u32[]{:S(2)}, u32[]{:S(2)}) collective-permute-start(bf16[96,256]{1,0:T(8,128)(2,1)} %get-tuple-element.39), channel_id=1, source_target_pairs={{32,0},{48,16},{64,32},{80,48},{96,64},{112,80},{0,96},{16,112},{3... | collective-permute-start | bytes 147464 | tf_op jit(solution)/shard_map/far/ppermute | solution.py:375
  116.9 4.7 %copy-start.8 = (bf16[96,256]{1,0:T(8,128)(2,1)}, bf16[96,256]{1,0:T(8,128)(2,1)S(1)}, u32[]{:S(2)}) copy-start(bf16[96,256]{1,0:T(8,128)(2,1)S(1)} %collective-permute-done.11.refs_5_) | copy-start | bytes 147460
  116.9 4.8 %collective-permute-start.9 = (bf16[96,256]{1,0:T(8,128)(2,1)}, bf16[96,256]{1,0:T(8,128)(2,1)S(1)}, u32[]{:S(2)}, u32[]{:S(2)}) collective-permute-start(bf16[96,256]{1,0:T(8,128)(2,1)} %get-tuple-element.40), channel_id=1, source_target_pairs={{48,0},{64,16},{80,32},{96,48},{112,64},{0,80},{16,96},{32,112},{4... | collective-permute-start | bytes 147464 | tf_op jit(solution)/shard_map/far/ppermute | solution.py:375
  148.1 21.7 %all-to-all-start.4 = ((bf16[128,8,384]{2,1,0:T(8,128)(2,1)}), bf16[128,8,384]{2,1,0:T(8,128)(2,1)}, u32[]{:S(2)}, u32[]{:S(2)}) async-start(bf16[128,8,384]{2,1,0:T(8,128)(2,1)} %bitcast.32), calls=%async_computation.4 | async-start | bytes 1572864 | tf_op jit(solution)/shard_map/back/all_to_all | solution.py:408
  156.7 16.1 %copy-start.4 = (bf16[384,4,1,192]{0,3,2,1:T(8,128)(2,1)S(1)}, bf16[384,4,1,192]{0,3,2,1:T(8,128)(2,1)}, u32[]{:S(2)}) copy-start(bf16[384,4,1,192]{0,3,2,1:T(8,128)(2,1)} %get-tuple-element.51) | copy-start | bytes 1769476
  172.8 5.1 %copy-start.1 = (bf16[384,768]{1,0:T(8,128)(2,1)S(1)}, bf16[384,768]{1,0:T(8,128)(2,1)}, u32[]{:S(2)}) copy-start(bf16[384,768]{1,0:T(8,128)(2,1)} %back.3) | copy-start | bytes 1769476
  172.8 5.1 %copy-start.3 = (bf16[384,4,1,192]{0,3,2,1:T(8,128)(2,1)S(1)}, bf16[384,4,1,192]{0,3,2,1:T(8,128)(2,1)}, u32[]{:S(2)}) copy-start(bf16[384,4,1,192]{0,3,2,1:T(8,128)(2,1)} %get-tuple-element.52) | copy-start | bytes 1769476
  174.8 3.1 %collective-permute-start.14 = (bf16[768,768]{1,0:T(8,128)(2,1)S(1)}, bf16[768,768]{1,0:T(8,128)(2,1)S(1)}, u32[]{:S(2)}, u32[]{:S(2)}) collective-permute-start(bf16[768,768]{1,0:T(8,128)(2,1)S(1)} %convolution_convert_fusion.1), channel_id=1, source_target_pairs={{0,16},{16,0},{32,48},{48,32},{64,80},{80,64},{96,112},{112,96},{1... | collective-permute-start | bytes 3538952 | tf_op jit(solution)/shard_map/embed_grad/ppermute | solution.py:430
  201.8 10.4 %all-to-all-start.6 = ((f32[4,48,192]{2,1,0:T(8,128)}), f32[4,48,192]{2,1,0:T(8,128)}, u32[]{:S(2)}, u32[]{:S(2)}) async-start(f32[4,48,192]{2,1,0:T(8,128)} %copy.15), calls=%async_computation.6 | async-start | bytes 393216 | tf_op jit(solution)/shard_map/embed_grad/all_to_all | solution.py:441
  212.2 11.2 %all-to-all-start.7 = ((bf16[8,96,144]{1,2,0:T(8,128)(2,1)}), bf16[8,96,144]{1,2,0:T(8,128)(2,1)S(1)}, u32[]{:S(2)}, u32[]{:S(2)}) async-start(bf16[8,96,144]{1,2,0:T(8,128)(2,1)} %copy.16), calls=%async_computation.7 | async-start | bytes 589824 | tf_op jit(solution)/shard_map/qkv_grad/all_to_all | solution.py:417
  (10 other events, 6.2 us)
Sparse Core Ops, SparseCore 0:
  70.6 47.1 all-gather.1

commit v2 on v1

--- a/solution.py
+++ b/solution.py
@@ -51,43 +51,46 @@
     return jax.ShapeDtypeStruct(shape, dtype)
 
 
-def place(pos, rank, off):
+def place(pos, live, rank, few):
     row = (pos & 4095) >> 9
-    dest = row * 16 + ((rank + off) & 15)
-    return dest * 8, rank >> 4
-
-
-def dispatch_body(me_ref, counts_ref, pos_row_ref, pos_col_ref, emb_ref, send_ref, base_ref):
-    slots = emb_ref.shape[0]
-    half = emb_ref.shape[1] // 2
-    counts = counts_ref[...]
-    before = (iota(counts.shape, 0) < me_ref[0]) & (iota(counts.shape, 1) == 0)
-    off = jnp.sum(
-        jnp.sum(jnp.where(before, counts, 0), axis=0, keepdims=True), axis=1, keepdims=True
-    )
+    dest = row * 128 + jnp.where(few, rank * 16, (rank & 15) * 8)
+    sub = jnp.where(few, 0, rank >> 4)
+    base = jnp.where(live, dest + 2 * sub, -16)
+    twin = jnp.where(live & few, dest + 8, -16)
+    return base, twin, sub
+
+
+def dispatch_body(pos_row_ref, pos_col_ref, tiles_ref, send_ref, base_ref):
+    slots = tiles_ref.shape[0]
+    half = tiles_ref.shape[1] // 2
     pos = pos_row_ref[...]
     live = pos >= 0
+    few = jnp.sum(jnp.where(live, 1, 0), axis=1, keepdims=True) <= 64
     pos = jnp.where(live, pos, 0)
     member = ((pos & 4095) >> 9 == iota((8, slots), 0)) & live
     upper = hot(iota((slots, slots), 0) < iota((slots, slots), 1))
     ranks = dot(hot(member), upper)
     rank = jnp.sum(jnp.where(member, ranks, 0.0), axis=0, keepdims=True).astype(jnp.int32)
-    dest, sub = place(pos, rank, off)
-    base = jnp.where(live, dest + 2 * sub, -16)
-    note = jnp.where(live, dest + 6, -16)
+    base, twin, sub = place(pos, live, rank, few)
+    note = jnp.where(live, base - 2 * sub + 6, -16)
+    note_twin = jnp.where(live & few, twin + 6, -16)
     local = ((pos >> 12) << 9) + (pos & 511)
-    lane = iota((128, slots), 0)
+    lane = iota((128, slots), 0) - 4 * sub
     notes = jnp.where(
-        lane == 4 * sub, (local >> 7) + 1, jnp.where(lane == 4 * sub + 1, local & 127, 0)
+        lane == 0,
+        (local >> 7) + 1,
+        jnp.where(lane == 1, local & 127, jnp.where((lane == 2) & few, 1, 0)),
     )
     notes = notes.astype(FLOATS).astype(HALFS)
     step = 256
     for start in range(0, send_ref.shape[0], step):
         rows = iota((step, slots), 0) + start
-        out = dot(hot(rows == base), emb_ref[:, :half])
-        out = out + dot(hot(rows == base + 1), emb_ref[:, half:])
+        out = dot(hot((rows == base) | (rows == twin)), tiles_ref[:, :half])
+        out = out + dot(
+            hot((rows == base + 1) | (rows == twin + 1)), tiles_ref[:, half:]
+        )
         send_ref[start : start + step, :] = out.astype(HALFS)
-        info = dot(hot(rows == note), notes, "nt")
+        info = dot(hot((rows == note) | (rows == note_twin)), notes, "nt")
         send_ref[start : start + step, :128] = (out[:, :128] + info).astype(HALFS)
     pos = pos_col_ref[...]
     live = pos >= 0
@@ -96,18 +99,33 @@
     lower = hot(iota((slots, slots), 0) > iota((slots, slots), 1))
     ranks = dot(lower, hot(member))
     rank = jnp.sum(jnp.where(member, ranks, 0.0), axis=1, keepdims=True).astype(jnp.int32)
-    dest, sub = place(pos, rank, off)
-    base_ref[...] = jnp.broadcast_to(jnp.where(live, dest + 2 * sub, -16), base_ref.shape)
-
-
-def project_body(recv_ref, weight_ref, emb_ref, chunk_ref, pick0_ref, pick1_ref):
+    base, twin, sub = place(pos, live, rank, few)
+    base_ref[...] = jnp.where(iota(base_ref.shape, 1) == 0, base, twin)
+
+
+def project_body(
+    odd_ref,
+    recv_ref,
+    embed_ref,
+    weight_ref,
+    emb_ref,
+    tiles_ref,
+    chunk_ref,
+    pick0_ref,
+    pick1_ref,
+):
     total = recv_ref.shape[0]
     senders = total // 8
     sel = hot(iota((senders, total), 1) == 8 * iota((senders, total), 0) + 6)
     notes = dot(sel, recv_ref[:, :128])
     lane = iota((senders, 128), 1)
-    valid = (notes > 0.5) & ((lane & 3) == 0) & (lane < 12)
     lower = hot(iota((senders, senders), 0) > iota((senders, senders), 1))
+    shared = (notes > 0.5) & (lane == 2)
+    order = dot(lower, hot(shared)).astype(jnp.int32)
+    other = shared & ((order & 1) != odd_ref[0])
+    to_first = hot((iota((128, 128), 0) == 2) & (iota((128, 128), 1) == 0))
+    other = dot(hot(other), to_first) > 0.5
+    valid = (notes > 0.5) & ((lane & 3) == 0) & (lane < 12) & jnp.logical_not(other)
     cum = dot(lower, hot(valid))
     ones = jnp.where(valid, 1.0, 0.0)
     first = jnp.sum(jnp.where(lane == 0, ones, 0.0), axis=0, keepdims=True)
@@ -132,13 +150,13 @@
     pick0_ref[...] = pick0
     pick1_ref[...] = pick1
     half = recv_ref.shape[1]
-    emb_ref[:, :half] = dot(pick0, recv_ref[...], "tn").astype(HALFS)
-    emb_ref[:, half:] = dot(pick1, recv_ref[...], "tn").astype(HALFS)
+    tiles_ref[:, :half] = dot(pick0, recv_ref[...], "tn").astype(HALFS)
+    tiles_ref[:, half:] = dot(pick1, recv_ref[...], "tn").astype(HALFS)
+    emb_ref[...] = dot(tiles_ref[...], embed_ref[...]).astype(HALFS)
     info = jnp.where(lanes == 0, high, jnp.where(lanes == 1, low, 0.0)).astype(HALFS)
     info = dot(info, pick0, "tn")[:16].astype(HALFS)
     heads = chunk_ref.shape[0] // CHUNK_ROWS
     for head in range(heads):
-        columns = slice(head * WIDTH, (head + 1) * WIDTH)
         top = head * CHUNK_ROWS
         if head % 8 == 0:
             wide = slice(head * WIDTH, (head + 8) * WIDTH)
@@ -162,7 +180,8 @@
         local_ref[:, lanes] = jnp.broadcast_to(local, (8, 128))
         total = total + dot(part, hot(target == local), "nt")
     query_ref[...] = total[:HEAD_SIZE].astype(HALFS)
-    far_ref[...] = total[HEAD_SIZE:].astype(HALFS)
+    for copy in range(far_ref.shape[0]):
+        far_ref[copy] = total[HEAD_SIZE:].astype(HALFS)
 
 
 def near_body(phase_ref, rows_ref, local_ref, grad_ref, place_ref, near_ref):
@@ -190,9 +209,10 @@
     near_ref[2 * HEAD_SIZE :, :] = dot(grad, prob.astype(HALFS), "nt")
 
 
-def far_body(phase_ref, query_ref, place_ref, grad_ref, *refs):
-    n = (len(refs) - 2) // 2
-    far_refs, dquery_ref, near_ref, out_refs = refs[:n], refs[n], refs[n + 1], refs[n + 2 :]
+def far_body(
+    phase_ref, query_ref, place_ref, grad_ref, far_ref, dquery_ref, near_ref, out_ref
+):
+    n = far_ref.shape[0]
     seg = grad_ref.shape[2]
     for pair in range(grad_ref.shape[0] // 2):
         lanes = slice(pair * 128, (pair + 1) * 128)
@@ -205,11 +225,12 @@
         grad = grad.astype(HALFS)
         key = jnp.concatenate(
             [place_ref[HEAD_SIZE : 2 * HEAD_SIZE, spots]]
-            + [ref[:HEAD_SIZE, lanes] for ref in far_refs],
+            + [far_ref[k, :HEAD_SIZE, lanes] for k in range(n)],
             axis=1,
         )
         value = jnp.concatenate(
-            [place_ref[2 * HEAD_SIZE :, spots]] + [ref[HEAD_SIZE:, lanes] for ref in far_refs],
+            [place_ref[2 * HEAD_SIZE :, spots]]
+            + [far_ref[k, HEAD_SIZE:, lanes] for k in range(n)],
             axis=1,
         )
         size = key.shape[1]
@@ -228,10 +249,10 @@
         dvalue = dot(grad, prob.astype(HALFS), "nt")
         near_ref[:HEAD_SIZE, spots] = dkey[:, : 2 * seg]
         near_ref[HEAD_SIZE:, spots] = dvalue[:, : 2 * seg]
-        for k, ref in enumerate(out_refs):
+        for k in range(n):
             part = slice(2 * seg + k * 128, 2 * seg + (k + 1) * 128)
-            ref[:HEAD_SIZE, lanes] = dkey[:, part].astype(HALFS)
-            ref[HEAD_SIZE:, lanes] = dvalue[:, part].astype(HALFS)
+            out_ref[k, :HEAD_SIZE, lanes] = dkey[:, part].astype(HALFS)
+            out_ref[k, HEAD_SIZE:, lanes] = dvalue[:, part].astype(HALFS)
 
 
 def unplace_body(local_ref, near_ref, extra_ref, out_ref):
@@ -244,11 +265,10 @@
     out_ref[...] = dot(jnp.concatenate([query, rest], axis=0), order)
 
 
-def finish_body(phase_ref, local_ref, main_ref, dquery_ref, *refs):
-    far_refs, chunk_ref, rows_ref = refs[:-2], refs[-2], refs[-1]
-    far = far_refs[0][...].astype(FLOATS)
-    for ref in far_refs[1:]:
-        far = far + ref[...].astype(FLOATS)
+def finish_body(phase_ref, local_ref, main_ref, dquery_ref, far_ref, chunk_ref, rows_ref):
+    far = far_ref[0].astype(FLOATS)
+    for k in range(1, far_ref.shape[0]):
+        far = far + far_ref[k].astype(FLOATS)
     sparse = jnp.concatenate([dquery_ref[...], far.astype(HALFS)], axis=0)
     local = local_ref[0:1, :]
     count = dquery_ref.shape[1]
@@ -261,19 +281,28 @@
         ]
 
 
-def back_body(rows_ref, weight_ref, pick0_ref, pick1_ref, back_ref):
+def tiles_grad_body(rows_ref, weight_ref, keep_ref, give_ref, grad_ref, kept_ref, given_ref):
+    grad = dot(weight_ref[...], rows_ref[...]).astype(HALFS)
+    grad_ref[...] = grad
+    given_ref[...] = dot(grad, give_ref[...]).astype(HALFS)
+    kept_ref[...] = dot(grad, keep_ref[...])
+
+
+def back_body(grad_ref, pick0_ref, pick1_ref, back_ref):
     half = back_ref.shape[1]
-    grad = dot(weight_ref[...], rows_ref[...]).astype(HALFS)
-    back = dot(pick0_ref[...], grad[:half], "nt") + dot(pick1_ref[...], grad[half:], "nt")
+    back = dot(pick0_ref[...], grad_ref[:half], "nt")
+    back = back + dot(pick1_ref[...], grad_ref[half:], "nt")
     back_ref[...] = back.astype(HALFS)
 
 
 def collect_body(recv_ref, base_ref, out_ref):
     total, half = recv_ref.shape
-    base = base_ref[:, 0:1]
+    base, twin = base_ref[:, 0:1], base_ref[:, 1:2]
     rows = iota((base.shape[0], total), 1)
-    out_ref[:, :half] = dot(hot(rows == base), recv_ref[...]).astype(HALFS)
-    out_ref[:, half:] = dot(hot(rows == base + 1), recv_ref[...]).astype(HALFS)
+    both = hot((rows == base) | (rows == twin))
+    out_ref[:, :half] = dot(both, recv_ref[...]).astype(HALFS)
+    both = hot((rows == base + 1) | (rows == twin + 1))
+    out_ref[:, half:] = dot(both, recv_ref[...]).astype(HALFS)
 
 
 def per_device(tile_features, embed_weight, qkv_weight, positions, out_grad):
@@ -289,37 +318,32 @@
     share = rows // n_tile
     row_here = lax.axis_index("slide")
     col_here = lax.axis_index("tile")
-    me = (row_here * n_tile + col_here).astype(jnp.int32).reshape(1)
     phase = (col_here % n_slide).astype(jnp.int32).reshape(1)
+    odd = (col_here % 2).astype(jnp.int32).reshape(1)
     core = row_here % 2
-
-    with jax.named_scope("counts"):
-        count = jnp.sum((positions >= 0).astype(jnp.int32)) // n_slide
-        counts = lax.all_to_all(
-            jnp.broadcast_to(count, (devices, 1, 128)), every, 0, 0, tiled=True
-        ).reshape(devices, 128)
-    with jax.named_scope("embed"):
-        embedded = jnp.dot(tile_features, embed_weight, preferred_element_type=FLOATS).astype(HALFS)
+    tiles = tile_features.shape[1]
+
     with jax.named_scope("dispatch"):
         sent, base = call(
             dispatch_body,
-            [shaped((devices * 8, half)), shaped((slots, 128), jnp.int32)],
-            [me, counts, positions.reshape(1, slots), positions.reshape(slots, 1), embedded],
-            smem=(0,),
+            [shaped((devices * 8, tiles // 2)), shaped((slots, 128), jnp.int32)],
+            [positions.reshape(1, slots), positions.reshape(slots, 1), tile_features],
         )
         arrived = lax.all_to_all(
-            sent.reshape(devices, 8, half), every, 0, 0, tiled=True
-        ).reshape(devices * 8, half)
+            sent.reshape(devices, 8, tiles // 2), every, 0, 0, tiled=True
+        ).reshape(devices * 8, tiles // 2)
     with jax.named_scope("project"):
-        emb_rows, chunks, pick0, pick1 = call(
+        emb_rows, tile_rows, chunks, pick0, pick1 = call(
             project_body,
             [
                 shaped((share, wide)),
+                shaped((share, tiles)),
                 shaped((n_tile * CHUNK_ROWS, 128)),
                 shaped((devices * 8, 128)),
                 shaped((devices * 8, 128)),
             ],
-            [arrived, qkv_weight],
+            [odd, arrived, embed_weight, qkv_weight],
+            smem=(0,),
         )
         chunks = lax.all_to_all(
             chunks.reshape(n_tile, CHUNK_ROWS, 128), "tile", 0, 0, tiled=True
@@ -330,17 +354,14 @@
             dilated_body,
             [
                 shaped((HEAD_SIZE, few)),
-                shaped((2 * HEAD_SIZE, few)),
+                shaped((n_slide, 2 * HEAD_SIZE, few)),
                 shaped((WIDTH, rows)),
                 shaped((8, rows), jnp.int32),
             ],
             [phase, chunks],
             smem=(0,),
         )
-        fars = [far] + [
-            lax.ppermute(far, "slide", [(i, (i + k) % n_slide) for i in range(n_slide)])
-            for k in range(1, n_slide)
-        ]
+        far = lax.all_to_all(far, "slide", 0, 0, tiled=True)
     with jax.named_scope("near"):
         grads = out_grad.transpose(0, 2, 1)
         placed, near = pl.pallas_call(
@@ -363,18 +384,17 @@
             ),
         )(phase, head_rows, local, grads)
     with jax.named_scope("far"):
-        results = call(
+        dquery, extra, far_grads = call(
             far_body,
-            [shaped((HEAD_SIZE, few)), shaped((2 * HEAD_SIZE, rows), FLOATS)]
-            + [shaped((2 * HEAD_SIZE, few))] * n_slide,
-            [phase, query, placed, grads] + fars,
+            [
+                shaped((HEAD_SIZE, few)),
+                shaped((2 * HEAD_SIZE, rows), FLOATS),
+                shaped((n_slide, 2 * HEAD_SIZE, few)),
+            ],
+            [phase, query, placed, grads, far],
             smem=(0,),
         )
-        dquery, extra, outs = results[0], results[1], results[2:]
-        returned = [outs[0]] + [
-            lax.ppermute(outs[k], "slide", [((i + k) % n_slide, i) for i in range(n_slide)])
-            for k in range(1, n_slide)
-        ]
+        far_grads = lax.all_to_all(far_grads, "slide", 0, 0, tiled=True)
     with jax.named_scope("unplace"):
         block = rows // 4
         main = pl.pallas_call(
@@ -395,20 +415,12 @@
         back_chunks, d_rows = call(
             finish_body,
             [shaped((n_tile * WIDTH, 128)), shaped((WIDTH, rows))],
-            [phase, local, main, dquery] + returned,
+            [phase, local, main, dquery, far_grads],
             smem=(0,),
         )
         back_rows = lax.all_to_all(
             back_chunks.reshape(n_tile, WIDTH, 128), "tile", 0, 0, tiled=True
         ).reshape(n_tile * WIDTH, 128)
-    with jax.named_scope("back"):
-        back = call(
-            back_body, shaped((devices * 8, half)), [back_rows, qkv_weight, pick0, pick1]
-        )
-        back = lax.all_to_all(
-            back.reshape(devices, 8, half), every, 0, 0, tiled=True
-        ).reshape(devices * 8, half)
-        d_embedded = call(collect_body, shaped((slots, wide)), [back, base])
     with jax.named_scope("qkv_grad"):
         all_rows = lax.all_gather(emb_rows, "tile", axis=0, tiled=True)
         qkv_part = lax.dot_general(
@@ -417,20 +429,30 @@
         qkv_parts = lax.all_to_all(
             qkv_part.reshape(n_slide, wide // n_slide, WIDTH), "slide", 0, 0, tiled=True
         )
+        back_rows, qkv_parts = lax.optimization_barrier((back_rows, qkv_parts))
         qkv_grad = jnp.sum(qkv_parts.astype(FLOATS), axis=0)
+    with jax.named_scope("tiles_grad"):
+        narrow = tiles // n_slide
+        split = tile_rows.reshape(share, n_slide // 2, 2, narrow)
+        keep_cols = lax.dynamic_index_in_dim(split, core, 2, False).reshape(share, tiles // 2)
+        give_cols = lax.dynamic_index_in_dim(split, 1 - core, 2, False).reshape(share, tiles // 2)
+        grad_rows, kept, given = call(
+            tiles_grad_body,
+            [
+                shaped((wide, share)),
+                shaped((wide, tiles // 2), FLOATS),
+                shaped((wide, tiles // 2)),
+            ],
+            [back_rows, qkv_weight, keep_cols, give_cols],
+        )
+        given = lax.ppermute(given, "slide", [(i, i ^ 1) for i in range(n_slide)])
+    with jax.named_scope("back"):
+        back = call(back_body, shaped((devices * 8, half)), [grad_rows, pick0, pick1])
+        back = lax.all_to_all(
+            back.reshape(devices, 8, half), every, 0, 0, tiled=True
+        ).reshape(devices * 8, half)
+        d_embedded = call(collect_body, shaped((slots, wide)), [back, base])
     with jax.named_scope("embed_grad"):
-        tiles = tile_features.shape[1]
-        narrow = tiles // n_slide
-        split = tile_features.reshape(slots, n_slide // 2, 2, narrow)
-        keep_cols = lax.dynamic_index_in_dim(split, core, 2, False).reshape(slots, tiles // 2)
-        give_cols = lax.dynamic_index_in_dim(split, 1 - core, 2, False).reshape(slots, tiles // 2)
-        given = lax.dot_general(
-            d_embedded, give_cols, (((0,), (0,)), ((), ())), preferred_element_type=FLOATS
-        ).astype(HALFS)
-        given = lax.ppermute(given, "slide", [(i, i ^ 1) for i in range(n_slide)])
-        kept = lax.dot_general(
-            d_embedded, keep_cols, (((0,), (0,)), ((), ())), preferred_element_type=FLOATS
-        )
         kept = (kept + given.astype(FLOATS)).astype(HALFS)
         parts = lax.all_to_all(
             kept.reshape(n_tile, wide // n_tile, tiles // 2), "tile", 0, 0, tiled=True

time: 233 us -> 220 us (0.944)
  blocking collectives: 61.5 us -> 0 us
  waiting for transfers between devices: 40.9 us -> 90 us
  Pallas kernels: 43.8 us -> 50.8 us
  matrix products: 10.8 us -> 5.94 us
  between operations: 17 us -> 14.2 us
    all_to_all x3 -> x0, blocking collectives: 61.5 us -> none  [the longest x1 22 us: per_device(): lax.all_to_all(kept.reshape(n_tile, wide // n_tile, tiles // 2), 'tile',...]
    all_to_all x1 -> x5, waiting for transfers between devices: 4.83 us -> 52.6 us  [the longest x1 24.4 us: per_device(): lax.all_to_all(sent.reshape(devices, 8, tiles // 2), every, 0, 0, tiled=T...]
    all_to_all x1 -> x5, starting transfers between devices: 11.1 us -> 26.5 us  [the longest x1 11.1 us: per_device(): lax.all_to_all(sent.reshape(devices, 8, tiles // 2), every, 0, 0, tiled=T...]
    ppermute x14 -> x0, starting transfers between devices: 15.4 us -> none  [the longest x7 8.29 us: per_device(): lax.ppermute(outs[k], 'slide', [((i + k) % n_slide, i) for i in range(n_s...]
    pallas_call x7 -> x8, Pallas kernels: 28.5 us -> 35.5 us  [call(): pl.pallas_call(body, out_shape=outs, in_specs=specs, out_specs=jax.tree.m...]
    dot_general x3 -> x0, matrix products: 6 us -> none  [the longest x1 3.2 us: per_device(): jnp.dot(tile_features, embed_weight, preferred_element_type=FLOATS)]
    ppermute x1, waiting for transfers between devices: 2.83 us -> 0.01 us  [per_device(): given = lax.ppermute(given, 'slide', [(i, i ^ 1) for i in range(n_slide)])]
    convert_element_type x0 -> x1, other arithmetic: none -> 2.53 us  [per_device(): kept = (kept + given.astype(FLOATS)).astype(HALFS)]
  transfers between devices with their start and end apart: 21 -> 11, of which waited for: 7 -> 8; matrix products, arithmetic and copies ran while one was open for 8% -> 6% of each run, Pallas kernels for 15% -> 15%
where the time goes in v2:
time: 220 us; the launch traced here: 218 us
  waiting for transfers between devices  90 us (41%)
  Pallas kernels  50.8 us (23%)
  starting transfers between devices  41.7 us (19%)
  between operations  14.2 us (6%)
  local copies, waits for them, and re-layouts  11 us (5%)
  matrix products  5.94 us (3%)
  other arithmetic  4.67 us (2%)
    pallas_call x8, Pallas kernels, call(): pl.pallas_call(body, out_shape=outs, in_specs=specs, out_specs=jax.tree.m...  35.5 us
    all_to_all x1, waiting for transfers between devices, per_device(): lax.all_to_all(sent.reshape(devices, 8, tiles // 2), every, 0, 0, tiled=T...  24.4 us
    all_to_all x1, waiting for transfers between devices, per_device(): lax.all_to_all(kept.reshape(n_tile, wide // n_tile, tiles // 2), 'tile',...  15.6 us
    all_to_all x1, waiting for transfers between devices, per_device(): lax.all_to_all(chunks.reshape(n_tile, CHUNK_ROWS, 128), 'tile', 0, 0, til...  14.7 us
    all_to_all x1, waiting for transfers between devices, per_device(): lax.all_to_all(back.reshape(devices, 8, half), every, 0, 0, tiled=True)  13.8 us
    all_to_all x1, starting transfers between devices, per_device(): lax.all_to_all(sent.reshape(devices, 8, tiles // 2), every, 0, 0, tiled=T...  11.1 us
    pallas_call x1, Pallas kernels, per_device(): pl.pallas_call(near_body, grid=(slides,), out_shape=[shaped((WIDTH, rows)...  10.6 us
    all_to_all x1, waiting for transfers between devices, per_device(): lax.all_to_all(back_chunks.reshape(n_tile, WIDTH, 128), 'tile', 0, 0, til...  8.39 us
  transfers between devices with their start and end apart: 11, of which 8 were waited for; matrix products, arithmetic and copies ran while one was open for 6% of the time, Pallas kernels for 15%

profile of v2, /device:TPU:0, one launch (start us, length us, event | category | flops | bytes accessed | tf_op | source)
XLA Modules:
  0.0 218.4 jit_solution(15262833524838195045)
XLA Ops:
  7.2 1.5 reshape.80.pos_col_ref
  8.6 1.2 reshape.64.pos_row_ref
  9.9 4.9 %dispatch.1 = (bf16[1024,768]{1,0:T(8,128)(2,1)}, s32[384,128]{1,0:T(8,128)}) custom-call(s32[1,384]{1,0:T(1,128)} %reshape.64.pos_row_ref, s32[384,1]{1,0:T(8,128)} %reshape.80.pos_col_ref, bf16[384,1536]{1,0:T(8,128)(2,1)} %tiles_ref.1), custom_call_target="tpu_custom_call" | custom-call | tf_op jit(solution)/shard_map/dispatch/pallas_call | solution.py:40
  14.8 11.1 %all-to-all-start = ((bf16[128,8,768]{2,1,0:T(8,128)(2,1)}), bf16[128,8,768]{2,1,0:T(8,128)(2,1)S(1)}, u32[]{:S(2)}, u32[]{:S(2)}) async-start(bf16[128,8,768]{2,1,0:T(8,128)(2,1)} %bitcast.28), calls=%async_computation | async-start | bytes 3145728 | tf_op jit(solution)/shard_map/dispatch/all_to_all | solution.py:332
  26.0 24.4 %all-to-all-done = bf16[128,8,768]{2,1,0:T(8,128)(2,1)S(1)} async-done(((bf16[128,8,768]{2,1,0:T(8,128)(2,1)}), bf16[128,8,768]{2,1,0:T(8,128)(2,1)S(1)}, u32[]{:S(2)}, u32[]{:S(2)}) %all-to-all-start) | async-done | bytes 1572896 | tf_op jit(solution)/shard_map/dispatch/all_to_all | solution.py:332
  51.6 6.9 %project.1 = (bf16[128,768]{1,0:T(8,128)(2,1)}, bf16[128,1536]{1,0:T(8,128)(2,1)}, bf16[2560,128]{1,0:T(8,128)(2,1)}, bf16[1024,128]{1,0:T(8,128)(2,1)}, bf16[1024,128]{1,0:T(8,128)(2,1)}) custom-call(s32[1]{0:T(128)} %bitcast.1.odd_ref, bf16[1024,768]{1,0:T(8,128)(2,1)} %bitcast.23, bf16[1536,768]{1,0:T(8,128)(2,1)} %embed_ref.1, bf16[768,2304]{1,0:T(8,128)(2,1)} %weight_ref.3), custom_call_target="tpu_custom_call" | custom-call | tf_op jit(solution)/shard_map/project/pallas_call | solution.py:40
  58.4 3.7 %all-to-all-start.1 = ((bf16[16,160,128]{2,1,0:T(8,128)(2,1)}), bf16[16,160,128]{2,1,0:T(8,128)(2,1)S(1)}, u32[]{:S(2)}, u32[]{:S(2)}) async-start(bf16[16,160,128]{2,1,0:T(8,128)(2,1)} %bitcast.33), calls=%async_computation.1 | async-start | bytes 1310720 | tf_op jit(solution)/shard_map/project/all_to_all | solution.py:348
  62.1 14.7 %all-to-all-done.1 = bf16[16,160,128]{2,1,0:T(8,128)(2,1)S(1)} async-done(((bf16[16,160,128]{2,1,0:T(8,128)(2,1)}), bf16[16,160,128]{2,1,0:T(8,128)(2,1)S(1)}, u32[]{:S(2)}, u32[]{:S(2)}) %all-to-all-start.1) | async-done | bytes 655392 | tf_op jit(solution)/shard_map/project/all_to_all | solution.py:348
  77.6 2.5 %dilated.1 = (bf16[48,256]{1,0:T(8,128)(2,1)}, bf16[8,96,256]{2,1,0:T(8,128)(2,1)}, bf16[144,2048]{1,0:T(8,128)(2,1)}, s32[8,2048]{1,0:T(8,128)}) custom-call(s32[1]{0:T(128)} %bitcast.phase_ref, bf16[2560,128]{1,0:T(8,128)(2,1)} %bitcast.26), custom_call_target="tpu_custom_call" | custom-call | tf_op jit(solution)/shard_map/dilated/pallas_call | solution.py:40
  80.2 3.5 %all-to-all-start.2 = ((bf16[8,96,256]{2,1,0:T(8,128)(2,1)}), bf16[8,96,256]{2,1,0:T(8,128)(2,1)S(1)}, u32[]{:S(2)}, u32[]{:S(2)}) async-start(bf16[8,96,256]{2,1,0:T(8,128)(2,1)} %get-tuple-element.33), calls=%async_computation.2 | async-start | bytes 786432 | tf_op jit(solution)/shard_map/dilated/all_to_all | solution.py:364
  83.6 10.6 %near.1 = (bf16[144,2048]{1,0:T(8,128)(2,1)}, f32[144,2048]{1,0:T(8,128)}) custom-call(s32[1]{0:T(128)} %bitcast.phase_ref, bf16[144,2048]{1,0:T(8,128)(2,1)} %get-tuple-element.29.rows_ref, s32[8,2048]{1,0:T(8,128)} %get-tuple-element.28.local_ref, bf16[4,48,512]{2,1,0:T(8,128)(2,1)} %bitcast.35), custom_call_target="tpu_custom_call" | custom-call | flops 8000000000 | bytes 8000000 | tf_op jit(solution)/shard_map/near/pallas_call | solution.py:367
  95.0 5.8 %far.1 = (bf16[48,256]{1,0:T(8,128)(2,1)}, f32[96,2048]{1,0:T(8,128)}, bf16[8,96,256]{2,1,0:T(8,128)(2,1)}) custom-call(s32[1]{0:T(128)} %bitcast.phase_ref, bf16[48,256]{1,0:T(8,128)(2,1)} %get-tuple-element.31.query_ref, bf16[144,2048]{1,0:T(8,128)(2,1)} %get-tuple-element.32.place_ref, bf16[4,48,512]{2,1,0:T(8,128)(2,1)} %bitcast.36, ...), custom_call_target="tpu_custom_call" | custom-call | tf_op jit(solution)/shard_map/far/pallas_call | solution.py:40
  100.8 4.7 %all-to-all-start.3 = ((bf16[8,96,256]{2,1,0:T(8,128)(2,1)}), bf16[8,96,256]{2,1,0:T(8,128)(2,1)S(1)}, u32[]{:S(2)}, u32[]{:S(2)}) async-start(bf16[8,96,256]{2,1,0:T(8,128)(2,1)} %get-tuple-element.36), calls=%async_computation.3 | async-start | bytes 786432 | tf_op jit(solution)/shard_map/far/all_to_all | solution.py:397
  105.5 4.7 %unplace.2.main_ref = f32[144,2048]{1,0:T(8,128)} custom-call(s32[8,2048]{1,0:T(8,128)} %get-tuple-element.28.local_ref, f32[144,2048]{1,0:T(8,128)} %get-tuple-element.30.near_ref, f32[96,2048]{1,0:T(8,128)} %get-tuple-element.34.extra_ref), custom_call_target="tpu_custom_call" | custom-call | flops 4000000000 | bytes 4000000 | tf_op jit(solution)/shard_map/unplace/pallas_call | solution.py:400
  110.2 4.2 %all-to-all-done.3.far_ref = bf16[8,96,256]{2,1,0:T(8,128)(2,1)S(1)} async-done(((bf16[8,96,256]{2,1,0:T(8,128)(2,1)}), bf16[8,96,256]{2,1,0:T(8,128)(2,1)S(1)}, u32[]{:S(2)}, u32[]{:S(2)}) %all-to-all-start.3) | async-done | bytes 393248 | tf_op jit(solution)/shard_map/far/all_to_all | solution.py:397
  115.2 2.8 %unplace.3 = (bf16[2304,128]{1,0:T(8,128)(2,1)}, bf16[144,2048]{1,0:T(8,128)(2,1)}) custom-call(s32[1]{0:T(128)} %bitcast.phase_ref, s32[8,2048]{1,0:T(8,128)} %get-tuple-element.28.local_ref, f32[144,2048]{1,0:T(8,128)} %unplace.2.main_ref, bf16[48,256]{1,0:T(8,128)(2,1)} %get-tuple-element.35.dquery_ref, bf16[8,96,256]{2,1,0:T(8,128)(2,1)} %copy-done.6), custom_call_target="tpu_custom_call" | custom-call | tf_op jit(solution)/shard_map/unplace/pallas_call | solution.py:40
  117.9 3.6 %all-to-all-start.4 = ((bf16[16,144,128]{2,1,0:T(8,128)(2,1)}), bf16[16,144,128]{2,1,0:T(8,128)(2,1)S(1)}, u32[]{:S(2)}, u32[]{:S(2)}) async-start(bf16[16,144,128]{2,1,0:T(8,128)(2,1)} %bitcast.34), calls=%async_computation.4 | async-start | bytes 1179648 | tf_op jit(solution)/shard_map/unplace/all_to_all | solution.py:421
  121.5 2.7 %convolution_convert_fusion.1 = bf16[768,144]{0,1:T(8,128)(2,1)S(1)} fusion(bf16[144,2048]{1,0:T(8,128)(2,1)} %get-tuple-element.39, bf16[2048,768]{1,0:T(8,128)(2,1)} %all-gather.2.cloned.1.call-done), kind=kOutput, calls=%fused_computation.3 | convolution fusion | flops 453095424 | bytes 3956736 | tf_op jit(solution)/shard_map/qkv_grad/dot_general | solution.py:426
  125.4 8.4 %all-to-all-done.4 = bf16[16,144,128]{2,1,0:T(8,128)(2,1)S(1)} async-done(((bf16[16,144,128]{2,1,0:T(8,128)(2,1)}), bf16[16,144,128]{2,1,0:T(8,128)(2,1)S(1)}, u32[]{:S(2)}, u32[]{:S(2)}) %all-to-all-start.4) | async-done | bytes 589856 | tf_op jit(solution)/shard_map/unplace/all_to_all | solution.py:421
  133.8 3.4 %all-to-all-start.5 = ((bf16[8,96,144]{1,2,0:T(8,128)(2,1)}), bf16[8,96,144]{1,2,0:T(8,128)(2,1)S(1)}, u32[]{:S(2)}, u32[]{:S(2)}) async-start(bf16[8,96,144]{1,2,0:T(8,128)(2,1)} %copy.20), calls=%async_computation.5 | async-start | bytes 589824 | tf_op jit(solution)/shard_map/qkv_grad/all_to_all | solution.py:429
  139.2 5.9 %all-to-all-done.5 = bf16[8,96,144]{1,2,0:T(8,128)(2,1)S(1)} async-done(((bf16[8,96,144]{1,2,0:T(8,128)(2,1)}), bf16[8,96,144]{1,2,0:T(8,128)(2,1)S(1)}, u32[]{:S(2)}, u32[]{:S(2)}) %all-to-all-start.5) | async-done | bytes 221216 | tf_op jit(solution)/shard_map/qkv_grad/all_to_all | solution.py:429
  145.0 6.8 %tiles_grad.1 = (bf16[768,128]{1,0:T(8,128)(2,1)}, f32[768,768]{1,0:T(8,128)}, bf16[768,768]{1,0:T(8,128)(2,1)}) custom-call(bf16[2304,128]{1,0:T(8,128)(2,1)} %bitcast.27, bf16[768,2304]{1,0:T(8,128)(2,1)} %weight_ref.3, bf16[128,768]{1,0:T(8,128)(2,1)} %copy.22.keep_ref, bf16[128,768]{1,0:T(8,128)(2,1)} %copy.23.give_ref), custom_call_target="tpu_custom_call" | custom-call | tf_op jit(solution)/shard_map/tiles_grad/pallas_call | solution.py:40
  151.9 2.7 %back.2 = bf16[1024,384]{1,0:T(8,128)(2,1)} custom-call(bf16[768,128]{1,0:T(8,128)(2,1)} %get-tuple-element.42.grad_ref, bf16[1024,128]{1,0:T(8,128)(2,1)} %get-tuple-element.43.pick0_ref, bf16[1024,128]{1,0:T(8,128)(2,1)} %get-tuple-element.44.pick1_ref), custom_call_target="tpu_custom_call" | custom-call | tf_op jit(solution)/shard_map/back/pallas_call | solution.py:40
  154.6 4.6 %all-to-all-start.6 = ((bf16[128,8,384]{2,1,0:T(8,128)(2,1)}), bf16[128,8,384]{2,1,0:T(8,128)(2,1)S(1)}, u32[]{:S(2)}, u32[]{:S(2)}) async-start(bf16[128,8,384]{2,1,0:T(8,128)(2,1)} %bitcast.25), calls=%async_computation.6 | async-start | bytes 1572864 | tf_op jit(solution)/shard_map/back/all_to_all | solution.py:451
  159.3 2.5 %add_convert_fusion = bf16[768,768]{1,0:T(8,128)(2,1)} fusion(f32[768,768]{1,0:T(8,128)S(1)} %copy-done.4, bf16[768,768]{1,0:T(8,128)(2,1)} %collective-permute-done), kind=kLoop, calls=%fused_computation.2 | loop fusion | flops 1769472 | bytes 4718592 | tf_op jit(solution)/shard_map/embed_grad/convert_element_type | solution.py:456
  161.8 13.8 %all-to-all-done.6 = bf16[128,8,384]{2,1,0:T(8,128)(2,1)S(1)} async-done(((bf16[128,8,384]{2,1,0:T(8,128)(2,1)}), bf16[128,8,384]{2,1,0:T(8,128)(2,1)S(1)}, u32[]{:S(2)}, u32[]{:S(2)}) %all-to-all-start.6) | async-done | bytes 786464 | tf_op jit(solution)/shard_map/back/all_to_all | solution.py:451
  175.6 3.7 %all-to-all-start.7 = ((bf16[16,48,768]{2,1,0:T(8,128)(2,1)}), bf16[16,48,768]{2,1,0:T(8,128)(2,1)S(1)}, u32[]{:S(2)}, u32[]{:S(2)}) async-start(bf16[16,48,768]{2,1,0:T(8,128)(2,1)} %bitcast.14), calls=%async_computation.7 | async-start | bytes 2359296 | tf_op jit(solution)/shard_map/embed_grad/all_to_all | solution.py:457
  180.0 3.1 %back.3 = bf16[384,768]{1,0:T(8,128)(2,1)} custom-call(bf16[1024,384]{1,0:T(8,128)(2,1)} %bitcast.24, s32[384,128]{1,0:T(8,128)} %get-tuple-element.45.base_ref), custom_call_target="tpu_custom_call" | custom-call | tf_op jit(solution)/shard_map/back/pallas_call | solution.py:40
  183.1 15.6 %all-to-all-done.7 = bf16[16,48,768]{2,1,0:T(8,128)(2,1)S(1)} async-done(((bf16[16,48,768]{2,1,0:T(8,128)(2,1)}), bf16[16,48,768]{2,1,0:T(8,128)(2,1)S(1)}, u32[]{:S(2)}, u32[]{:S(2)}) %all-to-all-start.7) | async-done | bytes 1179680 | tf_op jit(solution)/shard_map/embed_grad/all_to_all | solution.py:457
  201.2 3.4 %all-to-all-start.8 = ((f32[4,48,192]{2,1,0:T(8,128)}), f32[4,48,192]{2,1,0:T(8,128)S(1)}, u32[]{:S(2)}, u32[]{:S(2)}) async-start(f32[4,48,192]{2,1,0:T(8,128)} %copy.24), calls=%async_computation.8 | async-start | bytes 393216 | tf_op jit(solution)/shard_map/embed_grad/all_to_all | solution.py:463
  204.6 3.2 %convolution_convert_fusion = bf16[384,1536]{1,0:T(8,128)(2,1)} fusion(bf16[384,768]{1,0:T(8,128)(2,1)} %back.3, bf16[1536,768]{1,0:T(8,128)(2,1)S(1)} %copy-done.5), kind=kOutput, calls=%fused_computation | convolution fusion | flops 906559488 | bytes 4128768 | tf_op jit(solution)/shard_map/feature_grad/dot_general | solution.py:466
  207.8 3.1 %all-to-all-done.8 = f32[4,48,192]{2,1,0:T(8,128)S(1)} async-done(((f32[4,48,192]{2,1,0:T(8,128)}), f32[4,48,192]{2,1,0:T(8,128)S(1)}, u32[]{:S(2)}, u32[]{:S(2)}) %all-to-all-start.8) | async-done | bytes 147488 | tf_op jit(solution)/shard_map/embed_grad/all_to_all | solution.py:463
  (35 shorter events, 10.5 us)
Async XLA Ops:
  14.8 35.6 %all-to-all-start = ((bf16[128,8,768]{2,1,0:T(8,128)(2,1)}), bf16[128,8,768]{2,1,0:T(8,128)(2,1)S(1)}, u32[]{:S(2)}, u32[]{:S(2)}) async-start(bf16[128,8,768]{2,1,0:T(8,128)(2,1)} %bitcast.28), calls=%async_computation | async-start | bytes 3145728 | tf_op jit(solution)/shard_map/dispatch/all_to_all | solution.py:332
  25.9 95.6 %all-gather.2.cloned.1.call-start = ((), (), s32[]{:S(2)}) async-start(), calls=%async_computation.9 | async-start | bytes 3342336 | tf_op jit(solution)/shard_map/qkv_grad/all_gather | solution.py:425
  50.4 1.2 copy-start
  58.4 18.3 %all-to-all-start.1 = ((bf16[16,160,128]{2,1,0:T(8,128)(2,1)}), bf16[16,160,128]{2,1,0:T(8,128)(2,1)S(1)}, u32[]{:S(2)}, u32[]{:S(2)}) async-start(bf16[16,160,128]{2,1,0:T(8,128)(2,1)} %bitcast.33), calls=%async_computation.1 | async-start | bytes 1310720 | tf_op jit(solution)/shard_map/project/all_to_all | solution.py:348
  76.8 0.8 copy-start.2
  80.2 14.1 %all-to-all-start.2 = ((bf16[8,96,256]{2,1,0:T(8,128)(2,1)}), bf16[8,96,256]{2,1,0:T(8,128)(2,1)S(1)}, u32[]{:S(2)}, u32[]{:S(2)}) async-start(bf16[8,96,256]{2,1,0:T(8,128)(2,1)} %get-tuple-element.33), calls=%async_computation.2 | async-start | bytes 786432 | tf_op jit(solution)/shard_map/dilated/all_to_all | solution.py:364
  94.3 0.7 copy-start.7
  100.8 13.6 %all-to-all-start.3 = ((bf16[8,96,256]{2,1,0:T(8,128)(2,1)}), bf16[8,96,256]{2,1,0:T(8,128)(2,1)S(1)}, u32[]{:S(2)}, u32[]{:S(2)}) async-start(bf16[8,96,256]{2,1,0:T(8,128)(2,1)} %get-tuple-element.36), calls=%async_computation.3 | async-start | bytes 786432 | tf_op jit(solution)/shard_map/far/all_to_all | solution.py:397
  114.4 0.8 copy-start.6
  117.9 15.9 %all-to-all-start.4 = ((bf16[16,144,128]{2,1,0:T(8,128)(2,1)}), bf16[16,144,128]{2,1,0:T(8,128)(2,1)S(1)}, u32[]{:S(2)}, u32[]{:S(2)}) async-start(bf16[16,144,128]{2,1,0:T(8,128)(2,1)} %bitcast.34), calls=%async_computation.4 | async-start | bytes 1179648 | tf_op jit(solution)/shard_map/unplace/all_to_all | solution.py:421
  121.5 15.7 %copy-start.8 = (bf16[128,1536]{1,0:T(8,128)(2,1)S(1)}, bf16[128,1536]{1,0:T(8,128)(2,1)}, u32[]{:S(2)}) copy-start(bf16[128,1536]{1,0:T(8,128)(2,1)} %get-tuple-element.41) | copy-start | bytes 1179652
  133.8 11.2 %copy-start.3 = (bf16[16,144,128]{2,1,0:T(8,128)(2,1)}, bf16[16,144,128]{2,1,0:T(8,128)(2,1)S(1)}, u32[]{:S(2)}) copy-start(bf16[16,144,128]{2,1,0:T(8,128)(2,1)S(1)} %all-to-all-done.4) | copy-start | bytes 1769476
  133.8 11.2 %all-to-all-start.5 = ((bf16[8,96,144]{1,2,0:T(8,128)(2,1)}), bf16[8,96,144]{1,2,0:T(8,128)(2,1)S(1)}, u32[]{:S(2)}, u32[]{:S(2)}) async-start(bf16[8,96,144]{1,2,0:T(8,128)(2,1)} %copy.20), calls=%async_computation.5 | async-start | bytes 589824 | tf_op jit(solution)/shard_map/qkv_grad/all_to_all | solution.py:429
  151.9 7.4 %copy-start.4 = (f32[768,768]{1,0:T(8,128)S(1)}, f32[768,768]{1,0:T(8,128)}, u32[]{:S(2)}) copy-start(f32[768,768]{1,0:T(8,128)} %get-tuple-element.46) | copy-start | bytes 7077892
  151.9 7.4 %collective-permute-start = (bf16[768,768]{1,0:T(8,128)(2,1)}, bf16[768,768]{1,0:T(8,128)(2,1)}, u32[]{:S(2)}, u32[]{:S(2)}) collective-permute-start(bf16[768,768]{1,0:T(8,128)(2,1)} %get-tuple-element.47), channel_id=1, source_target_pairs={{0,16},{16,0},{32,48},{48,32},{64,80},{80,64},{96,112},{112,96},{1... | collective-permute-start | bytes 3538952 | tf_op jit(solution)/shard_map/tiles_grad/ppermute | solution.py:448
  154.6 21.0 %all-to-all-start.6 = ((bf16[128,8,384]{2,1,0:T(8,128)(2,1)}), bf16[128,8,384]{2,1,0:T(8,128)(2,1)S(1)}, u32[]{:S(2)}, u32[]{:S(2)}) async-start(bf16[128,8,384]{2,1,0:T(8,128)(2,1)} %bitcast.25), calls=%async_computation.6 | async-start | bytes 1572864 | tf_op jit(solution)/shard_map/back/all_to_all | solution.py:451
  175.6 4.4 %copy-start.1 = (bf16[128,8,384]{2,1,0:T(8,128)(2,1)}, bf16[128,8,384]{2,1,0:T(8,128)(2,1)S(1)}, u32[]{:S(2)}) copy-start(bf16[128,8,384]{2,1,0:T(8,128)(2,1)S(1)} %all-to-all-done.6) | copy-start | bytes 2359300
  175.6 23.0 %all-to-all-start.7 = ((bf16[16,48,768]{2,1,0:T(8,128)(2,1)}), bf16[16,48,768]{2,1,0:T(8,128)(2,1)S(1)}, u32[]{:S(2)}, u32[]{:S(2)}) async-start(bf16[16,48,768]{2,1,0:T(8,128)(2,1)} %bitcast.14), calls=%async_computation.7 | async-start | bytes 2359296 | tf_op jit(solution)/shard_map/embed_grad/all_to_all | solution.py:457
  183.0 21.5 %copy-start.5 = (bf16[1536,768]{1,0:T(8,128)(2,1)S(1)}, bf16[1536,768]{1,0:T(8,128)(2,1)}, u32[]{:S(2)}) copy-start(bf16[1536,768]{1,0:T(8,128)(2,1)} %embed_ref.1) | copy-start | bytes 7077892
  201.2 9.7 %all-to-all-start.8 = ((f32[4,48,192]{2,1,0:T(8,128)}), f32[4,48,192]{2,1,0:T(8,128)S(1)}, u32[]{:S(2)}, u32[]{:S(2)}) async-start(f32[4,48,192]{2,1,0:T(8,128)} %copy.24), calls=%async_computation.8 | async-start | bytes 393216 | tf_op jit(solution)/shard_map/embed_grad/all_to_all | solution.py:463
Sparse Core Ops, SparseCore 0:
  58.6 45.4 all-gather.1

commit v3 on v2

v3 whole, which is shorter than its diff:
```python
import functools

import jax
import jax.numpy as jnp
from jax import lax
from jax.experimental import pallas as pl
from jax.experimental.pallas import tpu as pltpu
from jax.sharding import PartitionSpec as P

HEAD_SIZE = 48
WIDTH = 3 * HEAD_SIZE
CHUNK_ROWS = 160
FLOATS = jnp.float32
HALFS = jnp.bfloat16
SCALE = HEAD_SIZE ** (-0.5)
VMEM = pltpu.CompilerParams(vmem_limit_bytes=56 * 1024 * 1024)


def iota(shape, dim):
    return lax.broadcasted_iota(jnp.int32, shape, dim)


def hot(cond):
    return jnp.where(cond, 1.0, 0.0).astype(HALFS)


def dot(a, b, dims="nn"):
    contract = (0 if dims[0] == "t" else 1, 1 if dims[1] == "t" else 0)
    return lax.dot_general(
        a, b, (((contract[0],), (contract[1],)), ((), ())), preferred_element_type=FLOATS
    )


def whole(memory=pltpu.VMEM):
    return pl.BlockSpec(memory_space=memory)


def call(body, outs, args, smem=(), **kw):
    specs = [whole(pltpu.SMEM if i in smem else pltpu.VMEM) for i in range(len(args))]
    return pl.pallas_call(
        body,
        out_shape=outs,
        in_specs=specs,
        out_specs=jax.tree.map(lambda _: whole(), outs),
        compiler_params=VMEM,
        **kw,
    )(*args)


def shaped(shape, dtype=HALFS):
    return jax.ShapeDtypeStruct(shape, dtype)


def resident(shape, dtype=HALFS):
    return pltpu.VMEM(shape, dtype)


def stay(*values):
    return [pltpu.with_memory_space_constraint(value, pltpu.VMEM) for value in values]


def place(pos_ref):
    slots = pos_ref.shape[0]
    pos = pos_ref[...].reshape(1, slots)
    live = pos >= 0
    few = jnp.sum(jnp.where(live, 1, 0), axis=1, keepdims=True) <= 64
    pos = jnp.where(live, pos, 0)
    member = ((pos & 4095) >> 9 == iota((8, slots), 0)) & live
    upper = hot(iota((slots, slots), 0) < iota((slots, slots), 1))
    ranks = dot(hot(member), upper)
    rank = jnp.sum(jnp.where(member, ranks, 0.0), axis=0, keepdims=True).astype(jnp.int32)
    dest = ((pos & 4095) >> 9) * 128 + jnp.where(few, rank * 16, (rank & 15) * 8)
    dest = jnp.where(live, dest, -16)
    sub = jnp.where(few, 0, rank >> 4)
    mask = jnp.where(few, -9, -1)
    return pos, few, dest, sub, mask


def dispatch_body(pos_ref, tiles_ref, send_ref):
    slots = tiles_ref.shape[0]
    half = tiles_ref.shape[1] // 2
    pos, few, dest, sub, mask = place(pos_ref)
    base = dest + 2 * sub
    local = ((pos >> 12) << 9) + (pos & 511)
    lane = iota((128, slots), 0) - 4 * sub
    notes = jnp.where(
        lane == 0,
        (local >> 7) + 1,
        jnp.where(lane == 1, local & 127, jnp.where((lane == 2) & few, 1, 0)),
    )
    notes = notes.astype(FLOATS).astype(HALFS)
    step = 256
    for start in range(0, send_ref.shape[0], step):
        rows = (iota((step, slots), 0) + start) & mask
        out = dot(hot(rows == base), tiles_ref[:, :half])
        out = out + dot(hot(rows == base + 1), tiles_ref[:, half:])
        send_ref[start : start + step, :] = out.astype(HALFS)
        info = dot(hot(rows == dest + 6), notes, "nt")
        send_ref[start : start + step, :128] = (out[:, :128] + info).astype(HALFS)


def slots_body(pos_ref, base_ref):
    slots = pos_ref.shape[0]
    _, _, dest, sub, mask = place(pos_ref)
    same = iota((slots, slots), 0) == iota((slots, slots), 1)
    base = jnp.sum(jnp.where(same, dest + 2 * sub, 0), axis=1, keepdims=True)
    base_ref[...] = jnp.where(iota(base_ref.shape, 1) == 0, base, mask)


def project_body(
    odd_ref,
    recv_ref,
    embed_ref,
    weight_ref,
    emb_ref,
    tiles_ref,
    chunk_ref,
    pick0_ref,
    pick1_ref,
):
    total = recv_ref.shape[0]
    senders = total // 8
    sel = hot(iota((senders, total), 1) == 8 * iota((senders, total), 0) + 6)
    notes = dot(sel, recv_ref[:, :128])
    lane = iota((senders, 128), 1)
    lower = hot(iota((senders, senders), 0) > iota((senders, senders), 1))
    shared = (notes > 0.5) & (lane == 2)
    order = dot(lower, hot(shared)).astype(jnp.int32)
    other = shared & ((order & 1) != odd_ref[0])
    to_first = hot((iota((128, 128), 0) == 2) & (iota((128, 128), 1) == 0))
    other = dot(hot(other), to_first) > 0.5
    valid = (notes > 0.5) & ((lane & 3) == 0) & (lane < 12) & jnp.logical_not(other)
    cum = dot(lower, hot(valid))
    ones = jnp.where(valid, 1.0, 0.0)
    first = jnp.sum(jnp.where(lane == 0, ones, 0.0), axis=0, keepdims=True)
    first = jnp.sum(first, axis=1, keepdims=True)
    second = jnp.sum(jnp.where(lane == 4, ones, 0.0), axis=0, keepdims=True)
    second = jnp.sum(second, axis=1, keepdims=True)
    shift = jnp.where(lane >= 4, first, 0.0) + jnp.where(lane >= 8, second, 0.0)
    index = jnp.where(valid, cum + shift, -1.0)
    repeat = hot(iota((total, senders), 0) >> 3 == iota((total, senders), 1))
    index_all = dot(repeat, index.astype(HALFS))
    notes_all = dot(repeat, notes.astype(HALFS))
    turn = iota((total, 128), 0) & 7
    lanes = iota((total, 128), 1)
    mine = (lanes == 4 * (turn >> 1)) & (turn < 6)
    mine_low = (lanes == 4 * (turn >> 1) + 1) & (turn < 6)
    spot = jnp.sum(jnp.where(mine, index_all + 1.0, 0.0), axis=1, keepdims=True) - 1.0
    high = jnp.sum(jnp.where(mine, notes_all, 0.0), axis=1, keepdims=True)
    low = jnp.sum(jnp.where(mine_low, notes_all, 0.0), axis=1, keepdims=True)
    match = spot.astype(jnp.int32) == lanes
    pick0 = hot(match & ((turn & 1) == 0))
    pick1 = hot(match & ((turn & 1) == 1))
    pick0_ref[...] = pick0
    pick1_ref[...] = pick1
    half = recv_ref.shape[1]
    tiles_ref[:, :half] = dot(pick0, recv_ref[...], "tn").astype(HALFS)
    tiles_ref[:, half:] = dot(pick1, recv_ref[...], "tn").astype(HALFS)
    emb_ref[...] = dot(tiles_ref[...], embed_ref[...]).astype(HALFS)
    info = jnp.where(lanes == 0, high, jnp.where(lanes == 1, low, 0.0)).astype(HALFS)
    info = dot(info, pick0, "tn")[:16].astype(HALFS)
    heads = chunk_ref.shape[0] // CHUNK_ROWS
    for head in range(heads):
        top = head * CHUNK_ROWS
        if head % 8 == 0:
            wide = slice(head * WIDTH, (head + 8) * WIDTH)
            part = dot(emb_ref[...], weight_ref[:, wide]).T
        columns = slice((head % 8) * WIDTH, (head % 8 + 1) * WIDTH)
        chunk_ref[top : top + WIDTH, :] = part[columns].astype(HALFS)
        chunk_ref[top + WIDTH : top + CHUNK_ROWS, :] = info


def dilated_body(phase_ref, chunk_ref, query_ref, far_ref, rows_ref, local_ref):
    blocks = chunk_ref.shape[0] // CHUNK_ROWS
    total = jnp.zeros((WIDTH, query_ref.shape[1]), FLOATS)
    target = 8 * iota((query_ref.shape[1], 128), 0) + phase_ref[0]
    for block in range(blocks):
        top = block * CHUNK_ROWS
        lanes = slice(block * 128, (block + 1) * 128)
        part = chunk_ref[top : top + WIDTH, :]
        info = chunk_ref[top + WIDTH : top + CHUNK_ROWS, :].astype(FLOATS)
        local = ((info[0:1] - 1.0) * 128.0 + info[1:2]).astype(jnp.int32)
        rows_ref[:, lanes] = part
        local_ref[:, lanes] = jnp.broadcast_to(local, (8, 128))
        total = total + dot(part, hot(target == local), "nt")
    query_ref[...] = total[:HEAD_SIZE].astype(HALFS)
    for copy in range(far_ref.shape[0]):
        far_ref[copy] = total[HEAD_SIZE:].astype(HALFS)


def near_body(phase_ref, rows_ref, local_ref, grad_ref, place_ref, near_ref):
    seg = grad_ref.shape[2]
    local = local_ref[0:1, :]
    dilated = (iota((1, seg), 1) & 7) == phase_ref[0]
    for slide in range(grad_ref.shape[0]):
        spots = slice(slide * seg, (slide + 1) * seg)
        order = hot(local == iota((seg, local.shape[1]), 0) + slide * seg)
        parts = dot(rows_ref[...], order, "nt").astype(HALFS)
        place_ref[:, spots] = parts
        query = parts[:HEAD_SIZE]
        key = parts[HEAD_SIZE : 2 * HEAD_SIZE]
        value = parts[2 * HEAD_SIZE :]
        grad = grad_ref[slide]
        score = dot(key, query, "tn") * SCALE
        top = jnp.max(score, axis=0, keepdims=True)
        prob = jnp.exp(score - top)
        norm = 1.0 / jnp.sum(prob, axis=0, keepdims=True)
        prob = prob * jnp.where(dilated, 0.0, norm)
        dprob = dot(value, grad, "tn")
        delta = jnp.sum(prob * dprob, axis=0, keepdims=True)
        dscore = (prob * (dprob - delta)).astype(HALFS)
        near_ref[:HEAD_SIZE, spots] = dot(key, dscore) * SCALE
        near_ref[HEAD_SIZE : 2 * HEAD_SIZE, spots] = dot(query, dscore, "nt") * SCALE
        near_ref[2 * HEAD_SIZE :, spots] = dot(grad, prob.astype(HALFS), "nt")


def pick_body(phase_ref, grad_ref, out_ref):
    seg = grad_ref.shape[2]
    for pair in range(grad_ref.shape[0] // 2):
        grad = jnp.zeros((HEAD_SIZE, 128), FLOATS)
        for b in range(2):
            target = 8 * (iota((seg, 128), 1) - 64 * b) + phase_ref[0]
            grad = grad + dot(grad_ref[2 * pair + b], hot(iota((seg, 128), 0) == target))
        out_ref[:, pair * 128 : (pair + 1) * 128] = grad.astype(HALFS)


def far_body(query_ref, grad_ref, place_ref, far_ref, out_ref, dscore_ref, prob_ref):
    n = far_ref.shape[0]
    near = place_ref.shape[1] // 2
    seg = near // 2
    for pair in range(2):
        lanes = slice(pair * 128, (pair + 1) * 128)
        spots = slice(pair * near, (pair + 1) * near)
        query = query_ref[:, lanes]
        grad = grad_ref[:, lanes]
        key = jnp.concatenate(
            [place_ref[HEAD_SIZE : 2 * HEAD_SIZE, spots]]
            + [far_ref[k, :HEAD_SIZE, lanes] for k in range(n)],
            axis=1,
        )
        value = jnp.concatenate(
            [place_ref[2 * HEAD_SIZE :, spots]]
            + [far_ref[k, HEAD_SIZE:, lanes] for k in range(n)],
            axis=1,
        )
        size = key.shape[1]
        row = iota((size, 128), 0)
        slide_of_key = jnp.where(row < near, row // seg, (row & 127) >> 6)
        same = slide_of_key == iota((size, 128), 1) >> 6
        score = jnp.where(same, dot(key, query, "tn") * SCALE, -1e30)
        top = jnp.max(score, axis=0, keepdims=True)
        prob = jnp.exp(score - top)
        prob = prob * (1.0 / jnp.sum(prob, axis=0, keepdims=True))
        dprob = dot(value, grad, "tn")
        delta = jnp.sum(prob * dprob, axis=0, keepdims=True)
        dscore = (prob * (dprob - delta)).astype(HALFS)
        prob = prob.astype(HALFS)
        dkey = dot(query, dscore[near:], "nt") * SCALE
        dvalue = dot(grad, prob[near:], "nt")
        for k in range(n):
            part = slice(k * 128, (k + 1) * 128)
            out_ref[k, :HEAD_SIZE, lanes] = dkey[:, part].astype(HALFS)
            out_ref[k, HEAD_SIZE:, lanes] = dvalue[:, part].astype(HALFS)
        dscore_ref[pair] = dscore
        prob_ref[pair] = prob[:near]


def sum_body(
    query_ref,
    grad_ref,
    place_ref,
    far_ref,
    dscore_ref,
    prob_ref,
    near_ref,
    dquery_ref,
    sum_ref,
):
    near = place_ref.shape[1] // 2
    sum_ref[:HEAD_SIZE, :] = near_ref[:HEAD_SIZE, :].astype(HALFS)
    for pair in range(2):
        lanes = slice(pair * 128, (pair + 1) * 128)
        spots = slice(pair * near, (pair + 1) * near)
        query = query_ref[:, lanes]
        grad = grad_ref[:, lanes]
        key = jnp.concatenate(
            [place_ref[HEAD_SIZE : 2 * HEAD_SIZE, spots]]
            + [far_ref[k, :HEAD_SIZE, lanes] for k in range(far_ref.shape[0])],
            axis=1,
        )
        dscore = dscore_ref[pair]
        dquery_ref[:, lanes] = (dot(key, dscore) * SCALE).astype(HALFS)
        dkey = dot(query, dscore[:near], "nt") * SCALE
        dvalue = dot(grad, prob_ref[pair], "nt")
        middle = slice(HEAD_SIZE, 2 * HEAD_SIZE)
        sum_ref[middle, spots] = (near_ref[middle, spots] + dkey).astype(HALFS)
        last = slice(2 * HEAD_SIZE, WIDTH)
        sum_ref[last, spots] = (near_ref[last, spots] + dvalue).astype(HALFS)


def unplace_body(local_ref, sum_ref, out_ref):
    block = 512
    for start in range(0, out_ref.shape[1], block):
        lanes = slice(start, start + block)
        order = hot(local_ref[0:1, lanes] == iota((sum_ref.shape[1], block), 0))
        out_ref[:, lanes] = dot(sum_ref[...], order)


def finish_body(phase_ref, local_ref, main_ref, dquery_ref, far_ref, chunk_ref, rows_ref):
    far = far_ref[0].astype(FLOATS)
    for k in range(1, far_ref.shape[0]):
        far = far + far_ref[k].astype(FLOATS)
    sparse = jnp.concatenate([dquery_ref[...], far.astype(HALFS)], axis=0)
    local = local_ref[0:1, :]
    count = dquery_ref.shape[1]
    order = hot(local == 8 * iota((count, local.shape[1]), 0) + phase_ref[0])
    rows = (main_ref[...] + dot(sparse, order)).astype(HALFS)
    rows_ref[...] = rows
    for block in range(chunk_ref.shape[0] // WIDTH):
        chunk_ref[block * WIDTH : (block + 1) * WIDTH, :] = rows[
            :, block * 128 : (block + 1) * 128
        ]


def qkv_grad_body(grad_ref, rows_ref, out_ref):
    out_ref[...] = dot(grad_ref[...], rows_ref[...]).T


def tiles_grad_body(rows_ref, weight_ref, give_ref, grad_ref, given_ref):
    grad = dot(weight_ref[...], rows_ref[...]).astype(HALFS)
    grad_ref[...] = grad
    for block in range(give_ref.shape[0]):
        given_ref[block] = dot(give_ref[block], grad, "nt").astype(HALFS)


def merge_body(chip_ref, grad_ref, keep_ref, given_ref, own_ref, *piece_refs):
    chips = keep_ref.shape[0]
    for k in range(chips):
        block = (chip_ref[0] + k) & (chips - 1)
        part = dot(keep_ref[block], grad_ref[...], "nt") + given_ref[block].astype(FLOATS)
        if k == 0:
            own_ref[...] = part
        else:
            piece_refs[k - 1][...] = part.astype(HALFS)


def back_body(grad_ref, pick0_ref, pick1_ref, back_ref):
    half = back_ref.shape[1]
    back = dot(pick0_ref[...], grad_ref[:half], "nt")
    back = back + dot(pick1_ref[...], grad_ref[half:], "nt")
    back_ref[...] = back.astype(HALFS)


def collect_body(recv_ref, base_ref, out_ref):
    total, half = recv_ref.shape
    base, mask = base_ref[:, 0:1], base_ref[:, 1:2]
    rows = iota((base.shape[0], total), 1) & mask
    out_ref[:, :half] = dot(hot(rows == base), recv_ref[...]).astype(HALFS)
    out_ref[:, half:] = dot(hot(rows == base + 1), recv_ref[...]).astype(HALFS)


def per_device(tile_features, embed_weight, qkv_weight, positions, out_grad):
    n_slide = lax.axis_size("slide")
    n_tile = lax.axis_size("tile")
    devices = n_slide * n_tile
    every = ("slide", "tile")
    slots = tile_features.shape[0]
    slides, seg = out_grad.shape[0], out_grad.shape[1]
    wide = embed_weight.shape[1]
    half = wide // 2
    rows = slides * seg
    share = rows // n_tile
    row_here = lax.axis_index("slide")
    col_here = lax.axis_index("tile")
    phase = (col_here % n_slide).astype(jnp.int32).reshape(1)
    odd = (col_here % 2).astype(jnp.int32).reshape(1)
    core = row_here % 2
    tiles = tile_features.shape[1]

    with jax.named_scope("dispatch"):
        sent = call(
            dispatch_body, shaped((devices * 8, tiles // 2)), [positions, tile_features]
        )
        base = call(slots_body, resident((slots, 128), jnp.int32), [positions])
        arrived = lax.all_to_all(
            sent.reshape(devices, 8, tiles // 2), every, 0, 0, tiled=True
        ).reshape(devices * 8, tiles // 2)
    with jax.named_scope("project"):
        emb_rows, tile_rows, chunks, pick0, pick1 = call(
            project_body,
            [
                shaped((share, wide)),
                shaped((share, tiles)),
                shaped((n_tile * CHUNK_ROWS, 128)),
                resident((devices * 8, 128)),
                resident((devices * 8, 128)),
            ],
            [odd, *stay(arrived), embed_weight, qkv_weight],
            smem=(0,),
        )
        chunks = lax.all_to_all(
            chunks.reshape(n_tile, CHUNK_ROWS, 128), "tile", 0, 0, tiled=True
        ).reshape(n_tile * CHUNK_ROWS, 128)
    with jax.named_scope("dilated"):
        few = rows // n_slide
        query, far, head_rows, local = call(
            dilated_body,
            [
                resident((HEAD_SIZE, few)),
                shaped((n_slide, 2 * HEAD_SIZE, few)),
                resident((WIDTH, rows)),
                resident((8, rows), jnp.int32),
            ],
            [phase, *stay(chunks)],
            smem=(0,),
        )
        far = lax.all_to_all(far, "slide", 0, 0, tiled=True)
    with jax.named_scope("near"):
        grads = out_grad.transpose(0, 2, 1)
        dilated_grads = call(pick_body, resident((HEAD_SIZE, few)), [phase, grads], smem=(0,))
        placed, near = call(
            near_body,
            [resident((WIDTH, rows)), resident((WIDTH, rows), FLOATS)],
            [phase, *stay(head_rows, local), grads],
            smem=(0,),
            cost_estimate=pl.CostEstimate(
                flops=8_000_000_000, bytes_accessed=8_000_000, transcendentals=1 << 20
            ),
        )
    with jax.named_scope("far"):
        far_grads, dscores, probs = call(
            far_body,
            [
                shaped((n_slide, 2 * HEAD_SIZE, few)),
                resident((2, rows, 128)),
                resident((2, rows // 2, 128)),
            ],
            stay(query, dilated_grads, placed, far),
        )
        far_grads = lax.all_to_all(far_grads, "slide", 0, 0, tiled=True)
    with jax.named_scope("unplace"):
        dquery, summed = call(
            sum_body,
            [resident((HEAD_SIZE, few)), resident((WIDTH, rows))],
            stay(query, dilated_grads, placed, far, dscores, probs, near),
        )
        main = call(
            unplace_body,
            resident((WIDTH, rows), FLOATS),
            stay(local, summed),
            cost_estimate=pl.CostEstimate(
                flops=4_000_000_000, bytes_accessed=4_000_000, transcendentals=0
            ),
        )
        back_chunks, d_rows = call(
            finish_body,
            [shaped((n_tile * WIDTH, 128)), resident((WIDTH, rows))],
            [phase, *stay(local, main, dquery, far_grads)],
            smem=(0,),
        )
        back_rows = lax.all_to_all(
            back_chunks.reshape(n_tile, WIDTH, 128), "tile", 0, 0, tiled=True
        ).reshape(n_tile * WIDTH, 128)
    with jax.named_scope("qkv_grad"):
        all_rows = lax.all_gather(emb_rows, "tile", axis=0, tiled=True)
        qkv_part = call(
            qkv_grad_body, shaped((wide, WIDTH), FLOATS), [*stay(d_rows), all_rows]
        )
        back_rows, qkv_part = lax.optimization_barrier((back_rows, qkv_part))
        qkv_grad = lax.psum_scatter(qkv_part, "slide", scatter_dimension=0, tiled=True)
    with jax.named_scope("tiles_grad"):
        narrow = tiles // n_slide
        chips = n_slide // 2
        split = tile_rows.reshape(share, chips, 2, narrow)
        keep_cols = lax.dynamic_index_in_dim(split, core, 2, False).transpose(1, 2, 0)
        give_cols = lax.dynamic_index_in_dim(split, 1 - core, 2, False).transpose(1, 2, 0)
        grad_rows, given = call(
            tiles_grad_body,
            [resident((wide, share)), shaped((chips, narrow, wide))],
            [*stay(back_rows), qkv_weight, give_cols],
        )
        given = lax.ppermute(given, "slide", [(i, i ^ 1) for i in range(n_slide)])
        own, *pieces = call(
            merge_body,
            [shaped((narrow, wide), FLOATS)] + [shaped((narrow, wide))] * (chips - 1),
            [(row_here // 2).astype(jnp.int32).reshape(1), *stay(grad_rows), keep_cols, *stay(given)],
            smem=(0,),
        )
    with jax.named_scope("back"):
        back = call(back_body, shaped((devices * 8, half)), stay(grad_rows, pick0, pick1))
        back, pieces = lax.optimization_barrier((back, pieces))
        part = own
        for k in range(1, chips):
            piece = lax.ppermute(
                pieces[k - 1], "slide", [(i, (i + 2 * k) % n_slide) for i in range(n_slide)]
            )
            part = part + piece.astype(FLOATS)
        part = part.astype(HALFS).T
        back = lax.all_to_all(
            back.reshape(devices, 8, half), every, 0, 0, tiled=True
        ).reshape(devices * 8, half)
        back, part = lax.optimization_barrier((back, part))
        d_embedded = call(collect_body, shaped((slots, wide)), stay(back, base))
    with jax.named_scope("embed_grad"):
        parts = lax.all_to_all(
            part.reshape(n_tile, wide // n_tile, narrow), "tile", 0, 0, tiled=True
        )
        parts, qkv_grad = lax.optimization_barrier((parts, qkv_grad))
        embed_grad = jnp.sum(parts.astype(FLOATS), axis=0).T
    with jax.named_scope("feature_grad"):
        feature_grad = lax.dot_general(
            d_embedded, embed_weight, (((1,), (1,)), ((), ())), preferred_element_type=FLOATS
        ).astype(HALFS)
    return feature_grad, embed_grad, qkv_grad


def solution(mesh):
    placed = (P(("slide", "tile"), None), P(), P(), P(("slide", "tile")), P(None, "slide", "tile"))
    return jax.shard_map(
        per_device,
        mesh=mesh,
        in_specs=placed,
        out_specs=(P(("slide", "tile"), None), P("slide", "tile"), P("slide", "tile")),
        check_vma=False,
    )
```

time: 220 us -> 194 us (0.88)
  waiting for transfers between devices: 90 us -> 78.3 us
  Pallas kernels: 50.8 us -> 44.7 us
  matrix products: 5.94 us -> 3.19 us
    ppermute x0 -> x3, waiting for transfers between devices: none -> 21.7 us  [per_device(): lax.ppermute(pieces[k - 1], 'slide', [(i, (i + 2 * k) % n_slide) for i in...]
    all_to_all x3 -> x1, waiting for transfers between devices: 24.5 us -> 4.45 us  [per_device(): lax.all_to_all(part.reshape(n_tile, wide // n_tile, narrow), 'tile', 0, 0...]
    pallas_call x2 -> x0, Pallas kernels: 15.3 us -> none  [the longest x1 10.6 us: per_device(): pl.pallas_call(near_body, grid=(slides,), out_shape=[shaped((WIDTH, rows)...]
    all_to_all x1, waiting for transfers between devices: 13.8 us -> 0.01 us  [per_device(): lax.all_to_all(back.reshape(devices, 8, half), every, 0, 0, tiled=True)]
    pallas_call x8 -> x15, Pallas kernels: 35.5 us -> 44.7 us  [call(): pl.pallas_call(body, out_shape=outs, in_specs=specs, out_specs=jax.tree.m...]
    reshape x7 -> x0, local copies, waits for them, and re-layouts: 6.53 us -> none  [the longest x1 1.48 us: per_device(): positions.reshape(slots, 1)]
    all_to_all x3 -> x1, starting transfers between devices: 10.5 us -> 5.17 us  [per_device(): lax.all_to_all(part.reshape(n_tile, wide // n_tile, narrow), 'tile', 0, 0...]
    ppermute x0 -> x3, starting transfers between devices: none -> 4.34 us  [per_device(): lax.ppermute(pieces[k - 1], 'slide', [(i, (i + 2 * k) % n_slide) for i in...]
  transfers between devices with their start and end apart: 11 -> 13, of which waited for: 8 -> 10; matrix products, arithmetic and copies ran while one was open for 6% -> 4% of each run, Pallas kernels for 15% -> 14%
where the time goes in v3:
time: 194 us; the launch traced here: 193 us
  waiting for transfers between devices  78.3 us (40%)
  Pallas kernels  44.7 us (23%)
  starting transfers between devices  41.1 us (21%)
  between operations  14.2 us (7%)
  local copies, waits for them, and re-layouts  8.98 us (5%)
  matrix products  3.19 us (2%)
  other arithmetic  2.53 us (1%)
    pallas_call x15, Pallas kernels, call(): pl.pallas_call(body, out_shape=outs, in_specs=specs, out_specs=jax.tree.m...  44.7 us
    all_to_all x1, waiting for transfers between devices, per_device(): lax.all_to_all(sent.reshape(devices, 8, tiles // 2), every, 0, 0, tiled=T...  24.4 us
    ppermute x3, waiting for transfers between devices, per_device(): lax.ppermute(pieces[k - 1], 'slide', [(i, (i + 2 * k) % n_slide) for i in...  21.7 us
    all_to_all x1, waiting for transfers between devices, per_device(): lax.all_to_all(chunks.reshape(n_tile, CHUNK_ROWS, 128), 'tile', 0, 0, til...  13.5 us
    all_to_all x1, starting transfers between devices, per_device(): lax.all_to_all(sent.reshape(devices, 8, tiles // 2), every, 0, 0, tiled=T...  11.1 us
    all_to_all x1, waiting for transfers between devices, per_device(): lax.all_to_all(back_chunks.reshape(n_tile, WIDTH, 128), 'tile', 0, 0, til...  6.42 us
    all_to_all x1, waiting for transfers between devices, per_device(): far_grads = lax.all_to_all(far_grads, 'slide', 0, 0, tiled=True)  5.57 us
    all_to_all x1, starting transfers between devices, per_device(): lax.all_to_all(part.reshape(n_tile, wide // n_tile, narrow), 'tile', 0, 0...  5.17 us
  transfers between devices with their start and end apart: 13, of which 10 were waited for; matrix products, arithmetic and copies ran while one was open for 4% of the time, Pallas kernels for 14%

profile of v3, /device:TPU:0, one launch (start us, length us, event | category | flops | bytes accessed | tf_op | source)
XLA Modules:
  0.0 193.1 jit_solution(12720752309521802339)
XLA Ops:
  7.2 4.7 %dispatch.2 = bf16[1024,768]{1,0:T(8,128)(2,1)} custom-call(s32[384]{0:T(512)} %pos_ref.3, bf16[384,1536]{1,0:T(8,128)(2,1)} %tiles_ref.1), custom_call_target="tpu_custom_call" | custom-call | tf_op jit(solution)/shard_map/dispatch/pallas_call | solution.py:40
  11.8 11.1 %all-to-all-start = ((bf16[128,8,768]{2,1,0:T(8,128)(2,1)}), bf16[128,8,768]{2,1,0:T(8,128)(2,1)S(1)}, u32[]{:S(2)}, u32[]{:S(2)}) async-start(bf16[128,8,768]{2,1,0:T(8,128)(2,1)} %bitcast.31), calls=%async_computation | async-start | bytes 3145728 | tf_op jit(solution)/shard_map/dispatch/all_to_all | solution.py:385
  23.0 24.4 %all-to-all-done = bf16[128,8,768]{2,1,0:T(8,128)(2,1)S(1)} async-done(((bf16[128,8,768]{2,1,0:T(8,128)(2,1)}), bf16[128,8,768]{2,1,0:T(8,128)(2,1)S(1)}, u32[]{:S(2)}, u32[]{:S(2)}) %all-to-all-start) | async-done | bytes 1572896 | tf_op jit(solution)/shard_map/dispatch/all_to_all | solution.py:385
  47.4 6.4 %project.1 = (bf16[128,768]{1,0:T(8,128)(2,1)}, bf16[128,1536]{1,0:T(8,128)(2,1)}, bf16[2560,128]{1,0:T(8,128)(2,1)}, bf16[1024,128]{1,0:T(8,128)(2,1)S(1)}, bf16[1024,128]{1,0:T(8,128)(2,1)S(1)}) custom-call(s32[1]{0:T(128)} %bitcast.1.odd_ref, bf16[1024,768]{1,0:T(8,128)(2,1)S(1)} %bitcast.27, bf16[1536,768]{1,0:T(8,128)(2,1)} %embed_ref.1, ...), custom_call_target="tpu_custom_call" | custom-call | tf_op jit(solution)/shard_map/project/pallas_call | solution.py:40
  53.8 3.7 %all-to-all-start.1 = ((bf16[16,160,128]{2,1,0:T(8,128)(2,1)}), bf16[16,160,128]{2,1,0:T(8,128)(2,1)S(1)}, u32[]{:S(2)}, u32[]{:S(2)}) async-start(bf16[16,160,128]{2,1,0:T(8,128)(2,1)} %bitcast.34), calls=%async_computation.1 | async-start | bytes 1310720 | tf_op jit(solution)/shard_map/project/all_to_all | solution.py:401
  58.7 13.5 %all-to-all-done.1 = bf16[16,160,128]{2,1,0:T(8,128)(2,1)S(1)} async-done(((bf16[16,160,128]{2,1,0:T(8,128)(2,1)}), bf16[16,160,128]{2,1,0:T(8,128)(2,1)S(1)}, u32[]{:S(2)}, u32[]{:S(2)}) %all-to-all-start.1) | async-done | bytes 655392 | tf_op jit(solution)/shard_map/project/all_to_all | solution.py:401
  72.2 1.3 dilated.1
  73.4 3.6 %all-to-all-start.2 = ((bf16[8,96,256]{2,1,0:T(8,128)(2,1)}), bf16[8,96,256]{2,1,0:T(8,128)(2,1)S(1)}, u32[]{:S(2)}, u32[]{:S(2)}) async-start(bf16[8,96,256]{2,1,0:T(8,128)(2,1)} %get-tuple-element.42), calls=%async_computation.2 | async-start | bytes 786432 | tf_op jit(solution)/shard_map/dilated/all_to_all | solution.py:417
  78.2 8.6 %near.3 = (bf16[144,2048]{1,0:T(8,128)(2,1)S(1)}, f32[144,2048]{1,0:T(8,128)S(1)}) custom-call(s32[1]{0:T(128)} %bitcast.phase_ref, bf16[144,2048]{1,0:T(8,128)(2,1)S(1)} %copy-done.5, s32[8,2048]{1,0:T(8,128)S(1)} %get-tuple-element.38.local_ref, bf16[4,48,512]{2,1,0:T(8,128)(2,1)} %bitcast.37), custom_call_target="tpu_custom_call" | custom-call | flops 8000000000 | bytes 8000000 | tf_op jit(solution)/shard_map/near/pallas_call | solution.py:40
  86.8 3.8 %far.1 = (bf16[8,96,256]{2,1,0:T(8,128)(2,1)}, bf16[2,2048,128]{2,1,0:T(8,128)(2,1)S(1)}, bf16[2,1024,128]{2,1,0:T(8,128)(2,1)S(1)}) custom-call(bf16[48,256]{1,0:T(8,128)(2,1)S(1)} %get-tuple-element.39.query_ref, bf16[48,256]{1,0:T(8,128)(2,1)S(1)} %near.2.grad_ref, bf16[144,2048]{1,0:T(8,128)(2,1)S(1)} %get-tuple-element.41.place_ref, ...), custom_call_target="tpu_custom_call" | custom-call | tf_op jit(solution)/shard_map/far/pallas_call | solution.py:40
  91.6 4.5 %all-to-all-start.3 = ((bf16[8,96,256]{2,1,0:T(8,128)(2,1)}), bf16[8,96,256]{2,1,0:T(8,128)(2,1)S(1)}, u32[]{:S(2)}, u32[]{:S(2)}) async-start(bf16[8,96,256]{2,1,0:T(8,128)(2,1)} %get-tuple-element.48), calls=%async_computation.3 | async-start | bytes 786432 | tf_op jit(solution)/shard_map/far/all_to_all | solution.py:440
  98.0 1.5 unplace.4.main_ref
  99.5 5.6 %all-to-all-done.3.far_ref = bf16[8,96,256]{2,1,0:T(8,128)(2,1)S(1)} async-done(((bf16[8,96,256]{2,1,0:T(8,128)(2,1)}), bf16[8,96,256]{2,1,0:T(8,128)(2,1)S(1)}, u32[]{:S(2)}, u32[]{:S(2)}) %all-to-all-start.3) | async-done | bytes 393248 | tf_op jit(solution)/shard_map/far/all_to_all | solution.py:440
  106.2 3.8 %all-to-all-start.4 = ((bf16[16,144,128]{2,1,0:T(8,128)(2,1)}), bf16[16,144,128]{2,1,0:T(8,128)(2,1)S(1)}, u32[]{:S(2)}, u32[]{:S(2)}) async-start(bf16[16,144,128]{2,1,0:T(8,128)(2,1)} %bitcast.35), calls=%async_computation.4 | async-start | bytes 1179648 | tf_op jit(solution)/shard_map/unplace/all_to_all | solution.py:461
  112.1 3.6 %qkv_grad.1 = f32[768,144]{1,0:T(8,128)} custom-call(bf16[144,2048]{1,0:T(8,128)(2,1)S(1)} %get-tuple-element.50.grad_ref, bf16[2048,768]{1,0:T(8,128)(2,1)} %all-gather.2.cloned.1.call-done.rows_ref), custom_call_target="tpu_custom_call" | custom-call | tf_op jit(solution)/shard_map/qkv_grad/pallas_call | solution.py:40
  115.7 6.4 %all-to-all-done.4 = bf16[16,144,128]{2,1,0:T(8,128)(2,1)S(1)} async-done(((bf16[16,144,128]{2,1,0:T(8,128)(2,1)}), bf16[16,144,128]{2,1,0:T(8,128)(2,1)S(1)}, u32[]{:S(2)}, u32[]{:S(2)}) %all-to-all-start.4) | async-done | bytes 589856 | tf_op jit(solution)/shard_map/unplace/all_to_all | solution.py:461
  122.1 5.1 %tiles_grad.2 = (bf16[768,128]{1,0:T(8,128)(2,1)S(1)}, bf16[4,192,768]{2,1,0:T(8,128)(2,1)}) custom-call(bf16[2304,128]{1,0:T(8,128)(2,1)S(1)} %bitcast.30, bf16[768,2304]{1,0:T(8,128)(2,1)} %weight_ref.3, bf16[4,192,128]{2,1,0:T(8,128)(2,1)} %get-tuple-element.78.give_ref), custom_call_target="tpu_custom_call" | custom-call | tf_op jit(solution)/shard_map/tiles_grad/pallas_call | solution.py:40
  127.2 1.5 back.2
  128.7 1.6 collective-permute-done.given_ref
  130.2 2.3 %tiles_grad.3 = (f32[192,768]{1,0:T(8,128)}, bf16[192,768]{1,0:T(8,128)(2,1)}, bf16[192,768]{1,0:T(8,128)(2,1)}, bf16[192,768]{1,0:T(8,128)(2,1)}) custom-call(s32[1]{0:T(128)} %bitcast.12.chip_ref, bf16[768,128]{1,0:T(8,128)(2,1)S(1)} %get-tuple-element.54.grad_ref, bf16[4,192,128]{2,1,0:T(8,128)(2,1)} %get-tuple-element.77.keep_ref, ...), custom_call_target="tpu_custom_call" | custom-call | tf_op jit(solution)/shard_map/tiles_grad/pallas_call | solution.py:40
  132.6 4.8 %all-to-all-start.5 = ((bf16[128,8,384]{2,1,0:T(8,128)(2,1)}), bf16[128,8,384]{2,1,0:T(8,128)(2,1)S(1)}, u32[]{:S(2)}, u32[]{:S(2)}) async-start(bf16[128,8,384]{2,1,0:T(8,128)(2,1)} %bitcast.15), calls=%async_computation.5 | async-start | bytes 1572864 | tf_op jit(solution)/shard_map/back/all_to_all | solution.py:499
  137.4 2.9 %collective-permute-start.3 = (bf16[192,768]{1,0:T(8,128)(2,1)S(1)}, bf16[192,768]{1,0:T(8,128)(2,1)S(1)}, u32[]{:S(2)}, u32[]{:S(2)}) collective-permute-start(bf16[192,768]{1,0:T(8,128)(2,1)S(1)} %copy-done.10), channel_id=1, source_target_pairs={{0,96},{16,112},{32,0},{48,16},{64,32},{80,48},{96,64},{112,80},{1... | collective-permute-start | bytes 884744 | tf_op jit(solution)/shard_map/back/ppermute | solution.py:494
  142.8 12.6 %collective-permute-done.3 = bf16[192,768]{1,0:T(8,128)(2,1)S(1)} collective-permute-done((bf16[192,768]{1,0:T(8,128)(2,1)S(1)}, bf16[192,768]{1,0:T(8,128)(2,1)S(1)}, u32[]{:S(2)}, u32[]{:S(2)}) %collective-permute-start.3) | collective-permute-done | bytes 294944 | tf_op jit(solution)/shard_map/back/ppermute | solution.py:494
  155.4 2.0 %collective-permute-done.2 = bf16[192,768]{1,0:T(8,128)(2,1)S(1)} collective-permute-done((bf16[192,768]{1,0:T(8,128)(2,1)S(1)}, bf16[192,768]{1,0:T(8,128)(2,1)S(1)}, u32[]{:S(2)}, u32[]{:S(2)}) %collective-permute-start.2) | collective-permute-done | bytes 294944 | tf_op jit(solution)/shard_map/back/ppermute | solution.py:494
  157.5 7.0 %collective-permute-done.1 = bf16[192,768]{1,0:T(8,128)(2,1)S(1)} collective-permute-done((bf16[192,768]{1,0:T(8,128)(2,1)S(1)}, bf16[192,768]{1,0:T(8,128)(2,1)S(1)}, u32[]{:S(2)}, u32[]{:S(2)}) %collective-permute-start.1) | collective-permute-done | bytes 294944 | tf_op jit(solution)/shard_map/back/ppermute | solution.py:494
  165.3 2.0 %copy.12 = bf16[768,192]{1,0:T(8,128)(2,1)} copy(bf16[768,192]{0,1:T(8,128)(2,1)} %fusion) | data formatting | bytes 589824 | tf_op jit(solution)/shard_map/back/optimization_barrier | solution.py:502
  167.4 5.2 %all-to-all-start.6 = ((bf16[16,48,192]{2,1,0:T(8,128)(2,1)}), bf16[16,48,192]{2,1,0:T(8,128)(2,1)}, u32[]{:S(2)}, u32[]{:S(2)}) async-start(bf16[16,48,192]{2,1,0:T(8,128)(2,1)} %bitcast.33), calls=%async_computation.6 | async-start | bytes 786432 | tf_op jit(solution)/shard_map/embed_grad/all_to_all | solution.py:505
  172.5 2.0 %back.3 = bf16[384,768]{1,0:T(8,128)(2,1)} custom-call(bf16[1024,384]{1,0:T(8,128)(2,1)S(1)} %bitcast.28, s32[384,128]{1,0:T(8,128)S(1)} %dispatch.3.base_ref), custom_call_target="tpu_custom_call" | custom-call | tf_op jit(solution)/shard_map/back/pallas_call | solution.py:40
  174.6 3.2 %convolution_convert_fusion = bf16[384,1536]{1,0:T(8,128)(2,1)} fusion(bf16[384,768]{1,0:T(8,128)(2,1)} %back.3, bf16[1536,768]{1,0:T(8,128)(2,1)S(1)} %copy-done.6), kind=kOutput, calls=%fused_computation | convolution fusion | flops 906559488 | bytes 4128768 | tf_op jit(solution)/shard_map/feature_grad/dot_general | solution.py:511
  178.5 4.5 %all-to-all-done.6 = bf16[16,48,192]{2,1,0:T(8,128)(2,1)} async-done(((bf16[16,48,192]{2,1,0:T(8,128)(2,1)}), bf16[16,48,192]{2,1,0:T(8,128)(2,1)}, u32[]{:S(2)}, u32[]{:S(2)}) %all-to-all-start.6) | async-done | bytes 294944 | tf_op jit(solution)/shard_map/embed_grad/all_to_all | solution.py:505
  182.9 1.7 convert_reduce_fusion
  184.6 1.6 copy.13
  (40 shorter events, 12.5 us)
Async XLA Ops:
  11.8 35.6 %all-to-all-start = ((bf16[128,8,768]{2,1,0:T(8,128)(2,1)}), bf16[128,8,768]{2,1,0:T(8,128)(2,1)S(1)}, u32[]{:S(2)}, u32[]{:S(2)}) async-start(bf16[128,8,768]{2,1,0:T(8,128)(2,1)} %bitcast.31), calls=%async_computation | async-start | bytes 3145728 | tf_op jit(solution)/shard_map/dispatch/all_to_all | solution.py:385
  23.0 89.2 %all-gather.2.cloned.1.call-start = ((), (), s32[]{:S(2)}) async-start(), calls=%async_computation.8 | async-start | bytes 3342336 | tf_op jit(solution)/shard_map/qkv_grad/all_gather | solution.py:465
  53.8 19.6 %copy-start.2 = (bf16[1024,128]{1,0:T(8,128)(2,1)}, bf16[1024,128]{1,0:T(8,128)(2,1)S(1)}, u32[]{:S(2)}) copy-start(bf16[1024,128]{1,0:T(8,128)(2,1)S(1)} %get-tuple-element.56.pick1_ref) | copy-start | bytes 786436
  53.8 18.3 %all-to-all-start.1 = ((bf16[16,160,128]{2,1,0:T(8,128)(2,1)}), bf16[16,160,128]{2,1,0:T(8,128)(2,1)S(1)}, u32[]{:S(2)}, u32[]{:S(2)}) async-start(bf16[16,160,128]{2,1,0:T(8,128)(2,1)} %bitcast.34), calls=%async_computation.1 | async-start | bytes 1310720 | tf_op jit(solution)/shard_map/project/all_to_all | solution.py:401
  73.4 3.6 %copy-start.4 = (bf16[144,2048]{1,0:T(8,128)(2,1)}, bf16[144,2048]{1,0:T(8,128)(2,1)S(1)}, u32[]{:S(2)}) copy-start(bf16[144,2048]{1,0:T(8,128)(2,1)S(1)} %get-tuple-element.40.rows_ref) | copy-start | bytes 1769476
  73.4 13.4 %all-to-all-start.2 = ((bf16[8,96,256]{2,1,0:T(8,128)(2,1)}), bf16[8,96,256]{2,1,0:T(8,128)(2,1)S(1)}, u32[]{:S(2)}, u32[]{:S(2)}) async-start(bf16[8,96,256]{2,1,0:T(8,128)(2,1)} %get-tuple-element.42), calls=%async_computation.2 | async-start | bytes 786432 | tf_op jit(solution)/shard_map/dilated/all_to_all | solution.py:417
  77.1 1.1 copy-start.5
  90.6 1.0 copy-start
  91.6 13.5 %all-to-all-start.3 = ((bf16[8,96,256]{2,1,0:T(8,128)(2,1)}), bf16[8,96,256]{2,1,0:T(8,128)(2,1)S(1)}, u32[]{:S(2)}, u32[]{:S(2)}) async-start(bf16[8,96,256]{2,1,0:T(8,128)(2,1)} %get-tuple-element.48), calls=%async_computation.3 | async-start | bytes 786432 | tf_op jit(solution)/shard_map/far/all_to_all | solution.py:440
  96.1 1.2 copy-start.1
  106.2 15.9 %all-to-all-start.4 = ((bf16[16,144,128]{2,1,0:T(8,128)(2,1)}), bf16[16,144,128]{2,1,0:T(8,128)(2,1)S(1)}, u32[]{:S(2)}, u32[]{:S(2)}) async-start(bf16[16,144,128]{2,1,0:T(8,128)(2,1)} %bitcast.35), calls=%async_computation.4 | async-start | bytes 1179648 | tf_op jit(solution)/shard_map/unplace/all_to_all | solution.py:461
  122.1 5.1 %copy-start.3 = (bf16[1024,128]{1,0:T(8,128)(2,1)S(1)}, bf16[1024,128]{1,0:T(8,128)(2,1)}, u32[]{:S(2)}) copy-start(bf16[1024,128]{1,0:T(8,128)(2,1)} %copy-done.2) | copy-start | bytes 786436
  127.2 3.1 %collective-permute-start = (bf16[4,192,768]{2,1,0:T(8,128)(2,1)}, bf16[4,192,768]{2,1,0:T(8,128)(2,1)S(1)}, u32[]{:S(2)}, u32[]{:S(2)}) collective-permute-start(bf16[4,192,768]{2,1,0:T(8,128)(2,1)} %get-tuple-element.57), channel_id=1, source_target_pairs={{0,16},{16,0},{32,48},{48,32},{64,80},{80,64},{96,112},{112,96},{1... | collective-permute-start | bytes 3538952 | tf_op jit(solution)/shard_map/tiles_grad/ppermute | solution.py:482
  132.5 4.8 %copy-start.10 = (bf16[192,768]{1,0:T(8,128)(2,1)S(1)}, bf16[192,768]{1,0:T(8,128)(2,1)}, u32[]{:S(2)}) copy-start(bf16[192,768]{1,0:T(8,128)(2,1)} %get-tuple-element.65) | copy-start | bytes 884740
  132.6 7.8 %copy-start.9 = (bf16[192,768]{1,0:T(8,128)(2,1)S(1)}, bf16[192,768]{1,0:T(8,128)(2,1)}, u32[]{:S(2)}) copy-start(bf16[192,768]{1,0:T(8,128)(2,1)} %get-tuple-element.64) | copy-start | bytes 884740
  132.6 8.1 %copy-start.8 = (bf16[192,768]{1,0:T(8,128)(2,1)S(1)}, bf16[192,768]{1,0:T(8,128)(2,1)}, u32[]{:S(2)}) copy-start(bf16[192,768]{1,0:T(8,128)(2,1)} %get-tuple-element.63) | copy-start | bytes 884740
  132.6 31.9 %copy-start.7 = (f32[192,768]{1,0:T(8,128)S(1)}, f32[192,768]{1,0:T(8,128)}, u32[]{:S(2)}) copy-start(f32[192,768]{1,0:T(8,128)} %get-tuple-element.62) | copy-start | bytes 1769476
  132.6 32.8 %all-to-all-start.5 = ((bf16[128,8,384]{2,1,0:T(8,128)(2,1)}), bf16[128,8,384]{2,1,0:T(8,128)(2,1)S(1)}, u32[]{:S(2)}, u32[]{:S(2)}) async-start(bf16[128,8,384]{2,1,0:T(8,128)(2,1)} %bitcast.15), calls=%async_computation.5 | async-start | bytes 1572864 | tf_op jit(solution)/shard_map/back/all_to_all | solution.py:499
  137.3 41.1 %reduce-scatter.2.cloned.1.call-start = ((), (), s32[]{:S(2)}) async-start(), calls=%async_computation.9 | async-start | bytes 884736 | tf_op jit(solution)/shard_map/qkv_grad/reduce_scatter | solution.py:470
  137.4 18.0 %collective-permute-start.3 = (bf16[192,768]{1,0:T(8,128)(2,1)S(1)}, bf16[192,768]{1,0:T(8,128)(2,1)S(1)}, u32[]{:S(2)}, u32[]{:S(2)}) collective-permute-start(bf16[192,768]{1,0:T(8,128)(2,1)S(1)} %copy-done.10), channel_id=1, source_target_pairs={{0,96},{16,112},{32,0},{48,16},{64,32},{80,48},{96,64},{112,80},{1... | collective-permute-start | bytes 884744 | tf_op jit(solution)/shard_map/back/ppermute | solution.py:494
  140.3 17.2 %collective-permute-start.2 = (bf16[192,768]{1,0:T(8,128)(2,1)S(1)}, bf16[192,768]{1,0:T(8,128)(2,1)S(1)}, u32[]{:S(2)}, u32[]{:S(2)}) collective-permute-start(bf16[192,768]{1,0:T(8,128)(2,1)S(1)} %copy-done.9), channel_id=1, source_target_pairs={{0,64},{16,80},{32,96},{48,112},{64,0},{80,16},{96,32},{112,48},{1... | collective-permute-start | bytes 884744 | tf_op jit(solution)/shard_map/back/ppermute | solution.py:494
  140.6 23.9 %collective-permute-start.1 = (bf16[192,768]{1,0:T(8,128)(2,1)S(1)}, bf16[192,768]{1,0:T(8,128)(2,1)S(1)}, u32[]{:S(2)}, u32[]{:S(2)}) collective-permute-start(bf16[192,768]{1,0:T(8,128)(2,1)S(1)} %copy-done.8), channel_id=1, source_target_pairs={{0,32},{16,48},{32,64},{48,80},{64,96},{80,112},{96,0},{112,16},{1... | collective-permute-start | bytes 884744 | tf_op jit(solution)/shard_map/back/ppermute | solution.py:494
  165.3 9.2 %copy-start.6 = (bf16[1536,768]{1,0:T(8,128)(2,1)S(1)}, bf16[1536,768]{1,0:T(8,128)(2,1)}, u32[]{:S(2)}) copy-start(bf16[1536,768]{1,0:T(8,128)(2,1)} %embed_ref.1) | copy-start | bytes 7077892
  167.4 15.6 %all-to-all-start.6 = ((bf16[16,48,192]{2,1,0:T(8,128)(2,1)}), bf16[16,48,192]{2,1,0:T(8,128)(2,1)}, u32[]{:S(2)}, u32[]{:S(2)}) async-start(bf16[16,48,192]{2,1,0:T(8,128)(2,1)} %bitcast.33), calls=%async_computation.6 | async-start | bytes 786432 | tf_op jit(solution)/shard_map/embed_grad/all_to_all | solution.py:505
Sparse Core Ops, SparseCore 0:
  53.9 45.4 all-gather.1
  141.9 36.5 reduce-scatter.1

commit v4 on v3

--- a/solution.py
+++ b/solution.py
@@ -35,13 +35,16 @@
     return pl.BlockSpec(memory_space=memory)
 
 
-def call(body, outs, args, smem=(), **kw):
+def call(body, outs, args, smem=(), anywhere=(), **kw):
     specs = [whole(pltpu.SMEM if i in smem else pltpu.VMEM) for i in range(len(args))]
+    for i in anywhere:
+        specs[i] = whole(pl.ANY)
+    out_specs = jax.tree.map(lambda _: whole(), outs)
     return pl.pallas_call(
         body,
         out_shape=outs,
         in_specs=specs,
-        out_specs=jax.tree.map(lambda _: whole(), outs),
+        out_specs=out_specs,
         compiler_params=VMEM,
         **kw,
     )(*args)
@@ -110,14 +113,22 @@
 def project_body(
     odd_ref,
     recv_ref,
-    embed_ref,
-    weight_ref,
+    embed_hbm_ref,
+    weight_hbm_ref,
     emb_ref,
     tiles_ref,
     chunk_ref,
     pick0_ref,
     pick1_ref,
+    embed_ref,
+    weight_ref,
+    embed_sem,
+    weight_sem,
 ):
+    embed_load = pltpu.make_async_copy(embed_hbm_ref, embed_ref, embed_sem)
+    embed_load.start()
+    weight_load = pltpu.make_async_copy(weight_hbm_ref, weight_ref, weight_sem)
+    weight_load.start()
     total = recv_ref.shape[0]
     senders = total // 8
     sel = hot(iota((senders, total), 1) == 8 * iota((senders, total), 0) + 6)
@@ -156,9 +167,11 @@
     half = recv_ref.shape[1]
     tiles_ref[:, :half] = dot(pick0, recv_ref[...], "tn").astype(HALFS)
     tiles_ref[:, half:] = dot(pick1, recv_ref[...], "tn").astype(HALFS)
+    embed_load.wait()
     emb_ref[...] = dot(tiles_ref[...], embed_ref[...]).astype(HALFS)
     info = jnp.where(lanes == 0, high, jnp.where(lanes == 1, low, 0.0)).astype(HALFS)
     info = dot(info, pick0, "tn")[:16].astype(HALFS)
+    weight_load.wait()
     heads = chunk_ref.shape[0] // CHUNK_ROWS
     for head in range(heads):
         top = head * CHUNK_ROWS
@@ -322,32 +335,71 @@
         ]
 
 
-def qkv_grad_body(grad_ref, rows_ref, out_ref):
-    out_ref[...] = dot(grad_ref[...], rows_ref[...]).T
-
-
-def tiles_grad_body(rows_ref, weight_ref, give_ref, grad_ref, given_ref):
-    grad = dot(weight_ref[...], rows_ref[...]).astype(HALFS)
-    grad_ref[...] = grad
-    for block in range(give_ref.shape[0]):
-        given_ref[block] = dot(give_ref[block], grad, "nt").astype(HALFS)
-
-
-def merge_body(chip_ref, grad_ref, keep_ref, given_ref, own_ref, *piece_refs):
+def qkv_grad_body(core_ref, grad_ref, rows_ref, keep_ref, give_ref, all_ref):
+    block = keep_ref.shape[1]
+    part = dot(grad_ref[...], rows_ref[...]).T
+    all_ref[...] = jnp.concatenate([part, jnp.zeros_like(part[:, : 256 - WIDTH])], axis=1)
+    for chip in range(keep_ref.shape[0]):
+        mine = pl.multiple_of((2 * chip + core_ref[0]) * block, block)
+        other = pl.multiple_of((2 * chip + 1 - core_ref[0]) * block, block)
+        keep_ref[chip] = all_ref[pl.ds(mine, block), :]
+        give_ref[chip] = all_ref[pl.ds(other, block), :].astype(HALFS)
+
+
+def give_body(grad_ref, give_ref, given_ref):
+    given_ref[...] = dot(grad_ref[...], give_ref[...]).astype(HALFS)
+
+
+def merge_body(grad_ref, keep_ref, given_ref, out_ref):
+    rows, size = out_ref.shape[1] * 2 // 3, 128
+    part = dot(grad_ref[...], keep_ref[...]) + given_ref[...].astype(FLOATS)
+    part = part.astype(HALFS)
+    columns = part.shape[0] // rows
+    for block in range(out_ref.shape[0] // columns):
+        left = block // 2 * 3 * size
+        first = left if block % 2 == 0 else left + 2 * size
+        other = left + size if block % 2 == 0 else left + size + 64
+        for column in range(columns):
+            here = part[column * rows : (column + 1) * rows]
+            spot = block * columns + column
+            out_ref[spot, :rows, :] = here[:, first : first + size]
+            rest = here[:, other : other + 64]
+            out_ref[spot, rows:, :] = jnp.concatenate(
+                [rest[: rows // 2], rest[rows // 2 :]], axis=1
+            )
+
+
+def merge_qkv_body(chip_ref, keep_ref, given_ref, own_ref, *piece_refs):
     chips = keep_ref.shape[0]
     for k in range(chips):
         block = (chip_ref[0] + k) & (chips - 1)
-        part = dot(keep_ref[block], grad_ref[...], "nt") + given_ref[block].astype(FLOATS)
+        part = keep_ref[block] + given_ref[block].astype(FLOATS)
         if k == 0:
             own_ref[...] = part
         else:
             piece_refs[k - 1][...] = part.astype(HALFS)
 
 
-def back_body(grad_ref, pick0_ref, pick1_ref, back_ref):
+def last_body(chip_ref, parts_ref, own_ref, *refs):
+    piece_refs, embed_ref, qkv_ref = refs[:-2], refs[-2], refs[-1]
+    total = parts_ref[0].astype(FLOATS)
+    for k in range(1, parts_ref.shape[0]):
+        total = total + parts_ref[k].astype(FLOATS)
+    rest = jnp.concatenate([total[48:, :64], total[48:, 64:]], axis=0)
+    even = jnp.concatenate([total[:48], rest], axis=1)
+    odd = jnp.concatenate([rest, total[:48]], axis=1)
+    embed_ref[...] = jnp.where((chip_ref[0] & 1) == 0, even, odd)
+    qkv = own_ref[...]
+    for ref in piece_refs:
+        qkv = qkv + ref[...].astype(FLOATS)
+    qkv_ref[...] = qkv.T[:WIDTH]
+
+
+def back_body(rows_ref, weight_ref, pick0_ref, pick1_ref, grad_ref, back_ref):
     half = back_ref.shape[1]
-    back = dot(pick0_ref[...], grad_ref[:half], "nt")
-    back = back + dot(pick1_ref[...], grad_ref[half:], "nt")
+    grad = dot(weight_ref[...], rows_ref[...]).astype(HALFS)
+    grad_ref[...] = grad
+    back = dot(pick0_ref[...], grad[:half], "nt") + dot(pick1_ref[...], grad[half:], "nt")
     back_ref[...] = back.astype(HALFS)
 
 
@@ -379,7 +431,7 @@
 
     with jax.named_scope("dispatch"):
         sent = call(
-            dispatch_body, shaped((devices * 8, tiles // 2)), [positions, tile_features]
+            dispatch_body, resident((devices * 8, tiles // 2)), [positions, tile_features]
         )
         base = call(slots_body, resident((slots, 128), jnp.int32), [positions])
         arrived = lax.all_to_all(
@@ -391,12 +443,19 @@
             [
                 shaped((share, wide)),
                 shaped((share, tiles)),
-                shaped((n_tile * CHUNK_ROWS, 128)),
-                resident((devices * 8, 128)),
-                resident((devices * 8, 128)),
+                resident((n_tile * CHUNK_ROWS, 128)),
+                shaped((devices * 8, 128)),
+                shaped((devices * 8, 128)),
             ],
             [odd, *stay(arrived), embed_weight, qkv_weight],
             smem=(0,),
+            anywhere=(2, 3),
+            scratch_shapes=[
+                pltpu.VMEM(embed_weight.shape, HALFS),
+                pltpu.VMEM(qkv_weight.shape, HALFS),
+                pltpu.SemaphoreType.DMA,
+                pltpu.SemaphoreType.DMA,
+            ],
         )
         chunks = lax.all_to_all(
             chunks.reshape(n_tile, CHUNK_ROWS, 128), "tile", 0, 0, tiled=True
@@ -407,8 +466,8 @@
             dilated_body,
             [
                 resident((HEAD_SIZE, few)),
-                shaped((n_slide, 2 * HEAD_SIZE, few)),
-                resident((WIDTH, rows)),
+                resident((n_slide, 2 * HEAD_SIZE, few)),
+                shaped((WIDTH, rows)),
                 resident((8, rows), jnp.int32),
             ],
             [phase, *stay(chunks)],
@@ -421,7 +480,7 @@
         placed, near = call(
             near_body,
             [resident((WIDTH, rows)), resident((WIDTH, rows), FLOATS)],
-            [phase, *stay(head_rows, local), grads],
+            [phase, head_rows, *stay(local), grads],
             smem=(0,),
             cost_estimate=pl.CostEstimate(
                 flops=8_000_000_000, bytes_accessed=8_000_000, transcendentals=1 << 20
@@ -431,9 +490,9 @@
         far_grads, dscores, probs = call(
             far_body,
             [
-                shaped((n_slide, 2 * HEAD_SIZE, few)),
-                resident((2, rows, 128)),
-                resident((2, rows // 2, 128)),
+                resident((n_slide, 2 * HEAD_SIZE, few)),
+                shaped((2, rows, 128)),
+                shaped((2, rows // 2, 128)),
             ],
             stay(query, dilated_grads, placed, far),
         )
@@ -442,7 +501,7 @@
         dquery, summed = call(
             sum_body,
             [resident((HEAD_SIZE, few)), resident((WIDTH, rows))],
-            stay(query, dilated_grads, placed, far, dscores, probs, near),
+            [*stay(query, dilated_grads, placed, far), dscores, probs, *stay(near)],
         )
         main = call(
             unplace_body,
@@ -454,7 +513,7 @@
         )
         back_chunks, d_rows = call(
             finish_body,
-            [shaped((n_tile * WIDTH, 128)), resident((WIDTH, rows))],
+            [resident((n_tile * WIDTH, 128)), shaped((WIDTH, rows))],
             [phase, *stay(local, main, dquery, far_grads)],
             smem=(0,),
         )
@@ -463,50 +522,66 @@
         ).reshape(n_tile * WIDTH, 128)
     with jax.named_scope("qkv_grad"):
         all_rows = lax.all_gather(emb_rows, "tile", axis=0, tiled=True)
-        qkv_part = call(
-            qkv_grad_body, shaped((wide, WIDTH), FLOATS), [*stay(d_rows), all_rows]
-        )
-        back_rows, qkv_part = lax.optimization_barrier((back_rows, qkv_part))
-        qkv_grad = lax.psum_scatter(qkv_part, "slide", scatter_dimension=0, tiled=True)
+        chips = n_slide // 2
+        block = wide // n_slide
+        keep_qkv, give_qkv = call(
+            qkv_grad_body,
+            [shaped((chips, block, 256), FLOATS), shaped((chips, block, 256))],
+            [core.astype(jnp.int32).reshape(1), d_rows, all_rows],
+            smem=(0,),
+            scratch_shapes=[pltpu.VMEM((wide, 256), FLOATS)],
+        )
+        chip = (row_here // 2).astype(jnp.int32).reshape(1)
+        swap = [(i, i ^ 1) for i in range(n_slide)]
+        given_qkv = lax.ppermute(give_qkv, "slide", swap)
+        own_qkv, *pieces = call(
+            merge_qkv_body,
+            [shaped((block, 256), FLOATS)] + [shaped((block, 256))] * (chips - 1),
+            [chip, keep_qkv, given_qkv],
+            smem=(0,),
+        )
+        pieces = [
+            lax.ppermute(
+                pieces[k - 1], "slide", [(i, (i + 2 * k) % n_slide) for i in range(n_slide)]
+            )
+            for k in range(1, chips)
+        ]
     with jax.named_scope("tiles_grad"):
         narrow = tiles // n_slide
-        chips = n_slide // 2
         split = tile_rows.reshape(share, chips, 2, narrow)
-        keep_cols = lax.dynamic_index_in_dim(split, core, 2, False).transpose(1, 2, 0)
-        give_cols = lax.dynamic_index_in_dim(split, 1 - core, 2, False).transpose(1, 2, 0)
-        grad_rows, given = call(
-            tiles_grad_body,
-            [resident((wide, share)), shaped((chips, narrow, wide))],
-            [*stay(back_rows), qkv_weight, give_cols],
-        )
-        given = lax.ppermute(given, "slide", [(i, i ^ 1) for i in range(n_slide)])
-        own, *pieces = call(
-            merge_body,
-            [shaped((narrow, wide), FLOATS)] + [shaped((narrow, wide))] * (chips - 1),
-            [(row_here // 2).astype(jnp.int32).reshape(1), *stay(grad_rows), keep_cols, *stay(given)],
-            smem=(0,),
-        )
-    with jax.named_scope("back"):
-        back = call(back_body, shaped((devices * 8, half)), stay(grad_rows, pick0, pick1))
-        back, pieces = lax.optimization_barrier((back, pieces))
-        part = own
-        for k in range(1, chips):
-            piece = lax.ppermute(
-                pieces[k - 1], "slide", [(i, (i + 2 * k) % n_slide) for i in range(n_slide)]
-            )
-            part = part + piece.astype(FLOATS)
-        part = part.astype(HALFS).T
+        keep_cols = lax.dynamic_index_in_dim(split, core, 2, False).reshape(share, tiles // 2)
+        give_cols = lax.dynamic_index_in_dim(split, 1 - core, 2, False).reshape(share, tiles // 2)
+        grad_rows, back = call(
+            back_body,
+            [shaped((wide, share)), shaped((devices * 8, half))],
+            [*stay(back_rows), qkv_weight, pick0, pick1],
+        )
         back = lax.all_to_all(
             back.reshape(devices, 8, half), every, 0, 0, tiled=True
         ).reshape(devices * 8, half)
-        back, part = lax.optimization_barrier((back, part))
+        given = call(give_body, shaped((wide, tiles // 2)), [grad_rows, give_cols])
+        given = lax.ppermute(given, "slide", swap)
+        merged = call(
+            merge_body, shaped((chips * n_tile, 72, 128)), [grad_rows, keep_cols, given]
+        )
+        merged, back = lax.optimization_barrier((merged, back))
+    with jax.named_scope("collect"):
         d_embedded = call(collect_body, shaped((slots, wide)), stay(back, base))
     with jax.named_scope("embed_grad"):
+        same_core = [
+            [(2 * z + c) * n_tile + t for z in range(chips) for t in range(n_tile)]
+            for c in range(2)
+        ]
         parts = lax.all_to_all(
-            part.reshape(n_tile, wide // n_tile, narrow), "tile", 0, 0, tiled=True
-        )
-        parts, qkv_grad = lax.optimization_barrier((parts, qkv_grad))
-        embed_grad = jnp.sum(parts.astype(FLOATS), axis=0).T
+            merged, every, 0, 0, axis_index_groups=same_core, tiled=True
+        )
+        embed_grad, qkv_grad = call(
+            last_body,
+            [shaped((wide // n_tile, narrow), FLOATS), shaped((WIDTH, wide // n_slide), FLOATS)],
+            [chip, *stay(parts), own_qkv, *pieces],
+            smem=(0,),
+        )
+        embed_grad, qkv_grad = embed_grad.T, qkv_grad.T
     with jax.named_scope("feature_grad"):
         feature_grad = lax.dot_general(
             d_embedded, embed_weight, (((1,), (1,)), ((), ())), preferred_element_type=FLOATS

time: 194 us -> 186 us (0.959)
  waiting for transfers between devices: 78.3 us -> 67.3 us
  Pallas kernels: 44.7 us -> 51.9 us
  local copies, waits for them, and re-layouts: 8.98 us -> 4.28 us
  other arithmetic: 2.53 us -> 0 us
    ppermute x3, waiting for transfers between devices: 21.7 us -> 0.16 us  [per_device(): lax.ppermute(pieces[k - 1], 'slide', [(i, (i + 2 * k) % n_slide) for i in...]
    all_to_all x1, waiting for transfers between devices: 0.01 us -> 11.4 us  [per_device(): lax.all_to_all(back.reshape(devices, 8, half), every, 0, 0, tiled=True)]
    pallas_call x15 -> x17, Pallas kernels: 44.7 us -> 51.9 us  [call(): pl.pallas_call(body, out_shape=outs, in_specs=specs, out_specs=out_specs,...]
    all_to_all x1, waiting for transfers between devices: 6.42 us -> 10.9 us  [per_device(): lax.all_to_all(back_chunks.reshape(n_tile, WIDTH, 128), 'tile', 0, 0, til...]
    all_to_all x1, waiting for transfers between devices: 4.45 us -> 1.51 us  [per_device(): lax.all_to_all(merged, every, 0, 0, axis_index_groups=same_core, tiled=True)]
    unnamed x23 -> x12, local copies, waits for them, and re-layouts: 4.91 us -> 2.35 us
    optimization_barrier x1 -> x0, local copies, waits for them, and re-layouts: 2.03 us -> none  [per_device(): back, part = lax.optimization_barrier((back, part))]
  transfers between devices with their start and end apart: 13 -> 13, of which waited for: 10 -> 7; matrix products, arithmetic and copies ran while one was open for 4% -> 3% of each run, Pallas kernels for 14% -> 22%
where the time goes in v4:
time: 186 us; the launch traced here: 184 us
  waiting for transfers between devices  67.3 us (36%)
  Pallas kernels  51.9 us (28%)
  starting transfers between devices  42 us (23%)
  between operations  14.2 us (8%)
  local copies, waits for them, and re-layouts  4.28 us (2%)
  matrix products  3.98 us (2%)
    pallas_call x17, Pallas kernels, call(): pl.pallas_call(body, out_shape=outs, in_specs=specs, out_specs=out_specs,...  51.9 us
    all_to_all x1, waiting for transfers between devices, per_device(): lax.all_to_all(sent.reshape(devices, 8, tiles // 2), every, 0, 0, tiled=T...  24.4 us
    all_to_all x1, waiting for transfers between devices, per_device(): lax.all_to_all(chunks.reshape(n_tile, CHUNK_ROWS, 128), 'tile', 0, 0, til...  13.5 us
    all_to_all x1, waiting for transfers between devices, per_device(): lax.all_to_all(back.reshape(devices, 8, half), every, 0, 0, tiled=True)  11.4 us
    all_to_all x1, starting transfers between devices, per_device(): lax.all_to_all(sent.reshape(devices, 8, tiles // 2), every, 0, 0, tiled=T...  11.1 us
    all_to_all x1, waiting for transfers between devices, per_device(): lax.all_to_all(back_chunks.reshape(n_tile, WIDTH, 128), 'tile', 0, 0, til...  10.9 us
    ppermute x3, starting transfers between devices, per_device(): lax.ppermute(pieces[k - 1], 'slide', [(i, (i + 2 * k) % n_slide) for i in...  5.81 us
    all_to_all x1, waiting for transfers between devices, per_device(): far_grads = lax.all_to_all(far_grads, 'slide', 0, 0, tiled=True)  5.34 us
  transfers between devices with their start and end apart: 13, of which 7 were waited for; matrix products, arithmetic and copies ran while one was open for 3% of the time, Pallas kernels for 22%

profile of v4, /device:TPU:0, one launch (start us, length us, event | category | flops | bytes accessed | tf_op | source)
XLA Modules:
  0.0 183.7 jit_solution(13325133636408319258)
XLA Ops:
  7.2 4.7 %dispatch.2 = bf16[1024,768]{1,0:T(8,128)(2,1)} custom-call(s32[384]{0:T(512)} %pos_ref.3, bf16[384,1536]{1,0:T(8,128)(2,1)} %tiles_ref.1), custom_call_target="tpu_custom_call" | custom-call | tf_op jit(solution)/shard_map/dispatch/pallas_call | solution.py:43
  11.8 11.1 %all-to-all-start = ((bf16[128,8,768]{2,1,0:T(8,128)(2,1)}), bf16[128,8,768]{2,1,0:T(8,128)(2,1)S(1)}, u32[]{:S(2)}, u32[]{:S(2)}) async-start(bf16[128,8,768]{2,1,0:T(8,128)(2,1)} %bitcast.2), calls=%async_computation | async-start | bytes 3145728 | tf_op jit(solution)/shard_map/dispatch/all_to_all | solution.py:437
  23.0 24.4 %all-to-all-done = bf16[128,8,768]{2,1,0:T(8,128)(2,1)S(1)} async-done(((bf16[128,8,768]{2,1,0:T(8,128)(2,1)}), bf16[128,8,768]{2,1,0:T(8,128)(2,1)S(1)}, u32[]{:S(2)}, u32[]{:S(2)}) %all-to-all-start) | async-done | bytes 1572896 | tf_op jit(solution)/shard_map/dispatch/all_to_all | solution.py:437
  47.4 5.7 %project.1 = (bf16[128,768]{1,0:T(8,128)(2,1)}, bf16[128,1536]{1,0:T(8,128)(2,1)}, bf16[2560,128]{1,0:T(8,128)(2,1)}, bf16[1024,128]{1,0:T(8,128)(2,1)}, bf16[1024,128]{1,0:T(8,128)(2,1)}) custom-call(s32[1]{0:T(128)} %bitcast.1.odd_ref, bf16[1024,768]{1,0:T(8,128)(2,1)S(1)} %bitcast.20, bf16[1536,768]{1,0:T(8,128)(2,1)} %embed_hbm_ref.1, ...), custom_call_target="tpu_custom_call" | custom-call | tf_op jit(solution)/shard_map/project/pallas_call | solution.py:43
  53.1 3.7 %all-to-all-start.1 = ((bf16[16,160,128]{2,1,0:T(8,128)(2,1)}), bf16[16,160,128]{2,1,0:T(8,128)(2,1)S(1)}, u32[]{:S(2)}, u32[]{:S(2)}) async-start(bf16[16,160,128]{2,1,0:T(8,128)(2,1)} %bitcast.4), calls=%async_computation.1 | async-start | bytes 1310720 | tf_op jit(solution)/shard_map/project/all_to_all | solution.py:460
  58.0 13.5 %all-to-all-done.1 = bf16[16,160,128]{2,1,0:T(8,128)(2,1)S(1)} async-done(((bf16[16,160,128]{2,1,0:T(8,128)(2,1)}), bf16[16,160,128]{2,1,0:T(8,128)(2,1)S(1)}, u32[]{:S(2)}, u32[]{:S(2)}) %all-to-all-start.1) | async-done | bytes 655392 | tf_op jit(solution)/shard_map/project/all_to_all | solution.py:460
  71.4 1.3 dilated.1
  72.7 3.6 %all-to-all-start.2 = ((bf16[8,96,256]{2,1,0:T(8,128)(2,1)}), bf16[8,96,256]{2,1,0:T(8,128)(2,1)S(1)}, u32[]{:S(2)}, u32[]{:S(2)}) async-start(bf16[8,96,256]{2,1,0:T(8,128)(2,1)} %get-tuple-element.38), calls=%async_computation.2 | async-start | bytes 786432 | tf_op jit(solution)/shard_map/dilated/all_to_all | solution.py:476
  76.4 8.8 %near.3 = (bf16[144,2048]{1,0:T(8,128)(2,1)S(1)}, f32[144,2048]{1,0:T(8,128)S(1)}) custom-call(s32[1]{0:T(128)} %bitcast.phase_ref, bf16[144,2048]{1,0:T(8,128)(2,1)} %get-tuple-element.36.rows_ref, s32[8,2048]{1,0:T(8,128)S(1)} %get-tuple-element.34.local_ref, bf16[4,48,512]{2,1,0:T(8,128)(2,1)} %bitcast.28), custom_call_target="tpu_custom_call" | custom-call | flops 8000000000 | bytes 8000000 | tf_op jit(solution)/shard_map/near/pallas_call | solution.py:43
  85.2 4.1 %far.1 = (bf16[8,96,256]{2,1,0:T(8,128)(2,1)}, bf16[2,2048,128]{2,1,0:T(8,128)(2,1)}, bf16[2,1024,128]{2,1,0:T(8,128)(2,1)}) custom-call(bf16[48,256]{1,0:T(8,128)(2,1)S(1)} %get-tuple-element.35.query_ref, bf16[48,256]{1,0:T(8,128)(2,1)S(1)} %near.2.grad_ref, bf16[144,2048]{1,0:T(8,128)(2,1)S(1)} %get-tuple-element.37.place_ref, ...), custom_call_target="tpu_custom_call" | custom-call | tf_op jit(solution)/shard_map/far/pallas_call | solution.py:43
  89.4 4.5 %all-to-all-start.3 = ((bf16[8,96,256]{2,1,0:T(8,128)(2,1)}), bf16[8,96,256]{2,1,0:T(8,128)(2,1)S(1)}, u32[]{:S(2)}, u32[]{:S(2)}) async-start(bf16[8,96,256]{2,1,0:T(8,128)(2,1)} %get-tuple-element.44), calls=%async_computation.3 | async-start | bytes 786432 | tf_op jit(solution)/shard_map/far/all_to_all | solution.py:499
  93.9 2.1 %unplace.3 = (bf16[48,256]{1,0:T(8,128)(2,1)S(1)}, bf16[144,2048]{1,0:T(8,128)(2,1)S(1)}) custom-call(bf16[48,256]{1,0:T(8,128)(2,1)S(1)} %get-tuple-element.35.query_ref, bf16[48,256]{1,0:T(8,128)(2,1)S(1)} %near.2.grad_ref, bf16[144,2048]{1,0:T(8,128)(2,1)S(1)} %get-tuple-element.37.place_ref, bf16[8,96,256]{2,1,0:T(8,128)(2,1)S(1)} %all-to-all-done.2.far_ref, ...), custom_call_target="tpu_custom_call" | custom-call | tf_op jit(solution)/shard_map/unplace/pallas_call | solution.py:43
  96.0 1.5 unplace.4.main_ref
  97.5 5.3 %all-to-all-done.3.far_ref = bf16[8,96,256]{2,1,0:T(8,128)(2,1)S(1)} async-done(((bf16[8,96,256]{2,1,0:T(8,128)(2,1)}), bf16[8,96,256]{2,1,0:T(8,128)(2,1)S(1)}, u32[]{:S(2)}, u32[]{:S(2)}) %all-to-all-start.3) | async-done | bytes 393248 | tf_op jit(solution)/shard_map/far/all_to_all | solution.py:499
  102.8 1.4 unplace.5
  104.2 3.8 %all-to-all-start.4 = ((bf16[16,144,128]{2,1,0:T(8,128)(2,1)}), bf16[16,144,128]{2,1,0:T(8,128)(2,1)S(1)}, u32[]{:S(2)}, u32[]{:S(2)}) async-start(bf16[16,144,128]{2,1,0:T(8,128)(2,1)} %bitcast.7), calls=%async_computation.4 | async-start | bytes 1179648 | tf_op jit(solution)/shard_map/unplace/all_to_all | solution.py:520
  109.2 10.9 %all-to-all-done.4 = bf16[16,144,128]{2,1,0:T(8,128)(2,1)S(1)} async-done(((bf16[16,144,128]{2,1,0:T(8,128)(2,1)}), bf16[16,144,128]{2,1,0:T(8,128)(2,1)S(1)}, u32[]{:S(2)}, u32[]{:S(2)}) %all-to-all-start.4) | async-done | bytes 589856 | tf_op jit(solution)/shard_map/unplace/all_to_all | solution.py:520
  120.1 5.4 %tiles_grad.3 = (bf16[768,128]{1,0:T(8,128)(2,1)}, bf16[1024,384]{1,0:T(8,128)(2,1)}) custom-call(bf16[2304,128]{1,0:T(8,128)(2,1)S(1)} %bitcast.23, bf16[768,2304]{1,0:T(8,128)(2,1)} %weight_ref.1, bf16[1024,128]{1,0:T(8,128)(2,1)} %get-tuple-element.46.pick0_ref, bf16[1024,128]{1,0:T(8,128)(2,1)} %get-tuple-element.47.pick1_ref), custom_call_target="tpu_custom_call" | custom-call | tf_op jit(solution)/shard_map/tiles_grad/pallas_call | solution.py:43
  125.5 2.5 %tiles_grad.4 = bf16[768,768]{1,0:T(8,128)(2,1)} custom-call(bf16[768,128]{1,0:T(8,128)(2,1)} %get-tuple-element.48.grad_ref, bf16[128,768]{1,0:T(8,128)(2,1)} %copy.11.give_ref), custom_call_target="tpu_custom_call" | custom-call | tf_op jit(solution)/shard_map/tiles_grad/pallas_call | solution.py:43
  128.0 4.6 %all-to-all-start.5 = ((bf16[128,8,384]{2,1,0:T(8,128)(2,1)}), bf16[128,8,384]{2,1,0:T(8,128)(2,1)S(1)}, u32[]{:S(2)}, u32[]{:S(2)}) async-start(bf16[128,8,384]{2,1,0:T(8,128)(2,1)} %bitcast.12), calls=%async_computation.5 | async-start | bytes 1572864 | tf_op jit(solution)/shard_map/tiles_grad/all_to_all | solution.py:559
  134.5 3.0 %tiles_grad.5 = bf16[64,72,128]{2,1,0:T(8,128)(2,1)} custom-call(bf16[768,128]{1,0:T(8,128)(2,1)} %get-tuple-element.48.grad_ref, bf16[128,768]{1,0:T(8,128)(2,1)} %copy.12.keep_ref, bf16[768,768]{1,0:T(8,128)(2,1)} %copy-done), custom_call_target="tpu_custom_call" | custom-call | tf_op jit(solution)/shard_map/tiles_grad/pallas_call | solution.py:43
  137.5 11.4 %all-to-all-done.5 = bf16[128,8,384]{2,1,0:T(8,128)(2,1)S(1)} async-done(((bf16[128,8,384]{2,1,0:T(8,128)(2,1)}), bf16[128,8,384]{2,1,0:T(8,128)(2,1)S(1)}, u32[]{:S(2)}, u32[]{:S(2)}) %all-to-all-start.5) | async-done | bytes 786464 | tf_op jit(solution)/shard_map/tiles_grad/all_to_all | solution.py:559
  148.9 4.7 %all-to-all-start.6 = ((bf16[64,72,128]{2,1,0:T(8,128)(2,1)}), bf16[64,72,128]{2,1,0:T(8,128)(2,1)S(1)}, u32[]{:S(2)}, u32[]{:S(2)}) async-start(bf16[64,72,128]{2,1,0:T(8,128)(2,1)} %tiles_grad.5), calls=%async_computation.6 | async-start | bytes 2359296 | tf_op jit(solution)/shard_map/embed_grad/all_to_all | solution.py:575
  153.7 3.7 %qkv_grad.2 = (f32[4,96,256]{2,1,0:T(8,128)}, bf16[4,96,256]{2,1,0:T(8,128)(2,1)}) custom-call(s32[1]{0:T(128)} %bitcast.15.core_ref, bf16[144,2048]{1,0:T(8,128)(2,1)} %get-tuple-element.53.grad_ref, bf16[2048,768]{1,0:T(8,128)(2,1)} %all-gather.2.cloned.1.call-done.rows_ref), custom_call_target="tpu_custom_call" | custom-call | tf_op jit(solution)/shard_map/qkv_grad/pallas_call | solution.py:43
  158.4 2.0 %collect.1 = bf16[384,768]{1,0:T(8,128)(2,1)} custom-call(bf16[1024,384]{1,0:T(8,128)(2,1)S(1)} %bitcast.21, s32[384,128]{1,0:T(8,128)S(1)} %dispatch.3.base_ref), custom_call_target="tpu_custom_call" | custom-call | tf_op jit(solution)/shard_map/collect/pallas_call | solution.py:43
  161.1 1.7 qkv_grad.3
  162.9 1.6 collective-permute-start.2
  164.5 2.9 %collective-permute-start.3 = (bf16[96,256]{1,0:T(8,128)(2,1)}, bf16[96,256]{1,0:T(8,128)(2,1)S(1)}, u32[]{:S(2)}, u32[]{:S(2)}) collective-permute-start(bf16[96,256]{1,0:T(8,128)(2,1)} %get-tuple-element.59), channel_id=1, source_target_pairs={{0,64},{16,80},{32,96},{48,112},{64,0},{80,16},{96,32},{112,48},{1... | collective-permute-start | bytes 147464 | tf_op jit(solution)/shard_map/qkv_grad/ppermute | solution.py:544
  167.3 1.4 collective-permute-start.4
  168.7 4.0 %convolution_convert_fusion = bf16[384,1536]{1,0:T(8,128)(2,1)} fusion(bf16[384,768]{1,0:T(8,128)(2,1)} %collect.1, bf16[1536,768]{1,0:T(8,128)(2,1)} %embed_hbm_ref.1), kind=kOutput, calls=%fused_computation | convolution fusion | flops 906559488 | bytes 4128768 | tf_op jit(solution)/shard_map/feature_grad/dot_general | solution.py:586
  172.7 1.5 all-to-all-done.6.parts_ref
  175.0 1.9 %embed_grad.1 = (f32[48,192]{1,0:T(8,128)}, f32[144,96]{1,0:T(8,128)}) custom-call(s32[1]{0:T(128)} %bitcast.14.chip_ref, bf16[64,72,128]{2,1,0:T(8,128)(2,1)S(1)} %all-to-all-done.6.parts_ref, f32[96,256]{1,0:T(8,128)} %get-tuple-element.57.own_ref, bf16[96,256]{1,0:T(8,128)(2,1)} %copy-done.3, bf16[96,256]{1,0:T(8,128)(2,1)} %copy-done.4, ...), custom_call_target="tpu_custom_call" | custom-call | tf_op jit(solution)/shard_map/embed_grad/pallas_call | solution.py:43
  (29 shorter events, 6.7 us)
Async XLA Ops:
  11.8 35.6 %all-to-all-start = ((bf16[128,8,768]{2,1,0:T(8,128)(2,1)}), bf16[128,8,768]{2,1,0:T(8,128)(2,1)S(1)}, u32[]{:S(2)}, u32[]{:S(2)}) async-start(bf16[128,8,768]{2,1,0:T(8,128)(2,1)} %bitcast.2), calls=%async_computation | async-start | bytes 3145728 | tf_op jit(solution)/shard_map/dispatch/all_to_all | solution.py:437
  23.0 130.7 %all-gather.2.cloned.1.call-start = ((), (), s32[]{:S(2)}) async-start(), calls=%async_computation.7 | async-start | bytes 3342336 | tf_op jit(solution)/shard_map/qkv_grad/all_gather | solution.py:524
  53.1 18.3 %all-to-all-start.1 = ((bf16[16,160,128]{2,1,0:T(8,128)(2,1)}), bf16[16,160,128]{2,1,0:T(8,128)(2,1)S(1)}, u32[]{:S(2)}, u32[]{:S(2)}) async-start(bf16[16,160,128]{2,1,0:T(8,128)(2,1)} %bitcast.4), calls=%async_computation.1 | async-start | bytes 1310720 | tf_op jit(solution)/shard_map/project/all_to_all | solution.py:460
  72.7 12.5 %all-to-all-start.2 = ((bf16[8,96,256]{2,1,0:T(8,128)(2,1)}), bf16[8,96,256]{2,1,0:T(8,128)(2,1)S(1)}, u32[]{:S(2)}, u32[]{:S(2)}) async-start(bf16[8,96,256]{2,1,0:T(8,128)(2,1)} %get-tuple-element.38), calls=%async_computation.2 | async-start | bytes 786432 | tf_op jit(solution)/shard_map/dilated/all_to_all | solution.py:476
  89.4 13.5 %all-to-all-start.3 = ((bf16[8,96,256]{2,1,0:T(8,128)(2,1)}), bf16[8,96,256]{2,1,0:T(8,128)(2,1)S(1)}, u32[]{:S(2)}, u32[]{:S(2)}) async-start(bf16[8,96,256]{2,1,0:T(8,128)(2,1)} %get-tuple-element.44), calls=%async_computation.3 | async-start | bytes 786432 | tf_op jit(solution)/shard_map/far/all_to_all | solution.py:499
  97.5 10.6 %copy-start.1 = (bf16[128,1536]{1,0:T(8,128)(2,1)S(1)}, bf16[128,1536]{1,0:T(8,128)(2,1)}, u32[]{:S(2)}) copy-start(bf16[128,1536]{1,0:T(8,128)(2,1)} %get-tuple-element.49) | copy-start | bytes 1179652
  104.2 15.9 %all-to-all-start.4 = ((bf16[16,144,128]{2,1,0:T(8,128)(2,1)}), bf16[16,144,128]{2,1,0:T(8,128)(2,1)S(1)}, u32[]{:S(2)}, u32[]{:S(2)}) async-start(bf16[16,144,128]{2,1,0:T(8,128)(2,1)} %bitcast.7), calls=%async_computation.4 | async-start | bytes 1179648 | tf_op jit(solution)/shard_map/unplace/all_to_all | solution.py:520
  128.0 5.5 %collective-permute-start = (bf16[768,768]{1,0:T(8,128)(2,1)}, bf16[768,768]{1,0:T(8,128)(2,1)S(1)}, u32[]{:S(2)}, u32[]{:S(2)}) collective-permute-start(bf16[768,768]{1,0:T(8,128)(2,1)} %tiles_grad.4), channel_id=1, source_target_pairs={{0,16},{16,0},{32,48},{48,32},{64,80},{80,64},{96,112},{112,96},{1... | collective-permute-start | bytes 3538952 | tf_op jit(solution)/shard_map/tiles_grad/ppermute | solution.py:563
  128.0 21.0 %all-to-all-start.5 = ((bf16[128,8,384]{2,1,0:T(8,128)(2,1)}), bf16[128,8,384]{2,1,0:T(8,128)(2,1)S(1)}, u32[]{:S(2)}, u32[]{:S(2)}) async-start(bf16[128,8,384]{2,1,0:T(8,128)(2,1)} %bitcast.12), calls=%async_computation.5 | async-start | bytes 1572864 | tf_op jit(solution)/shard_map/tiles_grad/all_to_all | solution.py:559
  133.4 1.0 copy-start
  148.9 25.3 %all-to-all-start.6 = ((bf16[64,72,128]{2,1,0:T(8,128)(2,1)}), bf16[64,72,128]{2,1,0:T(8,128)(2,1)S(1)}, u32[]{:S(2)}, u32[]{:S(2)}) async-start(bf16[64,72,128]{2,1,0:T(8,128)(2,1)} %tiles_grad.5), calls=%async_computation.6 | async-start | bytes 2359296 | tf_op jit(solution)/shard_map/embed_grad/all_to_all | solution.py:575
  157.4 3.0 %collective-permute-start.1 = (bf16[4,96,256]{2,1,0:T(8,128)(2,1)}, bf16[4,96,256]{2,1,0:T(8,128)(2,1)S(1)}, u32[]{:S(2)}, u32[]{:S(2)}) collective-permute-start(bf16[4,96,256]{2,1,0:T(8,128)(2,1)} %get-tuple-element.56), channel_id=1, source_target_pairs={{0,16},{16,0},{32,48},{48,32},{64,80},{80,64},{96,112},{112,96},{1... | collective-permute-start | bytes 589832 | tf_op jit(solution)/shard_map/qkv_grad/ppermute | solution.py:536
  160.4 0.7 copy-start.2
  162.9 11.3 %collective-permute-start.2 = (bf16[96,256]{1,0:T(8,128)(2,1)}, bf16[96,256]{1,0:T(8,128)(2,1)S(1)}, u32[]{:S(2)}, u32[]{:S(2)}) collective-permute-start(bf16[96,256]{1,0:T(8,128)(2,1)} %get-tuple-element.58), channel_id=1, source_target_pairs={{0,32},{16,48},{32,64},{48,80},{64,96},{80,112},{96,0},{112,16},{1... | collective-permute-start | bytes 147464 | tf_op jit(solution)/shard_map/qkv_grad/ppermute | solution.py:544
  164.5 9.9 %collective-permute-start.3 = (bf16[96,256]{1,0:T(8,128)(2,1)}, bf16[96,256]{1,0:T(8,128)(2,1)S(1)}, u32[]{:S(2)}, u32[]{:S(2)}) collective-permute-start(bf16[96,256]{1,0:T(8,128)(2,1)} %get-tuple-element.59), channel_id=1, source_target_pairs={{0,64},{16,80},{32,96},{48,112},{64,0},{80,16},{96,32},{112,48},{1... | collective-permute-start | bytes 147464 | tf_op jit(solution)/shard_map/qkv_grad/ppermute | solution.py:544
  167.3 7.0 %collective-permute-start.4 = (bf16[96,256]{1,0:T(8,128)(2,1)}, bf16[96,256]{1,0:T(8,128)(2,1)S(1)}, u32[]{:S(2)}, u32[]{:S(2)}) collective-permute-start(bf16[96,256]{1,0:T(8,128)(2,1)} %get-tuple-element.60), channel_id=1, source_target_pairs={{0,96},{16,112},{32,0},{48,16},{64,32},{80,48},{96,64},{112,80},{1... | collective-permute-start | bytes 147464 | tf_op jit(solution)/shard_map/qkv_grad/ppermute | solution.py:544
  174.2 0.6 copy-start.3
  174.3 0.6 copy-start.4
  174.4 0.6 copy-start.5
Sparse Core Ops, SparseCore 0:
  53.2 45.4 all-gather.1

commit v5 on v4

--- a/solution.py
+++ b/solution.py
@@ -257,25 +257,25 @@
             axis=1,
         )
         size = key.shape[1]
-        row = iota((size, 128), 0)
-        slide_of_key = jnp.where(row < near, row // seg, (row & 127) >> 6)
-        same = slide_of_key == iota((size, 128), 1) >> 6
-        score = jnp.where(same, dot(key, query, "tn") * SCALE, -1e30)
-        top = jnp.max(score, axis=0, keepdims=True)
+        column = iota((128, size), 1)
+        slide_of_key = jnp.where(column < near, column // seg, (column & 127) >> 6)
+        same = slide_of_key == iota((128, size), 0) >> 6
+        score = jnp.where(same, dot(query, key, "tn") * SCALE, -1e30)
+        top = jnp.max(score, axis=1, keepdims=True)
         prob = jnp.exp(score - top)
-        prob = prob * (1.0 / jnp.sum(prob, axis=0, keepdims=True))
-        dprob = dot(value, grad, "tn")
-        delta = jnp.sum(prob * dprob, axis=0, keepdims=True)
+        prob = prob * (1.0 / jnp.sum(prob, axis=1, keepdims=True))
+        dprob = dot(grad, value, "tn")
+        delta = jnp.sum(prob * dprob, axis=1, keepdims=True)
         dscore = (prob * (dprob - delta)).astype(HALFS)
         prob = prob.astype(HALFS)
-        dkey = dot(query, dscore[near:], "nt") * SCALE
-        dvalue = dot(grad, prob[near:], "nt")
+        dkey = dot(query, dscore[:, near:]) * SCALE
+        dvalue = dot(grad, prob[:, near:])
         for k in range(n):
             part = slice(k * 128, (k + 1) * 128)
             out_ref[k, :HEAD_SIZE, lanes] = dkey[:, part].astype(HALFS)
             out_ref[k, HEAD_SIZE:, lanes] = dvalue[:, part].astype(HALFS)
         dscore_ref[pair] = dscore
-        prob_ref[pair] = prob[:near]
+        prob_ref[pair] = prob[:, :near]
 
 
 def sum_body(
@@ -302,9 +302,9 @@
             axis=1,
         )
         dscore = dscore_ref[pair]
-        dquery_ref[:, lanes] = (dot(key, dscore) * SCALE).astype(HALFS)
-        dkey = dot(query, dscore[:near], "nt") * SCALE
-        dvalue = dot(grad, prob_ref[pair], "nt")
+        dquery_ref[:, lanes] = (dot(key, dscore, "nt") * SCALE).astype(HALFS)
+        dkey = dot(query, dscore[:, :near]) * SCALE
+        dvalue = dot(grad, prob_ref[pair])
         middle = slice(HEAD_SIZE, 2 * HEAD_SIZE)
         sum_ref[middle, spots] = (near_ref[middle, spots] + dkey).astype(HALFS)
         last = slice(2 * HEAD_SIZE, WIDTH)
@@ -346,13 +346,10 @@
         give_ref[chip] = all_ref[pl.ds(other, block), :].astype(HALFS)
 
 
-def give_body(grad_ref, give_ref, given_ref):
-    given_ref[...] = dot(grad_ref[...], give_ref[...]).astype(HALFS)
-
-
-def merge_body(grad_ref, keep_ref, given_ref, out_ref):
+def merge_body(grad_ref, other_grad_ref, keep_ref, other_keep_ref, out_ref):
     rows, size = out_ref.shape[1] * 2 // 3, 128
-    part = dot(grad_ref[...], keep_ref[...]) + given_ref[...].astype(FLOATS)
+    grad = jnp.concatenate([grad_ref[...], other_grad_ref[...]], axis=1)
+    part = dot(grad, jnp.concatenate([keep_ref[...], other_keep_ref[...]], axis=0))
     part = part.astype(HALFS)
     columns = part.shape[0] // rows
     for block in range(out_ref.shape[0] // columns):
@@ -393,6 +390,12 @@
     for ref in piece_refs:
         qkv = qkv + ref[...].astype(FLOATS)
     qkv_ref[...] = qkv.T[:WIDTH]
+
+
+def load_body(_, hbm_ref, vmem_ref, sem):
+    load = pltpu.make_async_copy(hbm_ref, vmem_ref, sem)
+    load.start()
+    load.wait()
 
 
 def back_body(rows_ref, weight_ref, pick0_ref, pick1_ref, grad_ref, back_ref):
@@ -431,7 +434,9 @@
 
     with jax.named_scope("dispatch"):
         sent = call(
-            dispatch_body, resident((devices * 8, tiles // 2)), [positions, tile_features]
+            dispatch_body,
+            resident((devices * 8, tiles // 2)),
+            [positions, tile_features],
         )
         base = call(slots_body, resident((slots, 128), jnp.int32), [positions])
         arrived = lax.all_to_all(
@@ -460,6 +465,14 @@
         chunks = lax.all_to_all(
             chunks.reshape(n_tile, CHUNK_ROWS, 128), "tile", 0, 0, tiled=True
         ).reshape(n_tile * CHUNK_ROWS, 128)
+    with jax.named_scope("swap_tiles"):
+        swap = [(i, i ^ 1) for i in range(n_slide)]
+        chips = n_slide // 2
+        narrow = tiles // n_slide
+        split = tile_rows.reshape(share, chips, 2, narrow)
+        keep_cols = lax.dynamic_index_in_dim(split, core, 2, False).reshape(share, tiles // 2)
+        give_cols = lax.dynamic_index_in_dim(split, 1 - core, 2, False).reshape(share, tiles // 2)
+        got_cols = lax.ppermute(give_cols, "slide", swap)
     with jax.named_scope("dilated"):
         few = rows // n_slide
         query, far, head_rows, local = call(
@@ -491,8 +504,8 @@
             far_body,
             [
                 resident((n_slide, 2 * HEAD_SIZE, few)),
-                shaped((2, rows, 128)),
-                shaped((2, rows // 2, 128)),
+                shaped((2, 128, rows)),
+                shaped((2, 128, rows // 2)),
             ],
             stay(query, dilated_grads, placed, far),
         )
@@ -522,7 +535,6 @@
         ).reshape(n_tile * WIDTH, 128)
     with jax.named_scope("qkv_grad"):
         all_rows = lax.all_gather(emb_rows, "tile", axis=0, tiled=True)
-        chips = n_slide // 2
         block = wide // n_slide
         keep_qkv, give_qkv = call(
             qkv_grad_body,
@@ -532,7 +544,6 @@
             scratch_shapes=[pltpu.VMEM((wide, 256), FLOATS)],
         )
         chip = (row_here // 2).astype(jnp.int32).reshape(1)
-        swap = [(i, i ^ 1) for i in range(n_slide)]
         given_qkv = lax.ppermute(give_qkv, "slide", swap)
         own_qkv, *pieces = call(
             merge_qkv_body,
@@ -547,22 +558,26 @@
             for k in range(1, chips)
         ]
     with jax.named_scope("tiles_grad"):
-        narrow = tiles // n_slide
-        split = tile_rows.reshape(share, chips, 2, narrow)
-        keep_cols = lax.dynamic_index_in_dim(split, core, 2, False).reshape(share, tiles // 2)
-        give_cols = lax.dynamic_index_in_dim(split, 1 - core, 2, False).reshape(share, tiles // 2)
+        loaded = call(
+            load_body,
+            resident(qkv_weight.shape),
+            [d_rows, qkv_weight],
+            anywhere=(0, 1),
+            scratch_shapes=[pltpu.SemaphoreType.DMA],
+        )
         grad_rows, back = call(
             back_body,
             [shaped((wide, share)), shaped((devices * 8, half))],
-            [*stay(back_rows), qkv_weight, pick0, pick1],
+            [*stay(back_rows, loaded), pick0, pick1],
         )
         back = lax.all_to_all(
             back.reshape(devices, 8, half), every, 0, 0, tiled=True
         ).reshape(devices * 8, half)
-        given = call(give_body, shaped((wide, tiles // 2)), [grad_rows, give_cols])
-        given = lax.ppermute(given, "slide", swap)
+        other_rows = lax.ppermute(grad_rows, "slide", swap)
         merged = call(
-            merge_body, shaped((chips * n_tile, 72, 128)), [grad_rows, keep_cols, given]
+            merge_body,
+            shaped((chips * n_tile, 72, 128)),
+            [grad_rows, *stay(other_rows), keep_cols, got_cols],
         )
         merged, back = lax.optimization_barrier((merged, back))
     with jax.named_scope("collect"):

time: 186 us -> 182 us (0.978)
  Pallas kernels: 51.9 us -> 48.9 us
    pallas_call x17, Pallas kernels: 51.9 us -> 48.9 us  [call(): pl.pallas_call(body, out_shape=outs, in_specs=specs, out_specs=out_specs,...]
  transfers between devices with their start and end apart: 13 -> 14, of which waited for: 7 -> 9; matrix products, arithmetic and copies ran while one was open for 3% -> 3% of each run, Pallas kernels for 22% -> 20%
where the time goes in v5:
time: 182 us; the launch traced here: 180 us
  waiting for transfers between devices  66.5 us (37%)
  Pallas kernels  48.9 us (27%)
  starting transfers between devices  43.3 us (24%)
  between operations  14.3 us (8%)
  matrix products  3.99 us (2%)
  local copies, waits for them, and re-layouts  2.95 us (2%)
    pallas_call x17, Pallas kernels, call(): pl.pallas_call(body, out_shape=outs, in_specs=specs, out_specs=out_specs,...  48.9 us
    all_to_all x1, waiting for transfers between devices, per_device(): lax.all_to_all(sent.reshape(devices, 8, tiles // 2), every, 0, 0, tiled=T...  24.4 us
    all_to_all x1, waiting for transfers between devices, per_device(): lax.all_to_all(chunks.reshape(n_tile, CHUNK_ROWS, 128), 'tile', 0, 0, til...  13.5 us
    all_to_all x1, starting transfers between devices, per_device(): lax.all_to_all(sent.reshape(devices, 8, tiles // 2), every, 0, 0, tiled=T...  11.1 us
    all_to_all x1, waiting for transfers between devices, per_device(): lax.all_to_all(back.reshape(devices, 8, half), every, 0, 0, tiled=True)  10.7 us
    all_to_all x1, waiting for transfers between devices, per_device(): lax.all_to_all(back_chunks.reshape(n_tile, WIDTH, 128), 'tile', 0, 0, til...  10.3 us
    ppermute x3, starting transfers between devices, per_device(): lax.ppermute(pieces[k - 1], 'slide', [(i, (i + 2 * k) % n_slide) for i in...  5.81 us
    all_to_all x1, waiting for transfers between devices, per_device(): far_grads = lax.all_to_all(far_grads, 'slide', 0, 0, tiled=True)  5.44 us
  transfers between devices with their start and end apart: 14, of which 9 were waited for; matrix products, arithmetic and copies ran while one was open for 3% of the time, Pallas kernels for 20%

profile of v5, /device:TPU:0, one launch (start us, length us, event | category | flops | bytes accessed | tf_op | source)
XLA Modules:
  0.0 179.9 jit_solution(14754399684501186162)
XLA Ops:
  7.2 4.6 %dispatch.2 = bf16[1024,768]{1,0:T(8,128)(2,1)} custom-call(s32[384]{0:T(512)} %pos_ref.3, bf16[384,1536]{1,0:T(8,128)(2,1)} %tiles_ref.1), custom_call_target="tpu_custom_call" | custom-call | tf_op jit(solution)/shard_map/dispatch/pallas_call | solution.py:43
  11.8 11.1 %all-to-all-start = ((bf16[128,8,768]{2,1,0:T(8,128)(2,1)}), bf16[128,8,768]{2,1,0:T(8,128)(2,1)S(1)}, u32[]{:S(2)}, u32[]{:S(2)}) async-start(bf16[128,8,768]{2,1,0:T(8,128)(2,1)} %bitcast.2), calls=%async_computation | async-start | bytes 3145728 | tf_op jit(solution)/shard_map/dispatch/all_to_all | solution.py:442
  23.0 24.4 %all-to-all-done = bf16[128,8,768]{2,1,0:T(8,128)(2,1)S(1)} async-done(((bf16[128,8,768]{2,1,0:T(8,128)(2,1)}), bf16[128,8,768]{2,1,0:T(8,128)(2,1)S(1)}, u32[]{:S(2)}, u32[]{:S(2)}) %all-to-all-start) | async-done | bytes 1572896 | tf_op jit(solution)/shard_map/dispatch/all_to_all | solution.py:442
  47.4 5.7 %project.1 = (bf16[128,768]{1,0:T(8,128)(2,1)}, bf16[128,1536]{1,0:T(8,128)(2,1)}, bf16[2560,128]{1,0:T(8,128)(2,1)}, bf16[1024,128]{1,0:T(8,128)(2,1)}, bf16[1024,128]{1,0:T(8,128)(2,1)}) custom-call(s32[1]{0:T(128)} %bitcast.1.odd_ref, bf16[1024,768]{1,0:T(8,128)(2,1)S(1)} %bitcast.20, bf16[1536,768]{1,0:T(8,128)(2,1)} %embed_hbm_ref.1, ...), custom_call_target="tpu_custom_call" | custom-call | tf_op jit(solution)/shard_map/project/pallas_call | solution.py:43
  53.1 3.7 %all-to-all-start.1 = ((bf16[16,160,128]{2,1,0:T(8,128)(2,1)}), bf16[16,160,128]{2,1,0:T(8,128)(2,1)S(1)}, u32[]{:S(2)}, u32[]{:S(2)}) async-start(bf16[16,160,128]{2,1,0:T(8,128)(2,1)} %bitcast.4), calls=%async_computation.1 | async-start | bytes 1310720 | tf_op jit(solution)/shard_map/project/all_to_all | solution.py:465
  58.0 13.5 %all-to-all-done.1 = bf16[16,160,128]{2,1,0:T(8,128)(2,1)S(1)} async-done(((bf16[16,160,128]{2,1,0:T(8,128)(2,1)}), bf16[16,160,128]{2,1,0:T(8,128)(2,1)S(1)}, u32[]{:S(2)}, u32[]{:S(2)}) %all-to-all-start.1) | async-done | bytes 655392 | tf_op jit(solution)/shard_map/project/all_to_all | solution.py:465
  71.4 1.3 dilated.1
  72.7 3.6 %all-to-all-start.2 = ((bf16[8,96,256]{2,1,0:T(8,128)(2,1)}), bf16[8,96,256]{2,1,0:T(8,128)(2,1)S(1)}, u32[]{:S(2)}, u32[]{:S(2)}) async-start(bf16[8,96,256]{2,1,0:T(8,128)(2,1)} %get-tuple-element.38), calls=%async_computation.2 | async-start | bytes 786432 | tf_op jit(solution)/shard_map/dilated/all_to_all | solution.py:489
  76.4 8.8 %near.3 = (bf16[144,2048]{1,0:T(8,128)(2,1)S(1)}, f32[144,2048]{1,0:T(8,128)S(1)}) custom-call(s32[1]{0:T(128)} %bitcast.phase_ref, bf16[144,2048]{1,0:T(8,128)(2,1)} %get-tuple-element.36.rows_ref, s32[8,2048]{1,0:T(8,128)S(1)} %get-tuple-element.34.local_ref, bf16[4,48,512]{2,1,0:T(8,128)(2,1)} %bitcast.28), custom_call_target="tpu_custom_call" | custom-call | flops 8000000000 | bytes 8000000 | tf_op jit(solution)/shard_map/near/pallas_call | solution.py:43
  85.2 3.0 %far.1 = (bf16[8,96,256]{2,1,0:T(8,128)(2,1)}, bf16[2,128,2048]{2,1,0:T(8,128)(2,1)}, bf16[2,128,1024]{2,1,0:T(8,128)(2,1)}) custom-call(bf16[48,256]{1,0:T(8,128)(2,1)S(1)} %get-tuple-element.35.query_ref, bf16[48,256]{1,0:T(8,128)(2,1)S(1)} %near.2.grad_ref, bf16[144,2048]{1,0:T(8,128)(2,1)S(1)} %get-tuple-element.37.place_ref, ...), custom_call_target="tpu_custom_call" | custom-call | tf_op jit(solution)/shard_map/far/pallas_call | solution.py:43
  88.2 4.5 %all-to-all-start.3 = ((bf16[8,96,256]{2,1,0:T(8,128)(2,1)}), bf16[8,96,256]{2,1,0:T(8,128)(2,1)S(1)}, u32[]{:S(2)}, u32[]{:S(2)}) async-start(bf16[8,96,256]{2,1,0:T(8,128)(2,1)} %get-tuple-element.44), calls=%async_computation.3 | async-start | bytes 786432 | tf_op jit(solution)/shard_map/far/all_to_all | solution.py:512
  92.7 2.0 %unplace.3 = (bf16[48,256]{1,0:T(8,128)(2,1)S(1)}, bf16[144,2048]{1,0:T(8,128)(2,1)S(1)}) custom-call(bf16[48,256]{1,0:T(8,128)(2,1)S(1)} %get-tuple-element.35.query_ref, bf16[48,256]{1,0:T(8,128)(2,1)S(1)} %near.2.grad_ref, bf16[144,2048]{1,0:T(8,128)(2,1)S(1)} %get-tuple-element.37.place_ref, bf16[8,96,256]{2,1,0:T(8,128)(2,1)S(1)} %all-to-all-done.2.far_ref, ...), custom_call_target="tpu_custom_call" | custom-call | tf_op jit(solution)/shard_map/unplace/pallas_call | solution.py:43
  94.7 1.5 unplace.4.main_ref
  96.2 5.4 %all-to-all-done.3.far_ref = bf16[8,96,256]{2,1,0:T(8,128)(2,1)S(1)} async-done(((bf16[8,96,256]{2,1,0:T(8,128)(2,1)}), bf16[8,96,256]{2,1,0:T(8,128)(2,1)S(1)}, u32[]{:S(2)}, u32[]{:S(2)}) %all-to-all-start.3) | async-done | bytes 393248 | tf_op jit(solution)/shard_map/far/all_to_all | solution.py:512
  101.7 1.4 unplace.5
  103.0 4.3 %all-to-all-start.4 = ((bf16[16,144,128]{2,1,0:T(8,128)(2,1)}), bf16[16,144,128]{2,1,0:T(8,128)(2,1)}, u32[]{:S(2)}, u32[]{:S(2)}) async-start(bf16[16,144,128]{2,1,0:T(8,128)(2,1)} %bitcast.7), calls=%async_computation.4 | async-start | bytes 1179648 | tf_op jit(solution)/shard_map/unplace/all_to_all | solution.py:533
  107.3 2.0 %tiles_grad.3.weight_ref = bf16[768,2304]{1,0:T(8,128)(2,1)S(1)} custom-call(bf16[144,2048]{1,0:T(8,128)(2,1)} %get-tuple-element.46._.grad_ref, bf16[768,2304]{1,0:T(8,128)(2,1)} %hbm_ref.1), custom_call_target="tpu_custom_call" | custom-call | tf_op jit(solution)/shard_map/tiles_grad/pallas_call | solution.py:43
  109.3 10.3 %all-to-all-done.4 = bf16[16,144,128]{2,1,0:T(8,128)(2,1)} async-done(((bf16[16,144,128]{2,1,0:T(8,128)(2,1)}), bf16[16,144,128]{2,1,0:T(8,128)(2,1)}, u32[]{:S(2)}, u32[]{:S(2)}) %all-to-all-start.4) | async-done | bytes 589856 | tf_op jit(solution)/shard_map/unplace/all_to_all | solution.py:533
  119.6 4.5 %tiles_grad.4 = (bf16[768,128]{1,0:T(8,128)(2,1)}, bf16[1024,384]{1,0:T(8,128)(2,1)}) custom-call(bf16[2304,128]{1,0:T(8,128)(2,1)} %bitcast.8.rows_ref, bf16[768,2304]{1,0:T(8,128)(2,1)S(1)} %tiles_grad.3.weight_ref, bf16[1024,128]{1,0:T(8,128)(2,1)} %get-tuple-element.47.pick0_ref, bf16[1024,128]{1,0:T(8,128)(2,1)} %get-tuple-element.48.pick1_ref), custom_call_target="tpu_custom_call" | custom-call | tf_op jit(solution)/shard_map/tiles_grad/pallas_call | solution.py:43
  124.1 5.0 %all-to-all-start.5 = ((bf16[128,8,384]{2,1,0:T(8,128)(2,1)}), bf16[128,8,384]{2,1,0:T(8,128)(2,1)S(1)}, u32[]{:S(2)}, u32[]{:S(2)}) async-start(bf16[128,8,384]{2,1,0:T(8,128)(2,1)} %bitcast.24), calls=%async_computation.5 | async-start | bytes 1572864 | tf_op jit(solution)/shard_map/tiles_grad/all_to_all | solution.py:573
  131.7 2.7 %tiles_grad.5 = bf16[64,72,128]{2,1,0:T(8,128)(2,1)} custom-call(bf16[768,128]{1,0:T(8,128)(2,1)} %get-tuple-element.49.grad_ref, bf16[768,128]{1,0:T(8,128)(2,1)S(1)} %collective-permute-done.other_grad_ref, bf16[128,768]{1,0:T(8,128)(2,1)} %copy.12.keep_ref, bf16[128,768]{1,0:T(8,128)(2,1)} %copy-done.3), custom_call_target="tpu_custom_call" | custom-call | tf_op jit(solution)/shard_map/tiles_grad/pallas_call | solution.py:43
  134.4 10.7 %all-to-all-done.5 = bf16[128,8,384]{2,1,0:T(8,128)(2,1)S(1)} async-done(((bf16[128,8,384]{2,1,0:T(8,128)(2,1)}), bf16[128,8,384]{2,1,0:T(8,128)(2,1)S(1)}, u32[]{:S(2)}, u32[]{:S(2)}) %all-to-all-start.5) | async-done | bytes 786464 | tf_op jit(solution)/shard_map/tiles_grad/all_to_all | solution.py:573
  145.2 4.7 %all-to-all-start.6 = ((bf16[64,72,128]{2,1,0:T(8,128)(2,1)}), bf16[64,72,128]{2,1,0:T(8,128)(2,1)S(1)}, u32[]{:S(2)}, u32[]{:S(2)}) async-start(bf16[64,72,128]{2,1,0:T(8,128)(2,1)} %tiles_grad.5), calls=%async_computation.6 | async-start | bytes 2359296 | tf_op jit(solution)/shard_map/embed_grad/all_to_all | solution.py:590
  149.9 3.7 %qkv_grad.2 = (f32[4,96,256]{2,1,0:T(8,128)}, bf16[4,96,256]{2,1,0:T(8,128)(2,1)}) custom-call(s32[1]{0:T(128)} %bitcast.15.core_ref, bf16[144,2048]{1,0:T(8,128)(2,1)} %get-tuple-element.46._.grad_ref, bf16[2048,768]{1,0:T(8,128)(2,1)} %all-gather.2.cloned.1.call-done.rows_ref), custom_call_target="tpu_custom_call" | custom-call | tf_op jit(solution)/shard_map/qkv_grad/pallas_call | solution.py:43
  154.7 2.0 %collect.1 = bf16[384,768]{1,0:T(8,128)(2,1)} custom-call(bf16[1024,384]{1,0:T(8,128)(2,1)S(1)} %bitcast.21, s32[384,128]{1,0:T(8,128)S(1)} %dispatch.3.base_ref), custom_call_target="tpu_custom_call" | custom-call | tf_op jit(solution)/shard_map/collect/pallas_call | solution.py:43
  157.4 1.7 qkv_grad.3
  159.1 1.6 collective-permute-start.3
  160.7 2.9 %collective-permute-start.4 = (bf16[96,256]{1,0:T(8,128)(2,1)}, bf16[96,256]{1,0:T(8,128)(2,1)S(1)}, u32[]{:S(2)}, u32[]{:S(2)}) collective-permute-start(bf16[96,256]{1,0:T(8,128)(2,1)} %get-tuple-element.59), channel_id=1, source_target_pairs={{0,64},{16,80},{32,96},{48,112},{64,0},{80,16},{96,32},{112,48},{1... | collective-permute-start | bytes 147464 | tf_op jit(solution)/shard_map/qkv_grad/ppermute | solution.py:555
  163.6 1.4 collective-permute-start.5
  164.9 4.0 %convolution_convert_fusion = bf16[384,1536]{1,0:T(8,128)(2,1)} fusion(bf16[384,768]{1,0:T(8,128)(2,1)} %collect.1, bf16[1536,768]{1,0:T(8,128)(2,1)} %embed_hbm_ref.1), kind=kOutput, calls=%fused_computation | convolution fusion | flops 906559488 | bytes 4128768 | tf_op jit(solution)/shard_map/feature_grad/dot_general | solution.py:601
  168.9 1.5 all-to-all-done.6.parts_ref
  171.2 1.9 %embed_grad.1 = (f32[48,192]{1,0:T(8,128)}, f32[144,96]{1,0:T(8,128)}) custom-call(s32[1]{0:T(128)} %bitcast.14.chip_ref, bf16[64,72,128]{2,1,0:T(8,128)(2,1)S(1)} %all-to-all-done.6.parts_ref, f32[96,256]{1,0:T(8,128)} %get-tuple-element.57.own_ref, bf16[96,256]{1,0:T(8,128)(2,1)} %copy-done.4, bf16[96,256]{1,0:T(8,128)(2,1)} %copy-done.5, ...), custom_call_target="tpu_custom_call" | custom-call | tf_op jit(solution)/shard_map/embed_grad/pallas_call | solution.py:43
  (33 shorter events, 6.4 us)
Async XLA Ops:
  11.8 35.6 %all-to-all-start = ((bf16[128,8,768]{2,1,0:T(8,128)(2,1)}), bf16[128,8,768]{2,1,0:T(8,128)(2,1)S(1)}, u32[]{:S(2)}, u32[]{:S(2)}) async-start(bf16[128,8,768]{2,1,0:T(8,128)(2,1)} %bitcast.2), calls=%async_computation | async-start | bytes 3145728 | tf_op jit(solution)/shard_map/dispatch/all_to_all | solution.py:442
  23.0 127.0 %all-gather.2.cloned.1.call-start = ((), (), s32[]{:S(2)}) async-start(), calls=%async_computation.7 | async-start | bytes 3342336 | tf_op jit(solution)/shard_map/qkv_grad/all_gather | solution.py:537
  53.1 18.3 %all-to-all-start.1 = ((bf16[16,160,128]{2,1,0:T(8,128)(2,1)}), bf16[16,160,128]{2,1,0:T(8,128)(2,1)S(1)}, u32[]{:S(2)}, u32[]{:S(2)}) async-start(bf16[16,160,128]{2,1,0:T(8,128)(2,1)} %bitcast.4), calls=%async_computation.1 | async-start | bytes 1310720 | tf_op jit(solution)/shard_map/project/all_to_all | solution.py:465
  72.7 12.5 %all-to-all-start.2 = ((bf16[8,96,256]{2,1,0:T(8,128)(2,1)}), bf16[8,96,256]{2,1,0:T(8,128)(2,1)S(1)}, u32[]{:S(2)}, u32[]{:S(2)}) async-start(bf16[8,96,256]{2,1,0:T(8,128)(2,1)} %get-tuple-element.38), calls=%async_computation.2 | async-start | bytes 786432 | tf_op jit(solution)/shard_map/dilated/all_to_all | solution.py:489
  88.2 13.5 %all-to-all-start.3 = ((bf16[8,96,256]{2,1,0:T(8,128)(2,1)}), bf16[8,96,256]{2,1,0:T(8,128)(2,1)S(1)}, u32[]{:S(2)}, u32[]{:S(2)}) async-start(bf16[8,96,256]{2,1,0:T(8,128)(2,1)} %get-tuple-element.44), calls=%async_computation.3 | async-start | bytes 786432 | tf_op jit(solution)/shard_map/far/all_to_all | solution.py:512
  103.0 16.6 %all-to-all-start.4 = ((bf16[16,144,128]{2,1,0:T(8,128)(2,1)}), bf16[16,144,128]{2,1,0:T(8,128)(2,1)}, u32[]{:S(2)}, u32[]{:S(2)}) async-start(bf16[16,144,128]{2,1,0:T(8,128)(2,1)} %bitcast.7), calls=%async_computation.4 | async-start | bytes 1179648 | tf_op jit(solution)/shard_map/unplace/all_to_all | solution.py:533
  124.1 5.0 %copy-start = (bf16[128,1536]{1,0:T(8,128)(2,1)S(1)}, bf16[128,1536]{1,0:T(8,128)(2,1)}, u32[]{:S(2)}) copy-start(bf16[128,1536]{1,0:T(8,128)(2,1)} %get-tuple-element.50) | copy-start | bytes 1179652
  124.1 5.5 %copy-start.2 = (bf16[768,128]{1,0:T(8,128)(2,1)S(1)}, bf16[768,128]{1,0:T(8,128)(2,1)}, u32[]{:S(2)}) copy-start(bf16[768,128]{1,0:T(8,128)(2,1)} %get-tuple-element.49.grad_ref) | copy-start | bytes 589828
  124.1 21.1 %all-to-all-start.5 = ((bf16[128,8,384]{2,1,0:T(8,128)(2,1)}), bf16[128,8,384]{2,1,0:T(8,128)(2,1)S(1)}, u32[]{:S(2)}, u32[]{:S(2)}) async-start(bf16[128,8,384]{2,1,0:T(8,128)(2,1)} %bitcast.24), calls=%async_computation.5 | async-start | bytes 1572864 | tf_op jit(solution)/shard_map/tiles_grad/all_to_all | solution.py:573
  129.5 1.5 collective-permute-start.1
  129.6 1.7 collective-permute-start
  131.0 0.7 copy-start.3
  145.2 25.3 %all-to-all-start.6 = ((bf16[64,72,128]{2,1,0:T(8,128)(2,1)}), bf16[64,72,128]{2,1,0:T(8,128)(2,1)S(1)}, u32[]{:S(2)}, u32[]{:S(2)}) async-start(bf16[64,72,128]{2,1,0:T(8,128)(2,1)} %tiles_grad.5), calls=%async_computation.6 | async-start | bytes 2359296 | tf_op jit(solution)/shard_map/embed_grad/all_to_all | solution.py:590
  153.6 3.1 %collective-permute-start.2 = (bf16[4,96,256]{2,1,0:T(8,128)(2,1)}, bf16[4,96,256]{2,1,0:T(8,128)(2,1)S(1)}, u32[]{:S(2)}, u32[]{:S(2)}) collective-permute-start(bf16[4,96,256]{2,1,0:T(8,128)(2,1)} %get-tuple-element.56), channel_id=1, source_target_pairs={{0,16},{16,0},{32,48},{48,32},{64,80},{80,64},{96,112},{112,96},{1... | collective-permute-start | bytes 589832 | tf_op jit(solution)/shard_map/qkv_grad/ppermute | solution.py:547
  156.7 0.7 copy-start.1
  159.1 11.3 %collective-permute-start.3 = (bf16[96,256]{1,0:T(8,128)(2,1)}, bf16[96,256]{1,0:T(8,128)(2,1)S(1)}, u32[]{:S(2)}, u32[]{:S(2)}) collective-permute-start(bf16[96,256]{1,0:T(8,128)(2,1)} %get-tuple-element.58), channel_id=1, source_target_pairs={{0,32},{16,48},{32,64},{48,80},{64,96},{80,112},{96,0},{112,16},{1... | collective-permute-start | bytes 147464 | tf_op jit(solution)/shard_map/qkv_grad/ppermute | solution.py:555
  160.7 9.9 %collective-permute-start.4 = (bf16[96,256]{1,0:T(8,128)(2,1)}, bf16[96,256]{1,0:T(8,128)(2,1)S(1)}, u32[]{:S(2)}, u32[]{:S(2)}) collective-permute-start(bf16[96,256]{1,0:T(8,128)(2,1)} %get-tuple-element.59), channel_id=1, source_target_pairs={{0,64},{16,80},{32,96},{48,112},{64,0},{80,16},{96,32},{112,48},{1... | collective-permute-start | bytes 147464 | tf_op jit(solution)/shard_map/qkv_grad/ppermute | solution.py:555
  163.6 7.0 %collective-permute-start.5 = (bf16[96,256]{1,0:T(8,128)(2,1)}, bf16[96,256]{1,0:T(8,128)(2,1)S(1)}, u32[]{:S(2)}, u32[]{:S(2)}) collective-permute-start(bf16[96,256]{1,0:T(8,128)(2,1)} %get-tuple-element.60), channel_id=1, source_target_pairs={{0,96},{16,112},{32,0},{48,16},{64,32},{80,48},{96,64},{112,80},{1... | collective-permute-start | bytes 147464 | tf_op jit(solution)/shard_map/qkv_grad/ppermute | solution.py:555
  170.4 0.6 copy-start.4
  170.6 0.6 copy-start.5
  170.6 0.6 copy-start.6
Sparse Core Ops, SparseCore 0:
  53.2 45.4 all-gather.1

commit v6 on v5

--- a/solution.py
+++ b/solution.py
@@ -79,11 +79,23 @@
     return pos, few, dest, sub, mask
 
 
+def interleave(first, second):
+    step, half = first.shape
+    upper = (iota((step, half), 0) & 7) < 4
+    even = jnp.where(upper, first, pltpu.roll(second, 4, 0))
+    odd = jnp.where(upper, pltpu.roll(first, step - 4, 0), second)
+    both = jnp.stack(
+        [even.reshape(step // 8, 8, half), odd.reshape(step // 8, 8, half)], axis=1
+    )
+    return both.reshape(2 * step, half)
+
+
 def dispatch_body(pos_ref, tiles_ref, send_ref):
     slots = tiles_ref.shape[0]
-    half = tiles_ref.shape[1] // 2
+    half = send_ref.shape[1]
+    rest = tiles_ref.shape[1] - 2 * half
     pos, few, dest, sub, mask = place(pos_ref)
-    base = dest + 2 * sub
+    dest, mask = dest >> 1, jnp.where(few, -5, -1)
     local = ((pos >> 12) << 9) + (pos & 511)
     lane = iota((128, slots), 0) - 4 * sub
     notes = jnp.where(
@@ -92,21 +104,31 @@
         jnp.where(lane == 1, local & 127, jnp.where((lane == 2) & few, 1, 0)),
     )
     notes = notes.astype(FLOATS).astype(HALFS)
-    step = 256
-    for start in range(0, send_ref.shape[0], step):
+    last = [jnp.where(sub == k, dest + 3, -16) for k in range(3)]
+    step = 128
+    for start in range(0, send_ref.shape[0] // 2, step):
         rows = (iota((step, slots), 0) + start) & mask
-        out = dot(hot(rows == base), tiles_ref[:, :half])
-        out = out + dot(hot(rows == base + 1), tiles_ref[:, half:])
-        send_ref[start : start + step, :] = out.astype(HALFS)
-        info = dot(hot(rows == dest + 6), notes, "nt")
-        send_ref[start : start + step, :128] = (out[:, :128] + info).astype(HALFS)
+        whole_rows = hot(rows == dest + sub)
+        tail = tiles_ref[:, 2 * half :]
+        first = jnp.concatenate(
+            [dot(hot(rows == last[k]), tail) for k in range(2)]
+            + [dot(hot(rows == dest + 3), notes, "nt")],
+            axis=1,
+        )
+        first = first + dot(whole_rows, tiles_ref[:, :half])
+        second = dot(whole_rows, tiles_ref[:, half : 2 * half])
+        second = jnp.concatenate(
+            [second[:, :rest] + dot(hot(rows == last[2]), tail), second[:, rest:]], axis=1
+        )
+        both = interleave(first, second)
+        send_ref[2 * start : 2 * (start + step), :] = both.astype(HALFS)
 
 
 def slots_body(pos_ref, base_ref):
     slots = pos_ref.shape[0]
     _, _, dest, sub, mask = place(pos_ref)
     same = iota((slots, slots), 0) == iota((slots, slots), 1)
-    base = jnp.sum(jnp.where(same, dest + 2 * sub, 0), axis=1, keepdims=True)
+    base = jnp.sum(jnp.where(same, dest + sub, 0), axis=1, keepdims=True)
     base_ref[...] = jnp.where(iota(base_ref.shape, 1) == 0, base, mask)
 
 
@@ -118,8 +140,7 @@
     emb_ref,
     tiles_ref,
     chunk_ref,
-    pick0_ref,
-    pick1_ref,
+    pick_ref,
     embed_ref,
     weight_ref,
     embed_sem,
@@ -131,8 +152,9 @@
     weight_load.start()
     total = recv_ref.shape[0]
     senders = total // 8
-    sel = hot(iota((senders, total), 1) == 8 * iota((senders, total), 0) + 6)
-    notes = dot(sel, recv_ref[:, :128])
+    sel = hot(iota((senders, total), 1) == 8 * iota((senders, total), 0) + 3)
+    half = recv_ref.shape[1]
+    notes = dot(sel, recv_ref[:, half - 128 :])
     lane = iota((senders, 128), 1)
     lower = hot(iota((senders, senders), 0) > iota((senders, senders), 1))
     shared = (notes > 0.5) & (lane == 2)
@@ -154,19 +176,30 @@
     notes_all = dot(repeat, notes.astype(HALFS))
     turn = iota((total, 128), 0) & 7
     lanes = iota((total, 128), 1)
-    mine = (lanes == 4 * (turn >> 1)) & (turn < 6)
-    mine_low = (lanes == 4 * (turn >> 1) + 1) & (turn < 6)
+    slot = turn & 3
+    here = 4 * jnp.where(slot < 3, slot, jnp.where(turn == 3, 0, 2))
+    mine = lanes == here
+    mine_low = lanes == here + 1
     spot = jnp.sum(jnp.where(mine, index_all + 1.0, 0.0), axis=1, keepdims=True) - 1.0
+    middle = jnp.where((lanes == 4) & (turn == 3), index_all + 1.0, 0.0)
+    middle = jnp.sum(middle, axis=1, keepdims=True) - 1.0
     high = jnp.sum(jnp.where(mine, notes_all, 0.0), axis=1, keepdims=True)
     low = jnp.sum(jnp.where(mine_low, notes_all, 0.0), axis=1, keepdims=True)
     match = spot.astype(jnp.int32) == lanes
-    pick0 = hot(match & ((turn & 1) == 0))
-    pick1 = hot(match & ((turn & 1) == 1))
-    pick0_ref[...] = pick0
-    pick1_ref[...] = pick1
-    half = recv_ref.shape[1]
+    pick0 = hot(match & (turn < 3))
+    pick1 = hot(match & (turn > 3) & (turn < 7))
+    pick_rest = hot(match & (slot == 3))
+    pick_middle = hot(middle.astype(jnp.int32) == lanes)
+    slots_only = jnp.where(match & (slot < 3), 1.0, 0.0).reshape(senders // 2, 2, 8, 128)
+    upper = iota((senders // 2, 8, 128), 1) < 4
+    slots_only = jnp.where(upper, slots_only[:, 0], pltpu.roll(slots_only[:, 1], 4, 1))
+    pick_ref[...] = slots_only.reshape(total // 2, 128).astype(HALFS)
     tiles_ref[:, :half] = dot(pick0, recv_ref[...], "tn").astype(HALFS)
-    tiles_ref[:, half:] = dot(pick1, recv_ref[...], "tn").astype(HALFS)
+    tiles_ref[:, half : 2 * half] = dot(pick1, recv_ref[...], "tn").astype(HALFS)
+    rest = tiles_ref.shape[1] - 2 * half
+    tail = dot(pick_rest, recv_ref[:, :rest], "tn")
+    tail = tail + dot(pick_middle, recv_ref[:, rest : 2 * rest], "tn")
+    tiles_ref[:, 2 * half :] = tail.astype(HALFS)
     embed_load.wait()
     emb_ref[...] = dot(tiles_ref[...], embed_ref[...]).astype(HALFS)
     info = jnp.where(lanes == 0, high, jnp.where(lanes == 1, low, 0.0)).astype(HALFS)
@@ -392,18 +425,36 @@
     qkv_ref[...] = qkv.T[:WIDTH]
 
 
-def load_body(_, hbm_ref, vmem_ref, sem):
-    load = pltpu.make_async_copy(hbm_ref, vmem_ref, sem)
-    load.start()
-    load.wait()
-
-
-def back_body(rows_ref, weight_ref, pick0_ref, pick1_ref, grad_ref, back_ref):
+def load_body(_, *refs):
+    count, sems = len(refs) // 2, refs[-1]
+    loads = [
+        pltpu.make_async_copy(refs[k], refs[count + k], sems.at[k]) for k in range(count)
+    ]
+    for load in loads:
+        load.start()
+    for load in loads:
+        load.wait()
+
+
+def load(after, *values):
+    return call(
+        load_body,
+        [resident(value.shape) for value in values],
+        [after, *values],
+        anywhere=range(len(values) + 1),
+        scratch_shapes=[pltpu.SemaphoreType.DMA((len(values),))],
+    )
+
+
+def back_body(rows_ref, weight_ref, pick_ref, grad_ref, back_ref):
     half = back_ref.shape[1]
     grad = dot(weight_ref[...], rows_ref[...]).astype(HALFS)
     grad_ref[...] = grad
-    back = dot(pick0_ref[...], grad[:half], "nt") + dot(pick1_ref[...], grad[half:], "nt")
-    back_ref[...] = back.astype(HALFS)
+    step = 128
+    for start in range(0, pick_ref.shape[0], step):
+        pick = pick_ref[start : start + step, :]
+        both = interleave(dot(pick, grad[:half], "nt"), dot(pick, grad[half:], "nt"))
+        back_ref[2 * start : 2 * (start + step), :] = both.astype(HALFS)
 
 
 def collect_body(recv_ref, base_ref, out_ref):
@@ -411,7 +462,7 @@
     base, mask = base_ref[:, 0:1], base_ref[:, 1:2]
     rows = iota((base.shape[0], total), 1) & mask
     out_ref[:, :half] = dot(hot(rows == base), recv_ref[...]).astype(HALFS)
-    out_ref[:, half:] = dot(hot(rows == base + 1), recv_ref[...]).astype(HALFS)
+    out_ref[:, half:] = dot(hot(rows == base + 4), recv_ref[...]).astype(HALFS)
 
 
 def per_device(tile_features, embed_weight, qkv_weight, positions, out_grad):
@@ -431,26 +482,26 @@
     odd = (col_here % 2).astype(jnp.int32).reshape(1)
     core = row_here % 2
     tiles = tile_features.shape[1]
+    packed = (tiles - 256) // 2
 
     with jax.named_scope("dispatch"):
         sent = call(
             dispatch_body,
-            resident((devices * 8, tiles // 2)),
+            resident((devices * 8, packed)),
             [positions, tile_features],
         )
         base = call(slots_body, resident((slots, 128), jnp.int32), [positions])
         arrived = lax.all_to_all(
-            sent.reshape(devices, 8, tiles // 2), every, 0, 0, tiled=True
-        ).reshape(devices * 8, tiles // 2)
+            sent.reshape(devices, 8, packed), every, 0, 0, tiled=True
+        ).reshape(devices * 8, packed)
     with jax.named_scope("project"):
-        emb_rows, tile_rows, chunks, pick0, pick1 = call(
+        emb_rows, tile_rows, chunks, pick = call(
             project_body,
             [
                 shaped((share, wide)),
                 shaped((share, tiles)),
                 resident((n_tile * CHUNK_ROWS, 128)),
-                shaped((devices * 8, 128)),
-                shaped((devices * 8, 128)),
+                shaped((devices * 4, 128)),
             ],
             [odd, *stay(arrived), embed_weight, qkv_weight],
             smem=(0,),
@@ -558,17 +609,11 @@
             for k in range(1, chips)
         ]
     with jax.named_scope("tiles_grad"):
-        loaded = call(
-            load_body,
-            resident(qkv_weight.shape),
-            [d_rows, qkv_weight],
-            anywhere=(0, 1),
-            scratch_shapes=[pltpu.SemaphoreType.DMA],
-        )
+        (weight_here,) = load(d_rows, qkv_weight)
         grad_rows, back = call(
             back_body,
             [shaped((wide, share)), shaped((devices * 8, half))],
-            [*stay(back_rows, loaded), pick0, pick1],
+            [*stay(back_rows, weight_here), pick],
         )
         back = lax.all_to_all(
             back.reshape(devices, 8, half), every, 0, 0, tiled=True

time: 182 us -> 179 us (0.984)
  waiting for transfers between devices: 66.5 us -> 63.9 us
    all_to_all x1, waiting for transfers between devices: 24.4 us -> 21.7 us  [per_device(): lax.all_to_all(sent.reshape(devices, 8, packed), every, 0, 0, tiled=True)]
where the time goes in v6:
time: 179 us; the launch traced here: 176 us
  waiting for transfers between devices  63.9 us (36%)
  Pallas kernels  48.2 us (27%)
  starting transfers between devices  42.9 us (24%)
  between operations  14.3 us (8%)
  matrix products  3.99 us (2%)
  local copies, waits for them, and re-layouts  3.18 us (2%)
    pallas_call x17, Pallas kernels, call(): pl.pallas_call(body, out_shape=outs, in_specs=specs, out_specs=out_specs,...  48.2 us
    all_to_all x1, waiting for transfers between devices, per_device(): lax.all_to_all(sent.reshape(devices, 8, packed), every, 0, 0, tiled=True)  21.7 us
    all_to_all x1, waiting for transfers between devices, per_device(): lax.all_to_all(chunks.reshape(n_tile, CHUNK_ROWS, 128), 'tile', 0, 0, til...  13.4 us
    all_to_all x1, starting transfers between devices, per_device(): lax.all_to_all(sent.reshape(devices, 8, packed), every, 0, 0, tiled=True)  11.1 us
    all_to_all x1, waiting for transfers between devices, per_device(): lax.all_to_all(back.reshape(devices, 8, half), every, 0, 0, tiled=True)  10.8 us
    all_to_all x1, waiting for transfers between devices, per_device(): lax.all_to_all(back_chunks.reshape(n_tile, WIDTH, 128), 'tile', 0, 0, til...  10.3 us
    ppermute x3, starting transfers between devices, per_device(): lax.ppermute(pieces[k - 1], 'slide', [(i, (i + 2 * k) % n_slide) for i in...  5.81 us
    all_to_all x1, waiting for transfers between devices, per_device(): far_grads = lax.all_to_all(far_grads, 'slide', 0, 0, tiled=True)  5.44 us
  transfers between devices with their start and end apart: 14, of which 9 were waited for; matrix products, arithmetic and copies ran while one was open for 3% of the time, Pallas kernels for 20%

profile of v6, /device:TPU:0, one launch (start us, length us, event | category | flops | bytes accessed | tf_op | source)
XLA Modules:
  0.0 176.4 jit_solution(5361210878255507340)
XLA Ops:
  7.2 4.2 %dispatch.2 = bf16[1024,640]{1,0:T(8,128)(2,1)} custom-call(s32[384]{0:T(512)} %pos_ref.3, bf16[384,1536]{1,0:T(8,128)(2,1)} %tiles_ref.1), custom_call_target="tpu_custom_call" | custom-call | tf_op jit(solution)/shard_map/dispatch/pallas_call | solution.py:43
  11.4 11.1 %all-to-all-start = ((bf16[128,8,640]{2,1,0:T(8,128)(2,1)}), bf16[128,8,640]{2,1,0:T(8,128)(2,1)S(1)}, u32[]{:S(2)}, u32[]{:S(2)}) async-start(bf16[128,8,640]{2,1,0:T(8,128)(2,1)} %bitcast.2), calls=%async_computation | async-start | bytes 2621440 | tf_op jit(solution)/shard_map/dispatch/all_to_all | solution.py:494
  22.6 21.7 %all-to-all-done = bf16[128,8,640]{2,1,0:T(8,128)(2,1)S(1)} async-done(((bf16[128,8,640]{2,1,0:T(8,128)(2,1)}), bf16[128,8,640]{2,1,0:T(8,128)(2,1)S(1)}, u32[]{:S(2)}, u32[]{:S(2)}) %all-to-all-start) | async-done | bytes 1310752 | tf_op jit(solution)/shard_map/dispatch/all_to_all | solution.py:494
  44.3 6.0 %project.1 = (bf16[128,768]{1,0:T(8,128)(2,1)}, bf16[128,1536]{1,0:T(8,128)(2,1)}, bf16[2560,128]{1,0:T(8,128)(2,1)}, bf16[512,128]{1,0:T(8,128)(2,1)}) custom-call(s32[1]{0:T(128)} %bitcast.1.odd_ref, bf16[1024,640]{1,0:T(8,128)(2,1)S(1)} %bitcast.20, bf16[1536,768]{1,0:T(8,128)(2,1)} %embed_hbm_ref.1, bf16[768,2304]{1,0:T(8,128)(2,1)} %refs_0_.1), custom_call_target="tpu_custom_call" | custom-call | tf_op jit(solution)/shard_map/project/pallas_call | solution.py:43
  50.3 3.6 %all-to-all-start.1 = ((bf16[16,160,128]{2,1,0:T(8,128)(2,1)}), bf16[16,160,128]{2,1,0:T(8,128)(2,1)S(1)}, u32[]{:S(2)}, u32[]{:S(2)}) async-start(bf16[16,160,128]{2,1,0:T(8,128)(2,1)} %bitcast.4), calls=%async_computation.1 | async-start | bytes 1310720 | tf_op jit(solution)/shard_map/project/all_to_all | solution.py:516
  55.1 13.4 %all-to-all-done.1 = bf16[16,160,128]{2,1,0:T(8,128)(2,1)S(1)} async-done(((bf16[16,160,128]{2,1,0:T(8,128)(2,1)}), bf16[16,160,128]{2,1,0:T(8,128)(2,1)S(1)}, u32[]{:S(2)}, u32[]{:S(2)}) %all-to-all-start.1) | async-done | bytes 655392 | tf_op jit(solution)/shard_map/project/all_to_all | solution.py:516
  68.6 1.3 dilated.1
  69.8 3.6 %all-to-all-start.2 = ((bf16[8,96,256]{2,1,0:T(8,128)(2,1)}), bf16[8,96,256]{2,1,0:T(8,128)(2,1)S(1)}, u32[]{:S(2)}, u32[]{:S(2)}) async-start(bf16[8,96,256]{2,1,0:T(8,128)(2,1)} %get-tuple-element.37), calls=%async_computation.2 | async-start | bytes 786432 | tf_op jit(solution)/shard_map/dilated/all_to_all | solution.py:540
  73.5 8.8 %near.3 = (bf16[144,2048]{1,0:T(8,128)(2,1)S(1)}, f32[144,2048]{1,0:T(8,128)S(1)}) custom-call(s32[1]{0:T(128)} %bitcast.phase_ref, bf16[144,2048]{1,0:T(8,128)(2,1)} %get-tuple-element.35.rows_ref, s32[8,2048]{1,0:T(8,128)S(1)} %get-tuple-element.33.local_ref, bf16[4,48,512]{2,1,0:T(8,128)(2,1)} %bitcast.28), custom_call_target="tpu_custom_call" | custom-call | flops 8000000000 | bytes 8000000 | tf_op jit(solution)/shard_map/near/pallas_call | solution.py:43
  82.3 3.0 %far.1 = (bf16[8,96,256]{2,1,0:T(8,128)(2,1)}, bf16[2,128,2048]{2,1,0:T(8,128)(2,1)}, bf16[2,128,1024]{2,1,0:T(8,128)(2,1)}) custom-call(bf16[48,256]{1,0:T(8,128)(2,1)S(1)} %get-tuple-element.34.query_ref, bf16[48,256]{1,0:T(8,128)(2,1)S(1)} %near.2.grad_ref, bf16[144,2048]{1,0:T(8,128)(2,1)S(1)} %get-tuple-element.36.place_ref, ...), custom_call_target="tpu_custom_call" | custom-call | tf_op jit(solution)/shard_map/far/pallas_call | solution.py:43
  85.3 4.5 %all-to-all-start.3 = ((bf16[8,96,256]{2,1,0:T(8,128)(2,1)}), bf16[8,96,256]{2,1,0:T(8,128)(2,1)S(1)}, u32[]{:S(2)}, u32[]{:S(2)}) async-start(bf16[8,96,256]{2,1,0:T(8,128)(2,1)} %get-tuple-element.43), calls=%async_computation.3 | async-start | bytes 786432 | tf_op jit(solution)/shard_map/far/all_to_all | solution.py:563
  89.8 2.0 %unplace.3 = (bf16[48,256]{1,0:T(8,128)(2,1)S(1)}, bf16[144,2048]{1,0:T(8,128)(2,1)S(1)}) custom-call(bf16[48,256]{1,0:T(8,128)(2,1)S(1)} %get-tuple-element.34.query_ref, bf16[48,256]{1,0:T(8,128)(2,1)S(1)} %near.2.grad_ref, bf16[144,2048]{1,0:T(8,128)(2,1)S(1)} %get-tuple-element.36.place_ref, bf16[8,96,256]{2,1,0:T(8,128)(2,1)S(1)} %all-to-all-done.2.far_ref, ...), custom_call_target="tpu_custom_call" | custom-call | tf_op jit(solution)/shard_map/unplace/pallas_call | solution.py:43
  91.8 1.5 unplace.4.main_ref
  93.3 5.4 %all-to-all-done.3.far_ref = bf16[8,96,256]{2,1,0:T(8,128)(2,1)S(1)} async-done(((bf16[8,96,256]{2,1,0:T(8,128)(2,1)}), bf16[8,96,256]{2,1,0:T(8,128)(2,1)S(1)}, u32[]{:S(2)}, u32[]{:S(2)}) %all-to-all-start.3) | async-done | bytes 393248 | tf_op jit(solution)/shard_map/far/all_to_all | solution.py:563
  98.8 1.4 unplace.5
  100.1 4.3 %all-to-all-start.4 = ((bf16[16,144,128]{2,1,0:T(8,128)(2,1)}), bf16[16,144,128]{2,1,0:T(8,128)(2,1)}, u32[]{:S(2)}, u32[]{:S(2)}) async-start(bf16[16,144,128]{2,1,0:T(8,128)(2,1)} %bitcast.7), calls=%async_computation.4 | async-start | bytes 1179648 | tf_op jit(solution)/shard_map/unplace/all_to_all | solution.py:584
  104.4 2.0 %tiles_grad.3.weight_ref = bf16[768,2304]{1,0:T(8,128)(2,1)S(1)} custom-call(bf16[144,2048]{1,0:T(8,128)(2,1)} %get-tuple-element.45._.grad_ref, bf16[768,2304]{1,0:T(8,128)(2,1)} %refs_0_.1), custom_call_target="tpu_custom_call" | custom-call | tf_op jit(solution)/shard_map/tiles_grad/pallas_call | solution.py:43
  106.4 10.3 %all-to-all-done.4 = bf16[16,144,128]{2,1,0:T(8,128)(2,1)} async-done(((bf16[16,144,128]{2,1,0:T(8,128)(2,1)}), bf16[16,144,128]{2,1,0:T(8,128)(2,1)}, u32[]{:S(2)}, u32[]{:S(2)}) %all-to-all-start.4) | async-done | bytes 589856 | tf_op jit(solution)/shard_map/unplace/all_to_all | solution.py:584
  116.7 3.9 %tiles_grad.4 = (bf16[768,128]{1,0:T(8,128)(2,1)}, bf16[1024,384]{1,0:T(8,128)(2,1)}) custom-call(bf16[2304,128]{1,0:T(8,128)(2,1)} %bitcast.8.rows_ref, bf16[768,2304]{1,0:T(8,128)(2,1)S(1)} %tiles_grad.3.weight_ref, bf16[512,128]{1,0:T(8,128)(2,1)} %get-tuple-element.46.pick_ref), custom_call_target="tpu_custom_call" | custom-call | tf_op jit(solution)/shard_map/tiles_grad/pallas_call | solution.py:43
  120.6 5.0 %all-to-all-start.5 = ((bf16[128,8,384]{2,1,0:T(8,128)(2,1)}), bf16[128,8,384]{2,1,0:T(8,128)(2,1)S(1)}, u32[]{:S(2)}, u32[]{:S(2)}) async-start(bf16[128,8,384]{2,1,0:T(8,128)(2,1)} %bitcast.24), calls=%async_computation.5 | async-start | bytes 1572864 | tf_op jit(solution)/shard_map/tiles_grad/all_to_all | solution.py:618
  128.2 2.7 %tiles_grad.5 = bf16[64,72,128]{2,1,0:T(8,128)(2,1)} custom-call(bf16[768,128]{1,0:T(8,128)(2,1)} %get-tuple-element.47.grad_ref, bf16[768,128]{1,0:T(8,128)(2,1)S(1)} %collective-permute-done.other_grad_ref, bf16[128,768]{1,0:T(8,128)(2,1)} %copy.12.keep_ref, bf16[128,768]{1,0:T(8,128)(2,1)} %copy-done.3), custom_call_target="tpu_custom_call" | custom-call | tf_op jit(solution)/shard_map/tiles_grad/pallas_call | solution.py:43
  130.9 10.8 %all-to-all-done.5 = bf16[128,8,384]{2,1,0:T(8,128)(2,1)S(1)} async-done(((bf16[128,8,384]{2,1,0:T(8,128)(2,1)}), bf16[128,8,384]{2,1,0:T(8,128)(2,1)S(1)}, u32[]{:S(2)}, u32[]{:S(2)}) %all-to-all-start.5) | async-done | bytes 786464 | tf_op jit(solution)/shard_map/tiles_grad/all_to_all | solution.py:618
  141.7 4.7 %all-to-all-start.6 = ((bf16[64,72,128]{2,1,0:T(8,128)(2,1)}), bf16[64,72,128]{2,1,0:T(8,128)(2,1)S(1)}, u32[]{:S(2)}, u32[]{:S(2)}) async-start(bf16[64,72,128]{2,1,0:T(8,128)(2,1)} %tiles_grad.5), calls=%async_computation.6 | async-start | bytes 2359296 | tf_op jit(solution)/shard_map/embed_grad/all_to_all | solution.py:635
  146.4 3.7 %qkv_grad.2 = (f32[4,96,256]{2,1,0:T(8,128)}, bf16[4,96,256]{2,1,0:T(8,128)(2,1)}) custom-call(s32[1]{0:T(128)} %bitcast.15.core_ref, bf16[144,2048]{1,0:T(8,128)(2,1)} %get-tuple-element.45._.grad_ref, bf16[2048,768]{1,0:T(8,128)(2,1)} %all-gather.2.cloned.1.call-done.rows_ref), custom_call_target="tpu_custom_call" | custom-call | tf_op jit(solution)/shard_map/qkv_grad/pallas_call | solution.py:43
  151.2 2.0 %collect.1 = bf16[384,768]{1,0:T(8,128)(2,1)} custom-call(bf16[1024,384]{1,0:T(8,128)(2,1)S(1)} %bitcast.21, s32[384,128]{1,0:T(8,128)S(1)} %dispatch.3.base_ref), custom_call_target="tpu_custom_call" | custom-call | tf_op jit(solution)/shard_map/collect/pallas_call | solution.py:43
  153.9 1.7 qkv_grad.3
  155.6 1.6 collective-permute-start.3
  157.2 2.9 %collective-permute-start.4 = (bf16[96,256]{1,0:T(8,128)(2,1)}, bf16[96,256]{1,0:T(8,128)(2,1)S(1)}, u32[]{:S(2)}, u32[]{:S(2)}) collective-permute-start(bf16[96,256]{1,0:T(8,128)(2,1)} %get-tuple-element.57), channel_id=1, source_target_pairs={{0,64},{16,80},{32,96},{48,112},{64,0},{80,16},{96,32},{112,48},{1... | collective-permute-start | bytes 147464 | tf_op jit(solution)/shard_map/qkv_grad/ppermute | solution.py:606
  160.1 1.4 collective-permute-start.5
  161.5 4.0 %convolution_convert_fusion = bf16[384,1536]{1,0:T(8,128)(2,1)} fusion(bf16[384,768]{1,0:T(8,128)(2,1)} %collect.1, bf16[1536,768]{1,0:T(8,128)(2,1)} %embed_hbm_ref.1), kind=kOutput, calls=%fused_computation | convolution fusion | flops 906559488 | bytes 4128768 | tf_op jit(solution)/shard_map/feature_grad/dot_general | solution.py:646
  165.4 1.5 all-to-all-done.6.parts_ref
  167.7 1.9 %embed_grad.1 = (f32[48,192]{1,0:T(8,128)}, f32[144,96]{1,0:T(8,128)}) custom-call(s32[1]{0:T(128)} %bitcast.14.chip_ref, bf16[64,72,128]{2,1,0:T(8,128)(2,1)S(1)} %all-to-all-done.6.parts_ref, f32[96,256]{1,0:T(8,128)} %get-tuple-element.55.own_ref, bf16[96,256]{1,0:T(8,128)(2,1)} %copy-done.4, bf16[96,256]{1,0:T(8,128)(2,1)} %copy-done.5, ...), custom_call_target="tpu_custom_call" | custom-call | tf_op jit(solution)/shard_map/embed_grad/pallas_call | solution.py:43
  (33 shorter events, 6.3 us)
Async XLA Ops:
  11.4 32.9 %all-to-all-start = ((bf16[128,8,640]{2,1,0:T(8,128)(2,1)}), bf16[128,8,640]{2,1,0:T(8,128)(2,1)S(1)}, u32[]{:S(2)}, u32[]{:S(2)}) async-start(bf16[128,8,640]{2,1,0:T(8,128)(2,1)} %bitcast.2), calls=%async_computation | async-start | bytes 2621440 | tf_op jit(solution)/shard_map/dispatch/all_to_all | solution.py:494
  22.5 123.9 %all-gather.2.cloned.1.call-start = ((), (), s32[]{:S(2)}) async-start(), calls=%async_computation.7 | async-start | bytes 3342336 | tf_op jit(solution)/shard_map/qkv_grad/all_gather | solution.py:588
  50.3 18.2 %all-to-all-start.1 = ((bf16[16,160,128]{2,1,0:T(8,128)(2,1)}), bf16[16,160,128]{2,1,0:T(8,128)(2,1)S(1)}, u32[]{:S(2)}, u32[]{:S(2)}) async-start(bf16[16,160,128]{2,1,0:T(8,128)(2,1)} %bitcast.4), calls=%async_computation.1 | async-start | bytes 1310720 | tf_op jit(solution)/shard_map/project/all_to_all | solution.py:516
  69.8 12.5 %all-to-all-start.2 = ((bf16[8,96,256]{2,1,0:T(8,128)(2,1)}), bf16[8,96,256]{2,1,0:T(8,128)(2,1)S(1)}, u32[]{:S(2)}, u32[]{:S(2)}) async-start(bf16[8,96,256]{2,1,0:T(8,128)(2,1)} %get-tuple-element.37), calls=%async_computation.2 | async-start | bytes 786432 | tf_op jit(solution)/shard_map/dilated/all_to_all | solution.py:540
  85.3 13.5 %all-to-all-start.3 = ((bf16[8,96,256]{2,1,0:T(8,128)(2,1)}), bf16[8,96,256]{2,1,0:T(8,128)(2,1)S(1)}, u32[]{:S(2)}, u32[]{:S(2)}) async-start(bf16[8,96,256]{2,1,0:T(8,128)(2,1)} %get-tuple-element.43), calls=%async_computation.3 | async-start | bytes 786432 | tf_op jit(solution)/shard_map/far/all_to_all | solution.py:563
  100.1 16.6 %all-to-all-start.4 = ((bf16[16,144,128]{2,1,0:T(8,128)(2,1)}), bf16[16,144,128]{2,1,0:T(8,128)(2,1)}, u32[]{:S(2)}, u32[]{:S(2)}) async-start(bf16[16,144,128]{2,1,0:T(8,128)(2,1)} %bitcast.7), calls=%async_computation.4 | async-start | bytes 1179648 | tf_op jit(solution)/shard_map/unplace/all_to_all | solution.py:584
  120.6 5.0 %copy-start = (bf16[128,1536]{1,0:T(8,128)(2,1)S(1)}, bf16[128,1536]{1,0:T(8,128)(2,1)}, u32[]{:S(2)}) copy-start(bf16[128,1536]{1,0:T(8,128)(2,1)} %get-tuple-element.48) | copy-start | bytes 1179652
  120.6 21.1 %all-to-all-start.5 = ((bf16[128,8,384]{2,1,0:T(8,128)(2,1)}), bf16[128,8,384]{2,1,0:T(8,128)(2,1)S(1)}, u32[]{:S(2)}, u32[]{:S(2)}) async-start(bf16[128,8,384]{2,1,0:T(8,128)(2,1)} %bitcast.24), calls=%async_computation.5 | async-start | bytes 1572864 | tf_op jit(solution)/shard_map/tiles_grad/all_to_all | solution.py:618
  125.6 0.9 copy-start.2
  126.0 1.5 collective-permute-start.1
  126.5 1.4 collective-permute-start
  127.6 0.7 copy-start.3
  141.7 25.3 %all-to-all-start.6 = ((bf16[64,72,128]{2,1,0:T(8,128)(2,1)}), bf16[64,72,128]{2,1,0:T(8,128)(2,1)S(1)}, u32[]{:S(2)}, u32[]{:S(2)}) async-start(bf16[64,72,128]{2,1,0:T(8,128)(2,1)} %tiles_grad.5), calls=%async_computation.6 | async-start | bytes 2359296 | tf_op jit(solution)/shard_map/embed_grad/all_to_all | solution.py:635
  150.2 3.1 %collective-permute-start.2 = (bf16[4,96,256]{2,1,0:T(8,128)(2,1)}, bf16[4,96,256]{2,1,0:T(8,128)(2,1)S(1)}, u32[]{:S(2)}, u32[]{:S(2)}) collective-permute-start(bf16[4,96,256]{2,1,0:T(8,128)(2,1)} %get-tuple-element.54), channel_id=1, source_target_pairs={{0,16},{16,0},{32,48},{48,32},{64,80},{80,64},{96,112},{112,96},{1... | collective-permute-start | bytes 589832 | tf_op jit(solution)/shard_map/qkv_grad/ppermute | solution.py:598
  153.2 0.7 copy-start.1
  155.6 11.3 %collective-permute-start.3 = (bf16[96,256]{1,0:T(8,128)(2,1)}, bf16[96,256]{1,0:T(8,128)(2,1)S(1)}, u32[]{:S(2)}, u32[]{:S(2)}) collective-permute-start(bf16[96,256]{1,0:T(8,128)(2,1)} %get-tuple-element.56), channel_id=1, source_target_pairs={{0,32},{16,48},{32,64},{48,80},{64,96},{80,112},{96,0},{112,16},{1... | collective-permute-start | bytes 147464 | tf_op jit(solution)/shard_map/qkv_grad/ppermute | solution.py:606
  157.2 9.9 %collective-permute-start.4 = (bf16[96,256]{1,0:T(8,128)(2,1)}, bf16[96,256]{1,0:T(8,128)(2,1)S(1)}, u32[]{:S(2)}, u32[]{:S(2)}) collective-permute-start(bf16[96,256]{1,0:T(8,128)(2,1)} %get-tuple-element.57), channel_id=1, source_target_pairs={{0,64},{16,80},{32,96},{48,112},{64,0},{80,16},{96,32},{112,48},{1... | collective-permute-start | bytes 147464 | tf_op jit(solution)/shard_map/qkv_grad/ppermute | solution.py:606
  160.1 7.0 %collective-permute-start.5 = (bf16[96,256]{1,0:T(8,128)(2,1)}, bf16[96,256]{1,0:T(8,128)(2,1)S(1)}, u32[]{:S(2)}, u32[]{:S(2)}) collective-permute-start(bf16[96,256]{1,0:T(8,128)(2,1)} %get-tuple-element.58), channel_id=1, source_target_pairs={{0,96},{16,112},{32,0},{48,16},{64,32},{80,48},{96,64},{112,80},{1... | collective-permute-start | bytes 147464 | tf_op jit(solution)/shard_map/qkv_grad/ppermute | solution.py:606
  167.0 0.6 copy-start.4
  167.1 0.6 copy-start.5
  167.1 0.6 copy-start.6
Sparse Core Ops, SparseCore 0:
  50.4 45.3 all-gather.1

commit v7 on v6

--- a/solution.py
+++ b/solution.py
@@ -9,7 +9,7 @@
 
 HEAD_SIZE = 48
 WIDTH = 3 * HEAD_SIZE
-CHUNK_ROWS = 160
+CHUNK_ROWS = 152
 FLOATS = jnp.float32
 HALFS = jnp.bfloat16
 SCALE = HEAD_SIZE ** (-0.5)
@@ -35,10 +35,12 @@
     return pl.BlockSpec(memory_space=memory)
 
 
-def call(body, outs, args, smem=(), anywhere=(), **kw):
+def call(body, outs, args, smem=(), anywhere=(), blocks=None, **kw):
     specs = [whole(pltpu.SMEM if i in smem else pltpu.VMEM) for i in range(len(args))]
     for i in anywhere:
         specs[i] = whole(pl.ANY)
+    for i, block in (blocks or {}).items():
+        specs[i] = block
     out_specs = jax.tree.map(lambda _: whole(), outs)
     return pl.pallas_call(
         body,
@@ -90,10 +92,9 @@
     return both.reshape(2 * step, half)
 
 
-def dispatch_body(pos_ref, tiles_ref, send_ref):
-    slots = tiles_ref.shape[0]
-    half = send_ref.shape[1]
-    rest = tiles_ref.shape[1] - 2 * half
+def dispatch_body(pos_ref, left_ref, right_ref, rest_ref, send_ref):
+    slots, half = left_ref.shape
+    rest = rest_ref.shape[1]
     pos, few, dest, sub, mask = place(pos_ref)
     dest, mask = dest >> 1, jnp.where(few, -5, -1)
     local = ((pos >> 12) << 9) + (pos & 511)
@@ -109,14 +110,14 @@
     for start in range(0, send_ref.shape[0] // 2, step):
         rows = (iota((step, slots), 0) + start) & mask
         whole_rows = hot(rows == dest + sub)
-        tail = tiles_ref[:, 2 * half :]
+        tail = rest_ref[...]
         first = jnp.concatenate(
             [dot(hot(rows == last[k]), tail) for k in range(2)]
             + [dot(hot(rows == dest + 3), notes, "nt")],
             axis=1,
         )
-        first = first + dot(whole_rows, tiles_ref[:, :half])
-        second = dot(whole_rows, tiles_ref[:, half : 2 * half])
+        first = first + dot(whole_rows, left_ref[...])
+        second = dot(whole_rows, right_ref[...])
         second = jnp.concatenate(
             [second[:, :rest] + dot(hot(rows == last[2]), tail), second[:, rest:]], axis=1
         )
@@ -148,8 +149,15 @@
 ):
     embed_load = pltpu.make_async_copy(embed_hbm_ref, embed_ref, embed_sem)
     embed_load.start()
-    weight_load = pltpu.make_async_copy(weight_hbm_ref, weight_ref, weight_sem)
-    weight_load.start()
+    columns = weight_ref.shape[2]
+    weight_loads = [
+        pltpu.make_async_copy(
+            weight_hbm_ref.at[:, k * columns : (k + 1) * columns], weight_ref.at[k], weight_sem.at[k]
+        )
+        for k in range(2)
+    ]
+    for one in weight_loads:
+        one.start()
     total = recv_ref.shape[0]
     senders = total // 8
     sel = hot(iota((senders, total), 1) == 8 * iota((senders, total), 0) + 3)
@@ -203,28 +211,26 @@
     embed_load.wait()
     emb_ref[...] = dot(tiles_ref[...], embed_ref[...]).astype(HALFS)
     info = jnp.where(lanes == 0, high, jnp.where(lanes == 1, low, 0.0)).astype(HALFS)
-    info = dot(info, pick0, "tn")[:16].astype(HALFS)
-    weight_load.wait()
-    heads = chunk_ref.shape[0] // CHUNK_ROWS
+    info = dot(info, pick0, "tn")[: CHUNK_ROWS - WIDTH].astype(HALFS)
+    heads = chunk_ref.shape[0]
     for head in range(heads):
-        top = head * CHUNK_ROWS
-        if head % 8 == 0:
-            wide = slice(head * WIDTH, (head + 8) * WIDTH)
-            part = dot(emb_ref[...], weight_ref[:, wide]).T
-        columns = slice((head % 8) * WIDTH, (head % 8 + 1) * WIDTH)
-        chunk_ref[top : top + WIDTH, :] = part[columns].astype(HALFS)
-        chunk_ref[top + WIDTH : top + CHUNK_ROWS, :] = info
+        if head % (heads // 2) == 0:
+            group = head // (heads // 2)
+            weight_loads[group].wait()
+            part = dot(emb_ref[...], weight_ref[group]).T
+        first = (head % (heads // 2)) * WIDTH
+        chunk_ref[head, :WIDTH, :] = part[first : first + WIDTH].astype(HALFS)
+        chunk_ref[head, WIDTH:, :] = info
 
 
 def dilated_body(phase_ref, chunk_ref, query_ref, far_ref, rows_ref, local_ref):
-    blocks = chunk_ref.shape[0] // CHUNK_ROWS
+    blocks = chunk_ref.shape[0]
     total = jnp.zeros((WIDTH, query_ref.shape[1]), FLOATS)
     target = 8 * iota((query_ref.shape[1], 128), 0) + phase_ref[0]
     for block in range(blocks):
-        top = block * CHUNK_ROWS
         lanes = slice(block * 128, (block + 1) * 128)
-        part = chunk_ref[top : top + WIDTH, :]
-        info = chunk_ref[top + WIDTH : top + CHUNK_ROWS, :].astype(FLOATS)
+        part = chunk_ref[block, :WIDTH, :]
+        info = chunk_ref[block, WIDTH:, :].astype(FLOATS)
         local = ((info[0:1] - 1.0) * 128.0 + info[1:2]).astype(jnp.int32)
         rows_ref[:, lanes] = part
         local_ref[:, lanes] = jnp.broadcast_to(local, (8, 128))
@@ -488,7 +494,13 @@
         sent = call(
             dispatch_body,
             resident((devices * 8, packed)),
-            [positions, tile_features],
+            [positions] + [tile_features] * 3,
+            blocks={
+                1: pl.BlockSpec((slots, packed), lambda i: (0, 0)),
+                2: pl.BlockSpec((slots, packed), lambda i: (0, 1)),
+                3: pl.BlockSpec((slots, 256), lambda i: (0, (tiles - 256) // 256)),
+            },
+            grid=(1,),
         )
         base = call(slots_body, resident((slots, 128), jnp.int32), [positions])
         arrived = lax.all_to_all(
@@ -500,7 +512,7 @@
             [
                 shaped((share, wide)),
                 shaped((share, tiles)),
-                resident((n_tile * CHUNK_ROWS, 128)),
+                resident((n_tile, CHUNK_ROWS, 128)),
                 shaped((devices * 4, 128)),
             ],
             [odd, *stay(arrived), embed_weight, qkv_weight],
@@ -508,14 +520,12 @@
             anywhere=(2, 3),
             scratch_shapes=[
                 pltpu.VMEM(embed_weight.shape, HALFS),
-                pltpu.VMEM(qkv_weight.shape, HALFS),
+                pltpu.VMEM((2, wide, qkv_weight.shape[1] // 2), HALFS),
                 pltpu.SemaphoreType.DMA,
-                pltpu.SemaphoreType.DMA,
+                pltpu.SemaphoreType.DMA((2,)),
             ],
         )
-        chunks = lax.all_to_all(
-            chunks.reshape(n_tile, CHUNK_ROWS, 128), "tile", 0, 0, tiled=True
-        ).reshape(n_tile * CHUNK_ROWS, 128)
+        chunks = lax.all_to_all(chunks, "tile", 0, 0, tiled=True)
     with jax.named_scope("swap_tiles"):
         swap = [(i, i ^ 1) for i in range(n_slide)]
         chips = n_slide // 2

time: 179 us -> 178 us (level)
  transfers between devices with their start and end apart: 14 -> 14, of which waited for: 9 -> 9; matrix products, arithmetic and copies ran while one was open for 3% -> 3% of each run, Pallas kernels for 20% -> 21%
where the time goes in v7:
time: 178 us; the launch traced here: 175 us
  waiting for transfers between devices  63.6 us (36%)
  Pallas kernels  47.5 us (27%)
  starting transfers between devices  42.9 us (24%)
  between operations  14.3 us (8%)
  matrix products  3.99 us (2%)
  local copies, waits for them, and re-layouts  3.18 us (2%)
    pallas_call x17, Pallas kernels, call(): pl.pallas_call(body, out_shape=outs, in_specs=specs, out_specs=out_specs,...  47.5 us
    all_to_all x1, waiting for transfers between devices, per_device(): lax.all_to_all(sent.reshape(devices, 8, packed), every, 0, 0, tiled=True)  21.7 us
    all_to_all x1, waiting for transfers between devices, per_device(): chunks = lax.all_to_all(chunks, 'tile', 0, 0, tiled=True)  13.1 us
    all_to_all x1, starting transfers between devices, per_device(): lax.all_to_all(sent.reshape(devices, 8, packed), every, 0, 0, tiled=True)  11.1 us
    all_to_all x1, waiting for transfers between devices, per_device(): lax.all_to_all(back.reshape(devices, 8, half), every, 0, 0, tiled=True)  10.8 us
    all_to_all x1, waiting for transfers between devices, per_device(): lax.all_to_all(back_chunks.reshape(n_tile, WIDTH, 128), 'tile', 0, 0, til...  10.3 us
    ppermute x3, starting transfers between devices, per_device(): lax.ppermute(pieces[k - 1], 'slide', [(i, (i + 2 * k) % n_slide) for i in...  5.81 us
    all_to_all x1, waiting for transfers between devices, per_device(): far_grads = lax.all_to_all(far_grads, 'slide', 0, 0, tiled=True)  5.47 us
  transfers between devices with their start and end apart: 14, of which 9 were waited for; matrix products, arithmetic and copies ran while one was open for 3% of the time, Pallas kernels for 21%

profile of v7, /device:TPU:0, one launch (start us, length us, event | category | flops | bytes accessed | tf_op | source)
XLA Modules:
  0.0 175.5 jit_solution(11265433350006472484)
XLA Ops:
  7.2 4.2 %dispatch.2 = bf16[1024,640]{1,0:T(8,128)(2,1)} custom-call(s32[384]{0:T(512)} %pos_ref.3, bf16[384,1536]{1,0:T(8,128)(2,1)} %rest_ref.1, bf16[384,1536]{1,0:T(8,128)(2,1)} %rest_ref.1, bf16[384,1536]{1,0:T(8,128)(2,1)} %rest_ref.1), custom_call_target="tpu_custom_call" | custom-call | tf_op jit(solution)/shard_map/dispatch/pallas_call | solution.py:45
  11.3 11.1 %all-to-all-start = ((bf16[128,8,640]{2,1,0:T(8,128)(2,1)}), bf16[128,8,640]{2,1,0:T(8,128)(2,1)S(1)}, u32[]{:S(2)}, u32[]{:S(2)}) async-start(bf16[128,8,640]{2,1,0:T(8,128)(2,1)} %bitcast.2), calls=%async_computation | async-start | bytes 2621440 | tf_op jit(solution)/shard_map/dispatch/all_to_all | solution.py:506
  22.6 21.7 %all-to-all-done = bf16[128,8,640]{2,1,0:T(8,128)(2,1)S(1)} async-done(((bf16[128,8,640]{2,1,0:T(8,128)(2,1)}), bf16[128,8,640]{2,1,0:T(8,128)(2,1)S(1)}, u32[]{:S(2)}, u32[]{:S(2)}) %all-to-all-start) | async-done | bytes 1310752 | tf_op jit(solution)/shard_map/dispatch/all_to_all | solution.py:506
  44.3 5.3 %project.1 = (bf16[128,768]{1,0:T(8,128)(2,1)}, bf16[128,1536]{1,0:T(8,128)(2,1)}, bf16[16,152,128]{2,1,0:T(8,128)(2,1)}, bf16[512,128]{1,0:T(8,128)(2,1)}) custom-call(s32[1]{0:T(128)} %bitcast.1.odd_ref, bf16[1024,640]{1,0:T(8,128)(2,1)S(1)} %bitcast.18, bf16[1536,768]{1,0:T(8,128)(2,1)} %embed_hbm_ref.1, bf16[768,2304]{1,0:T(8,128)(2,1)} %refs_0_.1), custom_call_target="tpu_custom_call" | custom-call | tf_op jit(solution)/shard_map/project/pallas_call | solution.py:45
  49.6 3.6 %all-to-all-start.1 = ((bf16[16,152,128]{2,1,0:T(8,128)(2,1)}), bf16[16,152,128]{2,1,0:T(8,128)(2,1)S(1)}, u32[]{:S(2)}, u32[]{:S(2)}) async-start(bf16[16,152,128]{2,1,0:T(8,128)(2,1)} %get-tuple-element.32), calls=%async_computation.1 | async-start | bytes 1245184 | tf_op jit(solution)/shard_map/project/all_to_all | solution.py:528
  54.4 13.1 %all-to-all-done.1.chunk_ref = bf16[16,152,128]{2,1,0:T(8,128)(2,1)S(1)} async-done(((bf16[16,152,128]{2,1,0:T(8,128)(2,1)}), bf16[16,152,128]{2,1,0:T(8,128)(2,1)S(1)}, u32[]{:S(2)}, u32[]{:S(2)}) %all-to-all-start.1) | async-done | bytes 622624 | tf_op jit(solution)/shard_map/project/all_to_all | solution.py:528
  67.6 1.3 dilated.1
  68.8 3.6 %all-to-all-start.2 = ((bf16[8,96,256]{2,1,0:T(8,128)(2,1)}), bf16[8,96,256]{2,1,0:T(8,128)(2,1)S(1)}, u32[]{:S(2)}, u32[]{:S(2)}) async-start(bf16[8,96,256]{2,1,0:T(8,128)(2,1)} %get-tuple-element.37), calls=%async_computation.2 | async-start | bytes 786432 | tf_op jit(solution)/shard_map/dilated/all_to_all | solution.py:550
  72.5 8.8 %near.3 = (bf16[144,2048]{1,0:T(8,128)(2,1)S(1)}, f32[144,2048]{1,0:T(8,128)S(1)}) custom-call(s32[1]{0:T(128)} %bitcast.phase_ref, bf16[144,2048]{1,0:T(8,128)(2,1)} %get-tuple-element.35.rows_ref, s32[8,2048]{1,0:T(8,128)S(1)} %get-tuple-element.33.local_ref, bf16[4,48,512]{2,1,0:T(8,128)(2,1)} %bitcast.25), custom_call_target="tpu_custom_call" | custom-call | flops 8000000000 | bytes 8000000 | tf_op jit(solution)/shard_map/near/pallas_call | solution.py:45
  81.3 3.0 %far.1 = (bf16[8,96,256]{2,1,0:T(8,128)(2,1)}, bf16[2,128,2048]{2,1,0:T(8,128)(2,1)}, bf16[2,128,1024]{2,1,0:T(8,128)(2,1)}) custom-call(bf16[48,256]{1,0:T(8,128)(2,1)S(1)} %get-tuple-element.34.query_ref, bf16[48,256]{1,0:T(8,128)(2,1)S(1)} %near.2.grad_ref, bf16[144,2048]{1,0:T(8,128)(2,1)S(1)} %get-tuple-element.36.place_ref, ...), custom_call_target="tpu_custom_call" | custom-call | tf_op jit(solution)/shard_map/far/pallas_call | solution.py:45
  84.3 4.5 %all-to-all-start.3 = ((bf16[8,96,256]{2,1,0:T(8,128)(2,1)}), bf16[8,96,256]{2,1,0:T(8,128)(2,1)S(1)}, u32[]{:S(2)}, u32[]{:S(2)}) async-start(bf16[8,96,256]{2,1,0:T(8,128)(2,1)} %get-tuple-element.43), calls=%async_computation.3 | async-start | bytes 786432 | tf_op jit(solution)/shard_map/far/all_to_all | solution.py:573
  88.8 2.0 %unplace.3 = (bf16[48,256]{1,0:T(8,128)(2,1)S(1)}, bf16[144,2048]{1,0:T(8,128)(2,1)S(1)}) custom-call(bf16[48,256]{1,0:T(8,128)(2,1)S(1)} %get-tuple-element.34.query_ref, bf16[48,256]{1,0:T(8,128)(2,1)S(1)} %near.2.grad_ref, bf16[144,2048]{1,0:T(8,128)(2,1)S(1)} %get-tuple-element.36.place_ref, bf16[8,96,256]{2,1,0:T(8,128)(2,1)S(1)} %all-to-all-done.2.far_ref, ...), custom_call_target="tpu_custom_call" | custom-call | tf_op jit(solution)/shard_map/unplace/pallas_call | solution.py:45
  90.8 1.5 unplace.4.main_ref
  92.3 5.5 %all-to-all-done.3.far_ref = bf16[8,96,256]{2,1,0:T(8,128)(2,1)S(1)} async-done(((bf16[8,96,256]{2,1,0:T(8,128)(2,1)}), bf16[8,96,256]{2,1,0:T(8,128)(2,1)S(1)}, u32[]{:S(2)}, u32[]{:S(2)}) %all-to-all-start.3) | async-done | bytes 393248 | tf_op jit(solution)/shard_map/far/all_to_all | solution.py:573
  97.8 1.4 unplace.5
  99.1 4.3 %all-to-all-start.4 = ((bf16[16,144,128]{2,1,0:T(8,128)(2,1)}), bf16[16,144,128]{2,1,0:T(8,128)(2,1)}, u32[]{:S(2)}, u32[]{:S(2)}) async-start(bf16[16,144,128]{2,1,0:T(8,128)(2,1)} %bitcast.5), calls=%async_computation.4 | async-start | bytes 1179648 | tf_op jit(solution)/shard_map/unplace/all_to_all | solution.py:594
  103.4 2.0 %tiles_grad.3.weight_ref = bf16[768,2304]{1,0:T(8,128)(2,1)S(1)} custom-call(bf16[144,2048]{1,0:T(8,128)(2,1)} %get-tuple-element.45._.grad_ref, bf16[768,2304]{1,0:T(8,128)(2,1)} %refs_0_.1), custom_call_target="tpu_custom_call" | custom-call | tf_op jit(solution)/shard_map/tiles_grad/pallas_call | solution.py:45
  105.4 10.3 %all-to-all-done.4 = bf16[16,144,128]{2,1,0:T(8,128)(2,1)} async-done(((bf16[16,144,128]{2,1,0:T(8,128)(2,1)}), bf16[16,144,128]{2,1,0:T(8,128)(2,1)}, u32[]{:S(2)}, u32[]{:S(2)}) %all-to-all-start.4) | async-done | bytes 589856 | tf_op jit(solution)/shard_map/unplace/all_to_all | solution.py:594
  115.7 3.9 %tiles_grad.4 = (bf16[768,128]{1,0:T(8,128)(2,1)}, bf16[1024,384]{1,0:T(8,128)(2,1)}) custom-call(bf16[2304,128]{1,0:T(8,128)(2,1)} %bitcast.6.rows_ref, bf16[768,2304]{1,0:T(8,128)(2,1)S(1)} %tiles_grad.3.weight_ref, bf16[512,128]{1,0:T(8,128)(2,1)} %get-tuple-element.46.pick_ref), custom_call_target="tpu_custom_call" | custom-call | tf_op jit(solution)/shard_map/tiles_grad/pallas_call | solution.py:45
  119.6 5.0 %all-to-all-start.5 = ((bf16[128,8,384]{2,1,0:T(8,128)(2,1)}), bf16[128,8,384]{2,1,0:T(8,128)(2,1)S(1)}, u32[]{:S(2)}, u32[]{:S(2)}) async-start(bf16[128,8,384]{2,1,0:T(8,128)(2,1)} %bitcast.21), calls=%async_computation.5 | async-start | bytes 1572864 | tf_op jit(solution)/shard_map/tiles_grad/all_to_all | solution.py:628
  127.3 2.7 %tiles_grad.5 = bf16[64,72,128]{2,1,0:T(8,128)(2,1)} custom-call(bf16[768,128]{1,0:T(8,128)(2,1)} %get-tuple-element.47.grad_ref, bf16[768,128]{1,0:T(8,128)(2,1)S(1)} %collective-permute-done.other_grad_ref, bf16[128,768]{1,0:T(8,128)(2,1)} %copy.12.keep_ref, bf16[128,768]{1,0:T(8,128)(2,1)} %copy-done.3), custom_call_target="tpu_custom_call" | custom-call | tf_op jit(solution)/shard_map/tiles_grad/pallas_call | solution.py:45
  129.9 10.8 %all-to-all-done.5 = bf16[128,8,384]{2,1,0:T(8,128)(2,1)S(1)} async-done(((bf16[128,8,384]{2,1,0:T(8,128)(2,1)}), bf16[128,8,384]{2,1,0:T(8,128)(2,1)S(1)}, u32[]{:S(2)}, u32[]{:S(2)}) %all-to-all-start.5) | async-done | bytes 786464 | tf_op jit(solution)/shard_map/tiles_grad/all_to_all | solution.py:628
  140.7 4.7 %all-to-all-start.6 = ((bf16[64,72,128]{2,1,0:T(8,128)(2,1)}), bf16[64,72,128]{2,1,0:T(8,128)(2,1)S(1)}, u32[]{:S(2)}, u32[]{:S(2)}) async-start(bf16[64,72,128]{2,1,0:T(8,128)(2,1)} %tiles_grad.5), calls=%async_computation.6 | async-start | bytes 2359296 | tf_op jit(solution)/shard_map/embed_grad/all_to_all | solution.py:645
  145.5 3.7 %qkv_grad.2 = (f32[4,96,256]{2,1,0:T(8,128)}, bf16[4,96,256]{2,1,0:T(8,128)(2,1)}) custom-call(s32[1]{0:T(128)} %bitcast.13.core_ref, bf16[144,2048]{1,0:T(8,128)(2,1)} %get-tuple-element.45._.grad_ref, bf16[2048,768]{1,0:T(8,128)(2,1)} %all-gather.2.cloned.1.call-done.rows_ref), custom_call_target="tpu_custom_call" | custom-call | tf_op jit(solution)/shard_map/qkv_grad/pallas_call | solution.py:45
  150.2 2.0 %collect.1 = bf16[384,768]{1,0:T(8,128)(2,1)} custom-call(bf16[1024,384]{1,0:T(8,128)(2,1)S(1)} %bitcast.19, s32[384,128]{1,0:T(8,128)S(1)} %dispatch.3.base_ref), custom_call_target="tpu_custom_call" | custom-call | tf_op jit(solution)/shard_map/collect/pallas_call | solution.py:45
  152.9 1.7 qkv_grad.3
  154.7 1.6 collective-permute-start.3
  156.2 2.9 %collective-permute-start.4 = (bf16[96,256]{1,0:T(8,128)(2,1)}, bf16[96,256]{1,0:T(8,128)(2,1)S(1)}, u32[]{:S(2)}, u32[]{:S(2)}) collective-permute-start(bf16[96,256]{1,0:T(8,128)(2,1)} %get-tuple-element.57), channel_id=1, source_target_pairs={{0,64},{16,80},{32,96},{48,112},{64,0},{80,16},{96,32},{112,48},{1... | collective-permute-start | bytes 147464 | tf_op jit(solution)/shard_map/qkv_grad/ppermute | solution.py:616
  159.1 1.4 collective-permute-start.5
  160.5 4.0 %convolution_convert_fusion = bf16[384,1536]{1,0:T(8,128)(2,1)} fusion(bf16[384,768]{1,0:T(8,128)(2,1)} %collect.1, bf16[1536,768]{1,0:T(8,128)(2,1)} %embed_hbm_ref.1), kind=kOutput, calls=%fused_computation | convolution fusion | flops 906559488 | bytes 4128768 | tf_op jit(solution)/shard_map/feature_grad/dot_general | solution.py:656
  164.5 1.5 all-to-all-done.6.parts_ref
  166.8 1.9 %embed_grad.1 = (f32[48,192]{1,0:T(8,128)}, f32[144,96]{1,0:T(8,128)}) custom-call(s32[1]{0:T(128)} %bitcast.12.chip_ref, bf16[64,72,128]{2,1,0:T(8,128)(2,1)S(1)} %all-to-all-done.6.parts_ref, f32[96,256]{1,0:T(8,128)} %get-tuple-element.55.own_ref, bf16[96,256]{1,0:T(8,128)(2,1)} %copy-done.4, bf16[96,256]{1,0:T(8,128)(2,1)} %copy-done.5, ...), custom_call_target="tpu_custom_call" | custom-call | tf_op jit(solution)/shard_map/embed_grad/pallas_call | solution.py:45
  (33 shorter events, 6.3 us)
Async XLA Ops:
  11.3 32.9 %all-to-all-start = ((bf16[128,8,640]{2,1,0:T(8,128)(2,1)}), bf16[128,8,640]{2,1,0:T(8,128)(2,1)S(1)}, u32[]{:S(2)}, u32[]{:S(2)}) async-start(bf16[128,8,640]{2,1,0:T(8,128)(2,1)} %bitcast.2), calls=%async_computation | async-start | bytes 2621440 | tf_op jit(solution)/shard_map/dispatch/all_to_all | solution.py:506
  22.5 123.0 %all-gather.2.cloned.1.call-start = ((), (), s32[]{:S(2)}) async-start(), calls=%async_computation.7 | async-start | bytes 3342336 | tf_op jit(solution)/shard_map/qkv_grad/all_gather | solution.py:598
  49.6 17.9 %all-to-all-start.1 = ((bf16[16,152,128]{2,1,0:T(8,128)(2,1)}), bf16[16,152,128]{2,1,0:T(8,128)(2,1)S(1)}, u32[]{:S(2)}, u32[]{:S(2)}) async-start(bf16[16,152,128]{2,1,0:T(8,128)(2,1)} %get-tuple-element.32), calls=%async_computation.1 | async-start | bytes 1245184 | tf_op jit(solution)/shard_map/project/all_to_all | solution.py:528
  68.8 12.5 %all-to-all-start.2 = ((bf16[8,96,256]{2,1,0:T(8,128)(2,1)}), bf16[8,96,256]{2,1,0:T(8,128)(2,1)S(1)}, u32[]{:S(2)}, u32[]{:S(2)}) async-start(bf16[8,96,256]{2,1,0:T(8,128)(2,1)} %get-tuple-element.37), calls=%async_computation.2 | async-start | bytes 786432 | tf_op jit(solution)/shard_map/dilated/all_to_all | solution.py:550
  84.3 13.5 %all-to-all-start.3 = ((bf16[8,96,256]{2,1,0:T(8,128)(2,1)}), bf16[8,96,256]{2,1,0:T(8,128)(2,1)S(1)}, u32[]{:S(2)}, u32[]{:S(2)}) async-start(bf16[8,96,256]{2,1,0:T(8,128)(2,1)} %get-tuple-element.43), calls=%async_computation.3 | async-start | bytes 786432 | tf_op jit(solution)/shard_map/far/all_to_all | solution.py:573
  99.1 16.6 %all-to-all-start.4 = ((bf16[16,144,128]{2,1,0:T(8,128)(2,1)}), bf16[16,144,128]{2,1,0:T(8,128)(2,1)}, u32[]{:S(2)}, u32[]{:S(2)}) async-start(bf16[16,144,128]{2,1,0:T(8,128)(2,1)} %bitcast.5), calls=%async_computation.4 | async-start | bytes 1179648 | tf_op jit(solution)/shard_map/unplace/all_to_all | solution.py:594
  119.6 5.0 %copy-start = (bf16[128,1536]{1,0:T(8,128)(2,1)S(1)}, bf16[128,1536]{1,0:T(8,128)(2,1)}, u32[]{:S(2)}) copy-start(bf16[128,1536]{1,0:T(8,128)(2,1)} %get-tuple-element.48) | copy-start | bytes 1179652
  119.6 21.1 %all-to-all-start.5 = ((bf16[128,8,384]{2,1,0:T(8,128)(2,1)}), bf16[128,8,384]{2,1,0:T(8,128)(2,1)S(1)}, u32[]{:S(2)}, u32[]{:S(2)}) async-start(bf16[128,8,384]{2,1,0:T(8,128)(2,1)} %bitcast.21), calls=%async_computation.5 | async-start | bytes 1572864 | tf_op jit(solution)/shard_map/tiles_grad/all_to_all | solution.py:628
  124.6 0.9 copy-start.2
  125.1 1.5 collective-permute-start.1
  125.5 1.4 collective-permute-start
  126.6 0.7 copy-start.3
  140.7 25.3 %all-to-all-start.6 = ((bf16[64,72,128]{2,1,0:T(8,128)(2,1)}), bf16[64,72,128]{2,1,0:T(8,128)(2,1)S(1)}, u32[]{:S(2)}, u32[]{:S(2)}) async-start(bf16[64,72,128]{2,1,0:T(8,128)(2,1)} %tiles_grad.5), calls=%async_computation.6 | async-start | bytes 2359296 | tf_op jit(solution)/shard_map/embed_grad/all_to_all | solution.py:645
  149.2 3.1 %collective-permute-start.2 = (bf16[4,96,256]{2,1,0:T(8,128)(2,1)}, bf16[4,96,256]{2,1,0:T(8,128)(2,1)S(1)}, u32[]{:S(2)}, u32[]{:S(2)}) collective-permute-start(bf16[4,96,256]{2,1,0:T(8,128)(2,1)} %get-tuple-element.54), channel_id=1, source_target_pairs={{0,16},{16,0},{32,48},{48,32},{64,80},{80,64},{96,112},{112,96},{1... | collective-permute-start | bytes 589832 | tf_op jit(solution)/shard_map/qkv_grad/ppermute | solution.py:608
  152.2 0.7 copy-start.1
  154.7 11.3 %collective-permute-start.3 = (bf16[96,256]{1,0:T(8,128)(2,1)}, bf16[96,256]{1,0:T(8,128)(2,1)S(1)}, u32[]{:S(2)}, u32[]{:S(2)}) collective-permute-start(bf16[96,256]{1,0:T(8,128)(2,1)} %get-tuple-element.56), channel_id=1, source_target_pairs={{0,32},{16,48},{32,64},{48,80},{64,96},{80,112},{96,0},{112,16},{1... | collective-permute-start | bytes 147464 | tf_op jit(solution)/shard_map/qkv_grad/ppermute | solution.py:616
  156.2 9.9 %collective-permute-start.4 = (bf16[96,256]{1,0:T(8,128)(2,1)}, bf16[96,256]{1,0:T(8,128)(2,1)S(1)}, u32[]{:S(2)}, u32[]{:S(2)}) collective-permute-start(bf16[96,256]{1,0:T(8,128)(2,1)} %get-tuple-element.57), channel_id=1, source_target_pairs={{0,64},{16,80},{32,96},{48,112},{64,0},{80,16},{96,32},{112,48},{1... | collective-permute-start | bytes 147464 | tf_op jit(solution)/shard_map/qkv_grad/ppermute | solution.py:616
  159.1 7.0 %collective-permute-start.5 = (bf16[96,256]{1,0:T(8,128)(2,1)}, bf16[96,256]{1,0:T(8,128)(2,1)S(1)}, u32[]{:S(2)}, u32[]{:S(2)}) collective-permute-start(bf16[96,256]{1,0:T(8,128)(2,1)} %get-tuple-element.58), channel_id=1, source_target_pairs={{0,96},{16,112},{32,0},{48,16},{64,32},{80,48},{96,64},{112,80},{1... | collective-permute-start | bytes 147464 | tf_op jit(solution)/shard_map/qkv_grad/ppermute | solution.py:616
  166.0 0.6 copy-start.4
  166.1 0.6 copy-start.5
  166.1 0.6 copy-start.6
Sparse Core Ops, SparseCore 0:
  49.7 45.2 all-gather.1

commit v8 on v7

--- a/solution.py
+++ b/solution.py
@@ -240,6 +240,25 @@
         far_ref[copy] = total[HEAD_SIZE:].astype(HALFS)
 
 
+def near_attend(parts, grad, dilated):
+    query = parts[:HEAD_SIZE]
+    key = parts[HEAD_SIZE : 2 * HEAD_SIZE]
+    value = parts[2 * HEAD_SIZE :]
+    score = dot(key, query, "tn") * SCALE
+    top = jnp.max(score, axis=0, keepdims=True)
+    prob = jnp.exp(score - top)
+    norm = 1.0 / jnp.sum(prob, axis=0, keepdims=True)
+    prob = prob * jnp.where(dilated, 0.0, norm)
+    dprob = dot(value, grad, "tn")
+    delta = jnp.sum(prob * dprob, axis=0, keepdims=True)
+    dscore = (prob * (dprob - delta)).astype(HALFS)
+    return (
+        dot(key, dscore) * SCALE,
+        dot(query, dscore, "nt") * SCALE,
+        dot(grad, prob.astype(HALFS), "nt"),
+    )
+
+
 def near_body(phase_ref, rows_ref, local_ref, grad_ref, place_ref, near_ref):
     seg = grad_ref.shape[2]
     local = local_ref[0:1, :]
@@ -249,21 +268,10 @@
         order = hot(local == iota((seg, local.shape[1]), 0) + slide * seg)
         parts = dot(rows_ref[...], order, "nt").astype(HALFS)
         place_ref[:, spots] = parts
-        query = parts[:HEAD_SIZE]
-        key = parts[HEAD_SIZE : 2 * HEAD_SIZE]
-        value = parts[2 * HEAD_SIZE :]
-        grad = grad_ref[slide]
-        score = dot(key, query, "tn") * SCALE
-        top = jnp.max(score, axis=0, keepdims=True)
-        prob = jnp.exp(score - top)
-        norm = 1.0 / jnp.sum(prob, axis=0, keepdims=True)
-        prob = prob * jnp.where(dilated, 0.0, norm)
-        dprob = dot(value, grad, "tn")
-        delta = jnp.sum(prob * dprob, axis=0, keepdims=True)
-        dscore = (prob * (dprob - delta)).astype(HALFS)
-        near_ref[:HEAD_SIZE, spots] = dot(key, dscore) * SCALE
-        near_ref[HEAD_SIZE : 2 * HEAD_SIZE, spots] = dot(query, dscore, "nt") * SCALE
-        near_ref[2 * HEAD_SIZE :, spots] = dot(grad, prob.astype(HALFS), "nt")
+        if slide * seg < near_ref.shape[1]:
+            grads = near_attend(parts, grad_ref[slide], dilated)
+            for k in range(3):
+                near_ref[k * HEAD_SIZE : (k + 1) * HEAD_SIZE, spots] = grads[k]
 
 
 def pick_body(phase_ref, grad_ref, out_ref):
@@ -318,6 +326,8 @@
 
 
 def sum_body(
+    phase_ref,
+    all_grad_ref,
     query_ref,
     grad_ref,
     place_ref,
@@ -329,14 +339,14 @@
     sum_ref,
 ):
     near = place_ref.shape[1] // 2
-    sum_ref[:HEAD_SIZE, :] = near_ref[:HEAD_SIZE, :].astype(HALFS)
+    seg = near // 2
+    dilated = (iota((1, seg), 1) & 7) == phase_ref[0]
     for pair in range(2):
         lanes = slice(pair * 128, (pair + 1) * 128)
-        spots = slice(pair * near, (pair + 1) * near)
         query = query_ref[:, lanes]
         grad = grad_ref[:, lanes]
         key = jnp.concatenate(
-            [place_ref[HEAD_SIZE : 2 * HEAD_SIZE, spots]]
+            [place_ref[HEAD_SIZE : 2 * HEAD_SIZE, pair * near : (pair + 1) * near]]
             + [far_ref[k, :HEAD_SIZE, lanes] for k in range(far_ref.shape[0])],
             axis=1,
         )
@@ -344,10 +354,17 @@
         dquery_ref[:, lanes] = (dot(key, dscore, "nt") * SCALE).astype(HALFS)
         dkey = dot(query, dscore[:, :near]) * SCALE
         dvalue = dot(grad, prob_ref[pair])
-        middle = slice(HEAD_SIZE, 2 * HEAD_SIZE)
-        sum_ref[middle, spots] = (near_ref[middle, spots] + dkey).astype(HALFS)
-        last = slice(2 * HEAD_SIZE, WIDTH)
-        sum_ref[last, spots] = (near_ref[last, spots] + dvalue).astype(HALFS)
+        for b in range(2):
+            slide = 2 * pair + b
+            spots = slice(slide * seg, (slide + 1) * seg)
+            part = slice(b * seg, (b + 1) * seg)
+            if pair == 0:
+                grads = [near_ref[k * HEAD_SIZE : (k + 1) * HEAD_SIZE, spots] for k in range(3)]
+            else:
+                grads = near_attend(place_ref[:, spots], all_grad_ref[slide], dilated)
+            sum_ref[:HEAD_SIZE, spots] = grads[0].astype(HALFS)
+            sum_ref[HEAD_SIZE : 2 * HEAD_SIZE, spots] = (grads[1] + dkey[:, part]).astype(HALFS)
+            sum_ref[2 * HEAD_SIZE :, spots] = (grads[2] + dvalue[:, part]).astype(HALFS)
 
 
 def unplace_body(local_ref, sum_ref, out_ref):
@@ -553,7 +570,7 @@
         dilated_grads = call(pick_body, resident((HEAD_SIZE, few)), [phase, grads], smem=(0,))
         placed, near = call(
             near_body,
-            [resident((WIDTH, rows)), resident((WIDTH, rows), FLOATS)],
+            [resident((WIDTH, rows)), resident((WIDTH, rows // 2), FLOATS)],
             [phase, head_rows, *stay(local), grads],
             smem=(0,),
             cost_estimate=pl.CostEstimate(
@@ -575,7 +592,15 @@
         dquery, summed = call(
             sum_body,
             [resident((HEAD_SIZE, few)), resident((WIDTH, rows))],
-            [*stay(query, dilated_grads, placed, far), dscores, probs, *stay(near)],
+            [
+                phase,
+                grads,
+                *stay(query, dilated_grads, placed, far),
+                dscores,
+                probs,
+                *stay(near),
+            ],
+            smem=(0,),
         )
         main = call(
             unplace_body,

time: 178 us -> 176 us (0.989)
    all_to_all x1, waiting for transfers between devices: 0.01 us -> 2.31 us  [per_device(): far = lax.all_to_all(far, 'slide', 0, 0, tiled=True)]
    all_to_all x1, waiting for transfers between devices: 5.47 us -> 3.18 us  [per_device(): far_grads = lax.all_to_all(far_grads, 'slide', 0, 0, tiled=True)]
  transfers between devices with their start and end apart: 14 -> 14, of which waited for: 9 -> 10; matrix products, arithmetic and copies ran while one was open for 3% -> 4% of each run, Pallas kernels for 21% -> 21%
where the time goes in v8:
time: 176 us; the launch traced here: 174 us
  waiting for transfers between devices  62.7 us (36%)
  Pallas kernels  47.4 us (27%)
  starting transfers between devices  42 us (24%)
  between operations  14.3 us (8%)
  matrix products  3.99 us (2%)
  local copies, waits for them, and re-layouts  3.92 us (2%)
    pallas_call x17, Pallas kernels, call(): pl.pallas_call(body, out_shape=outs, in_specs=specs, out_specs=out_specs,...  47.4 us
    all_to_all x1, waiting for transfers between devices, per_device(): lax.all_to_all(sent.reshape(devices, 8, packed), every, 0, 0, tiled=True)  21.7 us
    all_to_all x1, waiting for transfers between devices, per_device(): chunks = lax.all_to_all(chunks, 'tile', 0, 0, tiled=True)  13 us
    all_to_all x1, starting transfers between devices, per_device(): lax.all_to_all(sent.reshape(devices, 8, packed), every, 0, 0, tiled=True)  11.1 us
    all_to_all x1, waiting for transfers between devices, per_device(): lax.all_to_all(back_chunks.reshape(n_tile, WIDTH, 128), 'tile', 0, 0, til...  10.3 us
    all_to_all x1, waiting for transfers between devices, per_device(): lax.all_to_all(back.reshape(devices, 8, half), every, 0, 0, tiled=True)  10 us
    ppermute x3, starting transfers between devices, per_device(): lax.ppermute(pieces[k - 1], 'slide', [(i, (i + 2 * k) % n_slide) for i in...  5.8 us
    all_to_all x1, starting transfers between devices, per_device(): lax.all_to_all(back.reshape(devices, 8, half), every, 0, 0, tiled=True)  4.76 us
  transfers between devices with their start and end apart: 14, of which 10 were waited for; matrix products, arithmetic and copies ran while one was open for 4% of the time, Pallas kernels for 21%

profile of v8, /device:TPU:0, one launch (start us, length us, event | category | flops | bytes accessed | tf_op | source)
XLA Modules:
  0.0 174.2 jit_solution(10716926692452415505)
XLA Ops:
  7.2 4.2 %dispatch.2 = bf16[1024,640]{1,0:T(8,128)(2,1)} custom-call(s32[384]{0:T(512)} %pos_ref.3, bf16[384,1536]{1,0:T(8,128)(2,1)} %rest_ref.1, bf16[384,1536]{1,0:T(8,128)(2,1)} %rest_ref.1, bf16[384,1536]{1,0:T(8,128)(2,1)} %rest_ref.1), custom_call_target="tpu_custom_call" | custom-call | tf_op jit(solution)/shard_map/dispatch/pallas_call | solution.py:45
  11.4 11.1 %all-to-all-start = ((bf16[128,8,640]{2,1,0:T(8,128)(2,1)}), bf16[128,8,640]{2,1,0:T(8,128)(2,1)S(1)}, u32[]{:S(2)}, u32[]{:S(2)}) async-start(bf16[128,8,640]{2,1,0:T(8,128)(2,1)} %bitcast.2), calls=%async_computation | async-start | bytes 2621440 | tf_op jit(solution)/shard_map/dispatch/all_to_all | solution.py:523
  22.6 21.7 %all-to-all-done = bf16[128,8,640]{2,1,0:T(8,128)(2,1)S(1)} async-done(((bf16[128,8,640]{2,1,0:T(8,128)(2,1)}), bf16[128,8,640]{2,1,0:T(8,128)(2,1)S(1)}, u32[]{:S(2)}, u32[]{:S(2)}) %all-to-all-start) | async-done | bytes 1310752 | tf_op jit(solution)/shard_map/dispatch/all_to_all | solution.py:523
  44.3 5.3 %project.1 = (bf16[128,768]{1,0:T(8,128)(2,1)}, bf16[128,1536]{1,0:T(8,128)(2,1)}, bf16[16,152,128]{2,1,0:T(8,128)(2,1)}, bf16[512,128]{1,0:T(8,128)(2,1)}) custom-call(s32[1]{0:T(128)} %bitcast.1.odd_ref, bf16[1024,640]{1,0:T(8,128)(2,1)S(1)} %bitcast.18, bf16[1536,768]{1,0:T(8,128)(2,1)} %embed_hbm_ref.1, bf16[768,2304]{1,0:T(8,128)(2,1)} %refs_0_.1), custom_call_target="tpu_custom_call" | custom-call | tf_op jit(solution)/shard_map/project/pallas_call | solution.py:45
  49.6 3.6 %all-to-all-start.1 = ((bf16[16,152,128]{2,1,0:T(8,128)(2,1)}), bf16[16,152,128]{2,1,0:T(8,128)(2,1)S(1)}, u32[]{:S(2)}, u32[]{:S(2)}) async-start(bf16[16,152,128]{2,1,0:T(8,128)(2,1)} %get-tuple-element.32), calls=%async_computation.1 | async-start | bytes 1245184 | tf_op jit(solution)/shard_map/project/all_to_all | solution.py:545
  54.4 13.0 %all-to-all-done.1.chunk_ref = bf16[16,152,128]{2,1,0:T(8,128)(2,1)S(1)} async-done(((bf16[16,152,128]{2,1,0:T(8,128)(2,1)}), bf16[16,152,128]{2,1,0:T(8,128)(2,1)S(1)}, u32[]{:S(2)}, u32[]{:S(2)}) %all-to-all-start.1) | async-done | bytes 622624 | tf_op jit(solution)/shard_map/project/all_to_all | solution.py:545
  68.7 3.5 %all-to-all-start.2 = ((bf16[8,96,256]{2,1,0:T(8,128)(2,1)}), bf16[8,96,256]{2,1,0:T(8,128)(2,1)S(1)}, u32[]{:S(2)}, u32[]{:S(2)}) async-start(bf16[8,96,256]{2,1,0:T(8,128)(2,1)} %get-tuple-element.37), calls=%async_computation.2 | async-start | bytes 786432 | tf_op jit(solution)/shard_map/dilated/all_to_all | solution.py:567
  72.2 6.5 %near.3 = (bf16[144,2048]{1,0:T(8,128)(2,1)S(1)}, f32[144,1024]{1,0:T(8,128)S(1)}) custom-call(s32[1]{0:T(128)} %bitcast.phase_ref, bf16[144,2048]{1,0:T(8,128)(2,1)} %get-tuple-element.35.rows_ref, s32[8,2048]{1,0:T(8,128)S(1)} %get-tuple-element.33.local_ref, bf16[4,48,512]{2,1,0:T(8,128)(2,1)} %bitcast.22), custom_call_target="tpu_custom_call" | custom-call | flops 8000000000 | bytes 8000000 | tf_op jit(solution)/shard_map/near/pallas_call | solution.py:45
  78.8 2.3 %all-to-all-done.2.far_ref = bf16[8,96,256]{2,1,0:T(8,128)(2,1)S(1)} async-done(((bf16[8,96,256]{2,1,0:T(8,128)(2,1)}), bf16[8,96,256]{2,1,0:T(8,128)(2,1)S(1)}, u32[]{:S(2)}, u32[]{:S(2)}) %all-to-all-start.2) | async-done | bytes 393248 | tf_op jit(solution)/shard_map/dilated/all_to_all | solution.py:567
  81.1 2.9 %far.1 = (bf16[8,96,256]{2,1,0:T(8,128)(2,1)}, bf16[2,128,2048]{2,1,0:T(8,128)(2,1)}, bf16[2,128,1024]{2,1,0:T(8,128)(2,1)}) custom-call(bf16[48,256]{1,0:T(8,128)(2,1)S(1)} %get-tuple-element.34.query_ref, bf16[48,256]{1,0:T(8,128)(2,1)S(1)} %near.2.grad_ref, bf16[144,2048]{1,0:T(8,128)(2,1)S(1)} %get-tuple-element.36.place_ref, ...), custom_call_target="tpu_custom_call" | custom-call | tf_op jit(solution)/shard_map/far/pallas_call | solution.py:45
  84.0 3.6 %all-to-all-start.3 = ((bf16[8,96,256]{2,1,0:T(8,128)(2,1)}), bf16[8,96,256]{2,1,0:T(8,128)(2,1)S(1)}, u32[]{:S(2)}, u32[]{:S(2)}) async-start(bf16[8,96,256]{2,1,0:T(8,128)(2,1)} %get-tuple-element.43), calls=%async_computation.3 | async-start | bytes 786432 | tf_op jit(solution)/shard_map/far/all_to_all | solution.py:590
  87.7 4.2 %unplace.3 = (bf16[48,256]{1,0:T(8,128)(2,1)S(1)}, bf16[144,2048]{1,0:T(8,128)(2,1)S(1)}) custom-call(s32[1]{0:T(128)} %bitcast.phase_ref, bf16[4,48,512]{2,1,0:T(8,128)(2,1)} %bitcast.23, bf16[48,256]{1,0:T(8,128)(2,1)S(1)} %get-tuple-element.34.query_ref, bf16[48,256]{1,0:T(8,128)(2,1)S(1)} %near.2.grad_ref, ...), custom_call_target="tpu_custom_call" | custom-call | tf_op jit(solution)/shard_map/unplace/pallas_call | solution.py:45
  91.8 1.5 unplace.4.main_ref
  93.3 3.2 %all-to-all-done.3.far_ref = bf16[8,96,256]{2,1,0:T(8,128)(2,1)S(1)} async-done(((bf16[8,96,256]{2,1,0:T(8,128)(2,1)}), bf16[8,96,256]{2,1,0:T(8,128)(2,1)S(1)}, u32[]{:S(2)}, u32[]{:S(2)}) %all-to-all-start.3) | async-done | bytes 393248 | tf_op jit(solution)/shard_map/far/all_to_all | solution.py:590
  96.5 1.4 unplace.5
  97.9 4.3 %all-to-all-start.4 = ((bf16[16,144,128]{2,1,0:T(8,128)(2,1)}), bf16[16,144,128]{2,1,0:T(8,128)(2,1)}, u32[]{:S(2)}, u32[]{:S(2)}) async-start(bf16[16,144,128]{2,1,0:T(8,128)(2,1)} %bitcast.5), calls=%async_computation.4 | async-start | bytes 1179648 | tf_op jit(solution)/shard_map/unplace/all_to_all | solution.py:619
  102.1 2.0 %tiles_grad.3.weight_ref = bf16[768,2304]{1,0:T(8,128)(2,1)S(1)} custom-call(bf16[144,2048]{1,0:T(8,128)(2,1)} %get-tuple-element.45._.grad_ref, bf16[768,2304]{1,0:T(8,128)(2,1)} %refs_0_.1), custom_call_target="tpu_custom_call" | custom-call | tf_op jit(solution)/shard_map/tiles_grad/pallas_call | solution.py:45
  104.2 10.3 %all-to-all-done.4 = bf16[16,144,128]{2,1,0:T(8,128)(2,1)} async-done(((bf16[16,144,128]{2,1,0:T(8,128)(2,1)}), bf16[16,144,128]{2,1,0:T(8,128)(2,1)}, u32[]{:S(2)}, u32[]{:S(2)}) %all-to-all-start.4) | async-done | bytes 589856 | tf_op jit(solution)/shard_map/unplace/all_to_all | solution.py:619
  114.5 3.9 %tiles_grad.4 = (bf16[768,128]{1,0:T(8,128)(2,1)}, bf16[1024,384]{1,0:T(8,128)(2,1)}) custom-call(bf16[2304,128]{1,0:T(8,128)(2,1)} %bitcast.6.rows_ref, bf16[768,2304]{1,0:T(8,128)(2,1)S(1)} %tiles_grad.3.weight_ref, bf16[512,128]{1,0:T(8,128)(2,1)} %get-tuple-element.46.pick_ref), custom_call_target="tpu_custom_call" | custom-call | tf_op jit(solution)/shard_map/tiles_grad/pallas_call | solution.py:45
  118.4 4.8 %all-to-all-start.5 = ((bf16[128,8,384]{2,1,0:T(8,128)(2,1)}), bf16[128,8,384]{2,1,0:T(8,128)(2,1)S(1)}, u32[]{:S(2)}, u32[]{:S(2)}) async-start(bf16[128,8,384]{2,1,0:T(8,128)(2,1)} %bitcast.24), calls=%async_computation.5 | async-start | bytes 1572864 | tf_op jit(solution)/shard_map/tiles_grad/all_to_all | solution.py:653
  126.7 2.7 %tiles_grad.5 = bf16[64,72,128]{2,1,0:T(8,128)(2,1)} custom-call(bf16[768,128]{1,0:T(8,128)(2,1)} %get-tuple-element.47.grad_ref, bf16[768,128]{1,0:T(8,128)(2,1)S(1)} %collective-permute-done.other_grad_ref, bf16[128,768]{1,0:T(8,128)(2,1)} %copy.12.keep_ref, bf16[128,768]{1,0:T(8,128)(2,1)} %copy-done.2), custom_call_target="tpu_custom_call" | custom-call | tf_op jit(solution)/shard_map/tiles_grad/pallas_call | solution.py:45
  129.4 10.0 %all-to-all-done.5 = bf16[128,8,384]{2,1,0:T(8,128)(2,1)S(1)} async-done(((bf16[128,8,384]{2,1,0:T(8,128)(2,1)}), bf16[128,8,384]{2,1,0:T(8,128)(2,1)S(1)}, u32[]{:S(2)}, u32[]{:S(2)}) %all-to-all-start.5) | async-done | bytes 786464 | tf_op jit(solution)/shard_map/tiles_grad/all_to_all | solution.py:653
  139.4 4.7 %all-to-all-start.6 = ((bf16[64,72,128]{2,1,0:T(8,128)(2,1)}), bf16[64,72,128]{2,1,0:T(8,128)(2,1)S(1)}, u32[]{:S(2)}, u32[]{:S(2)}) async-start(bf16[64,72,128]{2,1,0:T(8,128)(2,1)} %tiles_grad.5), calls=%async_computation.6 | async-start | bytes 2359296 | tf_op jit(solution)/shard_map/embed_grad/all_to_all | solution.py:670
  144.2 3.7 %qkv_grad.2 = (f32[4,96,256]{2,1,0:T(8,128)}, bf16[4,96,256]{2,1,0:T(8,128)(2,1)}) custom-call(s32[1]{0:T(128)} %bitcast.13.core_ref, bf16[144,2048]{1,0:T(8,128)(2,1)} %get-tuple-element.45._.grad_ref, bf16[2048,768]{1,0:T(8,128)(2,1)} %all-gather.2.cloned.1.call-done.rows_ref), custom_call_target="tpu_custom_call" | custom-call | tf_op jit(solution)/shard_map/qkv_grad/pallas_call | solution.py:45
  149.0 2.0 %collect.1 = bf16[384,768]{1,0:T(8,128)(2,1)} custom-call(bf16[1024,384]{1,0:T(8,128)(2,1)S(1)} %bitcast.19, s32[384,128]{1,0:T(8,128)S(1)} %dispatch.3.base_ref), custom_call_target="tpu_custom_call" | custom-call | tf_op jit(solution)/shard_map/collect/pallas_call | solution.py:45
  151.6 1.8 %qkv_grad.3 = (f32[96,256]{1,0:T(8,128)}, bf16[96,256]{1,0:T(8,128)(2,1)}, bf16[96,256]{1,0:T(8,128)(2,1)}, bf16[96,256]{1,0:T(8,128)(2,1)}) custom-call(s32[1]{0:T(128)} %bitcast.12.chip_ref, f32[4,96,256]{2,1,0:T(8,128)} %get-tuple-element.53.keep_ref, bf16[4,96,256]{2,1,0:T(8,128)(2,1)} %copy-done), custom_call_target="tpu_custom_call" | custom-call | tf_op jit(solution)/shard_map/qkv_grad/pallas_call | solution.py:45
  153.4 1.6 collective-permute-start.3
  155.0 2.9 %collective-permute-start.4 = (bf16[96,256]{1,0:T(8,128)(2,1)}, bf16[96,256]{1,0:T(8,128)(2,1)S(1)}, u32[]{:S(2)}, u32[]{:S(2)}) collective-permute-start(bf16[96,256]{1,0:T(8,128)(2,1)} %get-tuple-element.57), channel_id=1, source_target_pairs={{0,64},{16,80},{32,96},{48,112},{64,0},{80,16},{96,32},{112,48},{1... | collective-permute-start | bytes 147464 | tf_op jit(solution)/shard_map/qkv_grad/ppermute | solution.py:641
  157.8 1.3 collective-permute-start.5
  159.2 4.0 %convolution_convert_fusion = bf16[384,1536]{1,0:T(8,128)(2,1)} fusion(bf16[384,768]{1,0:T(8,128)(2,1)} %collect.1, bf16[1536,768]{1,0:T(8,128)(2,1)} %embed_hbm_ref.1), kind=kOutput, calls=%fused_computation | convolution fusion | flops 906559488 | bytes 4128768 | tf_op jit(solution)/shard_map/feature_grad/dot_general | solution.py:681
  163.2 1.5 all-to-all-done.6.parts_ref
  165.5 1.9 %embed_grad.1 = (f32[48,192]{1,0:T(8,128)}, f32[144,96]{1,0:T(8,128)}) custom-call(s32[1]{0:T(128)} %bitcast.12.chip_ref, bf16[64,72,128]{2,1,0:T(8,128)(2,1)S(1)} %all-to-all-done.6.parts_ref, f32[96,256]{1,0:T(8,128)} %get-tuple-element.55.own_ref, bf16[96,256]{1,0:T(8,128)(2,1)} %copy-done.3, bf16[96,256]{1,0:T(8,128)(2,1)} %copy-done.4, ...), custom_call_target="tpu_custom_call" | custom-call | tf_op jit(solution)/shard_map/embed_grad/pallas_call | solution.py:45
  (31 shorter events, 8.6 us)
Async XLA Ops:
  11.4 32.9 %all-to-all-start = ((bf16[128,8,640]{2,1,0:T(8,128)(2,1)}), bf16[128,8,640]{2,1,0:T(8,128)(2,1)S(1)}, u32[]{:S(2)}, u32[]{:S(2)}) async-start(bf16[128,8,640]{2,1,0:T(8,128)(2,1)} %bitcast.2), calls=%async_computation | async-start | bytes 2621440 | tf_op jit(solution)/shard_map/dispatch/all_to_all | solution.py:523
  22.5 121.7 %all-gather.2.cloned.1.call-start = ((), (), s32[]{:S(2)}) async-start(), calls=%async_computation.7 | async-start | bytes 3342336 | tf_op jit(solution)/shard_map/qkv_grad/all_gather | solution.py:623
  49.6 17.8 %all-to-all-start.1 = ((bf16[16,152,128]{2,1,0:T(8,128)(2,1)}), bf16[16,152,128]{2,1,0:T(8,128)(2,1)S(1)}, u32[]{:S(2)}, u32[]{:S(2)}) async-start(bf16[16,152,128]{2,1,0:T(8,128)(2,1)} %get-tuple-element.32), calls=%async_computation.1 | async-start | bytes 1245184 | tf_op jit(solution)/shard_map/project/all_to_all | solution.py:545
  68.7 12.3 %all-to-all-start.2 = ((bf16[8,96,256]{2,1,0:T(8,128)(2,1)}), bf16[8,96,256]{2,1,0:T(8,128)(2,1)S(1)}, u32[]{:S(2)}, u32[]{:S(2)}) async-start(bf16[8,96,256]{2,1,0:T(8,128)(2,1)} %get-tuple-element.37), calls=%async_computation.2 | async-start | bytes 786432 | tf_op jit(solution)/shard_map/dilated/all_to_all | solution.py:567
  84.0 12.5 %all-to-all-start.3 = ((bf16[8,96,256]{2,1,0:T(8,128)(2,1)}), bf16[8,96,256]{2,1,0:T(8,128)(2,1)S(1)}, u32[]{:S(2)}, u32[]{:S(2)}) async-start(bf16[8,96,256]{2,1,0:T(8,128)(2,1)} %get-tuple-element.43), calls=%async_computation.3 | async-start | bytes 786432 | tf_op jit(solution)/shard_map/far/all_to_all | solution.py:590
  97.9 16.6 %all-to-all-start.4 = ((bf16[16,144,128]{2,1,0:T(8,128)(2,1)}), bf16[16,144,128]{2,1,0:T(8,128)(2,1)}, u32[]{:S(2)}, u32[]{:S(2)}) async-start(bf16[16,144,128]{2,1,0:T(8,128)(2,1)} %bitcast.5), calls=%async_computation.4 | async-start | bytes 1179648 | tf_op jit(solution)/shard_map/unplace/all_to_all | solution.py:619
  118.3 6.3 %copy-start.1 = (bf16[768,128]{1,0:T(8,128)(2,1)S(1)}, bf16[768,128]{1,0:T(8,128)(2,1)}, u32[]{:S(2)}) copy-start(bf16[768,128]{1,0:T(8,128)(2,1)} %get-tuple-element.47.grad_ref) | copy-start | bytes 589828
  118.4 21.1 %all-to-all-start.5 = ((bf16[128,8,384]{2,1,0:T(8,128)(2,1)}), bf16[128,8,384]{2,1,0:T(8,128)(2,1)S(1)}, u32[]{:S(2)}, u32[]{:S(2)}) async-start(bf16[128,8,384]{2,1,0:T(8,128)(2,1)} %bitcast.24), calls=%async_computation.5 | async-start | bytes 1572864 | tf_op jit(solution)/shard_map/tiles_grad/all_to_all | solution.py:653
  124.6 1.5 collective-permute-start.1
  124.7 1.7 collective-permute-start
  126.1 0.7 copy-start.2
  139.4 25.3 %all-to-all-start.6 = ((bf16[64,72,128]{2,1,0:T(8,128)(2,1)}), bf16[64,72,128]{2,1,0:T(8,128)(2,1)S(1)}, u32[]{:S(2)}, u32[]{:S(2)}) async-start(bf16[64,72,128]{2,1,0:T(8,128)(2,1)} %tiles_grad.5), calls=%async_computation.6 | async-start | bytes 2359296 | tf_op jit(solution)/shard_map/embed_grad/all_to_all | solution.py:670
  147.9 3.0 %collective-permute-start.2 = (bf16[4,96,256]{2,1,0:T(8,128)(2,1)}, bf16[4,96,256]{2,1,0:T(8,128)(2,1)S(1)}, u32[]{:S(2)}, u32[]{:S(2)}) collective-permute-start(bf16[4,96,256]{2,1,0:T(8,128)(2,1)} %get-tuple-element.54), channel_id=1, source_target_pairs={{0,16},{16,0},{32,48},{48,32},{64,80},{80,64},{96,112},{112,96},{1... | collective-permute-start | bytes 589832 | tf_op jit(solution)/shard_map/qkv_grad/ppermute | solution.py:633
  151.0 0.7 copy-start
  153.4 11.3 %collective-permute-start.3 = (bf16[96,256]{1,0:T(8,128)(2,1)}, bf16[96,256]{1,0:T(8,128)(2,1)S(1)}, u32[]{:S(2)}, u32[]{:S(2)}) collective-permute-start(bf16[96,256]{1,0:T(8,128)(2,1)} %get-tuple-element.56), channel_id=1, source_target_pairs={{0,32},{16,48},{32,64},{48,80},{64,96},{80,112},{96,0},{112,16},{1... | collective-permute-start | bytes 147464 | tf_op jit(solution)/shard_map/qkv_grad/ppermute | solution.py:641
  155.0 9.9 %collective-permute-start.4 = (bf16[96,256]{1,0:T(8,128)(2,1)}, bf16[96,256]{1,0:T(8,128)(2,1)S(1)}, u32[]{:S(2)}, u32[]{:S(2)}) collective-permute-start(bf16[96,256]{1,0:T(8,128)(2,1)} %get-tuple-element.57), channel_id=1, source_target_pairs={{0,64},{16,80},{32,96},{48,112},{64,0},{80,16},{96,32},{112,48},{1... | collective-permute-start | bytes 147464 | tf_op jit(solution)/shard_map/qkv_grad/ppermute | solution.py:641
  157.8 7.0 %collective-permute-start.5 = (bf16[96,256]{1,0:T(8,128)(2,1)}, bf16[96,256]{1,0:T(8,128)(2,1)S(1)}, u32[]{:S(2)}, u32[]{:S(2)}) collective-permute-start(bf16[96,256]{1,0:T(8,128)(2,1)} %get-tuple-element.58), channel_id=1, source_target_pairs={{0,96},{16,112},{32,0},{48,16},{64,32},{80,48},{96,64},{112,80},{1... | collective-permute-start | bytes 147464 | tf_op jit(solution)/shard_map/qkv_grad/ppermute | solution.py:641
  164.7 0.6 copy-start.3
  164.9 0.6 copy-start.4
  164.9 0.6 copy-start.5
Sparse Core Ops, SparseCore 0:
  49.8 45.3 all-gather.1

commit v9 on v8

--- a/solution.py
+++ b/solution.py
@@ -259,7 +259,18 @@
     )
 
 
-def near_body(phase_ref, rows_ref, local_ref, grad_ref, place_ref, near_ref):
+def near_body(
+    phase_ref,
+    rows_ref,
+    local_ref,
+    grad_ref,
+    query_ref,
+    dilated_grad_ref,
+    place_ref,
+    near_ref,
+    score_ref,
+    dprob_ref,
+):
     seg = grad_ref.shape[2]
     local = local_ref[0:1, :]
     dilated = (iota((1, seg), 1) & 7) == phase_ref[0]
@@ -272,6 +283,14 @@
             grads = near_attend(parts, grad_ref[slide], dilated)
             for k in range(3):
                 near_ref[k * HEAD_SIZE : (k + 1) * HEAD_SIZE, spots] = grads[k]
+        pair, b = slide // 2, slide % 2
+        lanes = slice(pair * 128, (pair + 1) * 128)
+        part = slice(b * seg, (b + 1) * seg)
+        same = iota((128, seg), 0) >> 6 == b
+        key, value = parts[HEAD_SIZE : 2 * HEAD_SIZE], parts[2 * HEAD_SIZE :]
+        score = dot(query_ref[:, lanes], key, "tn") * SCALE
+        score_ref[pair, :, part] = jnp.where(same, score, -1e30)
+        dprob_ref[pair, :, part] = dot(dilated_grad_ref[:, lanes], value, "tn")
 
 
 def pick_body(phase_ref, grad_ref, out_ref):
@@ -284,34 +303,25 @@
         out_ref[:, pair * 128 : (pair + 1) * 128] = grad.astype(HALFS)
 
 
-def far_body(query_ref, grad_ref, place_ref, far_ref, out_ref, dscore_ref, prob_ref):
+def far_body(
+    query_ref, grad_ref, score_ref, dprob_ref, far_ref, out_ref, dscore_ref, prob_ref
+):
     n = far_ref.shape[0]
-    near = place_ref.shape[1] // 2
-    seg = near // 2
+    near = score_ref.shape[2]
     for pair in range(2):
         lanes = slice(pair * 128, (pair + 1) * 128)
-        spots = slice(pair * near, (pair + 1) * near)
         query = query_ref[:, lanes]
         grad = grad_ref[:, lanes]
-        key = jnp.concatenate(
-            [place_ref[HEAD_SIZE : 2 * HEAD_SIZE, spots]]
-            + [far_ref[k, :HEAD_SIZE, lanes] for k in range(n)],
-            axis=1,
-        )
-        value = jnp.concatenate(
-            [place_ref[2 * HEAD_SIZE :, spots]]
-            + [far_ref[k, HEAD_SIZE:, lanes] for k in range(n)],
-            axis=1,
-        )
+        key = jnp.concatenate([far_ref[k, :HEAD_SIZE, lanes] for k in range(n)], axis=1)
+        value = jnp.concatenate([far_ref[k, HEAD_SIZE:, lanes] for k in range(n)], axis=1)
         size = key.shape[1]
-        column = iota((128, size), 1)
-        slide_of_key = jnp.where(column < near, column // seg, (column & 127) >> 6)
-        same = slide_of_key == iota((128, size), 0) >> 6
+        same = (iota((128, size), 1) & 127) >> 6 == iota((128, size), 0) >> 6
         score = jnp.where(same, dot(query, key, "tn") * SCALE, -1e30)
+        score = jnp.concatenate([score_ref[pair], score], axis=1)
         top = jnp.max(score, axis=1, keepdims=True)
         prob = jnp.exp(score - top)
         prob = prob * (1.0 / jnp.sum(prob, axis=1, keepdims=True))
-        dprob = dot(grad, value, "tn")
+        dprob = jnp.concatenate([dprob_ref[pair], dot(grad, value, "tn")], axis=1)
         delta = jnp.sum(prob * dprob, axis=1, keepdims=True)
         dscore = (prob * (dprob - delta)).astype(HALFS)
         prob = prob.astype(HALFS)
@@ -568,10 +578,11 @@
     with jax.named_scope("near"):
         grads = out_grad.transpose(0, 2, 1)
         dilated_grads = call(pick_body, resident((HEAD_SIZE, few)), [phase, grads], smem=(0,))
-        placed, near = call(
+        placed, near, near_scores, near_dprobs = call(
             near_body,
-            [resident((WIDTH, rows)), resident((WIDTH, rows // 2), FLOATS)],
-            [phase, head_rows, *stay(local), grads],
+            [resident((WIDTH, rows)), shaped((WIDTH, rows // 2), FLOATS)]
+            + [resident((2, 128, rows // 2), FLOATS)] * 2,
+            [phase, head_rows, *stay(local), grads, *stay(query, dilated_grads)],
             smem=(0,),
             cost_estimate=pl.CostEstimate(
                 flops=8_000_000_000, bytes_accessed=8_000_000, transcendentals=1 << 20
@@ -585,7 +596,7 @@
                 shaped((2, 128, rows)),
                 shaped((2, 128, rows // 2)),
             ],
-            stay(query, dilated_grads, placed, far),
+            stay(query, dilated_grads, near_scores, near_dprobs, far),
         )
         far_grads = lax.all_to_all(far_grads, "slide", 0, 0, tiled=True)
     with jax.named_scope("unplace"):
@@ -598,7 +609,7 @@
                 *stay(query, dilated_grads, placed, far),
                 dscores,
                 probs,
-                *stay(near),
+                near,
             ],
             smem=(0,),
         )

time: 176 us -> 176 us (level)
  no operation moved by 1% of the time
where the time goes in v9:
time: 176 us; the launch traced here: 174 us
  waiting for transfers between devices  61.6 us (35%)
  Pallas kernels  47.9 us (27%)
  starting transfers between devices  42.2 us (24%)
  between operations  14.3 us (8%)
  matrix products  3.98 us (2%)
  local copies, waits for them, and re-layouts  3.92 us (2%)
    pallas_call x17, Pallas kernels, call(): pl.pallas_call(body, out_shape=outs, in_specs=specs, out_specs=out_specs,...  47.9 us
    all_to_all x1, waiting for transfers between devices, per_device(): lax.all_to_all(sent.reshape(devices, 8, packed), every, 0, 0, tiled=True)  21.7 us
    all_to_all x1, waiting for transfers between devices, per_device(): chunks = lax.all_to_all(chunks, 'tile', 0, 0, tiled=True)  13 us
    all_to_all x1, starting transfers between devices, per_device(): lax.all_to_all(sent.reshape(devices, 8, packed), every, 0, 0, tiled=True)  11.1 us
    all_to_all x1, waiting for transfers between devices, per_device(): lax.all_to_all(back_chunks.reshape(n_tile, WIDTH, 128), 'tile', 0, 0, til...  10.3 us
    all_to_all x1, waiting for transfers between devices, per_device(): lax.all_to_all(back.reshape(devices, 8, half), every, 0, 0, tiled=True)  9.78 us
    ppermute x3, starting transfers between devices, per_device(): lax.ppermute(pieces[k - 1], 'slide', [(i, (i + 2 * k) % n_slide) for i in...  5.8 us
    all_to_all x1, starting transfers between devices, per_device(): lax.all_to_all(back.reshape(devices, 8, half), every, 0, 0, tiled=True)  4.98 us
  transfers between devices with their start and end apart: 14, of which 10 were waited for; matrix products, arithmetic and copies ran while one was open for 4% of the time, Pallas kernels for 21%

profile of v9, /device:TPU:0, one launch (start us, length us, event | category | flops | bytes accessed | tf_op | source)
XLA Modules:
  0.0 173.9 jit_solution(6903887779471099550)
XLA Ops:
  7.2 4.2 %dispatch.2 = bf16[1024,640]{1,0:T(8,128)(2,1)} custom-call(s32[384]{0:T(512)} %pos_ref.3, bf16[384,1536]{1,0:T(8,128)(2,1)} %rest_ref.1, bf16[384,1536]{1,0:T(8,128)(2,1)} %rest_ref.1, bf16[384,1536]{1,0:T(8,128)(2,1)} %rest_ref.1), custom_call_target="tpu_custom_call" | custom-call | tf_op jit(solution)/shard_map/dispatch/pallas_call | solution.py:45
  11.4 11.1 %all-to-all-start = ((bf16[128,8,640]{2,1,0:T(8,128)(2,1)}), bf16[128,8,640]{2,1,0:T(8,128)(2,1)S(1)}, u32[]{:S(2)}, u32[]{:S(2)}) async-start(bf16[128,8,640]{2,1,0:T(8,128)(2,1)} %bitcast.2), calls=%async_computation | async-start | bytes 2621440 | tf_op jit(solution)/shard_map/dispatch/all_to_all | solution.py:533
  22.6 21.7 %all-to-all-done = bf16[128,8,640]{2,1,0:T(8,128)(2,1)S(1)} async-done(((bf16[128,8,640]{2,1,0:T(8,128)(2,1)}), bf16[128,8,640]{2,1,0:T(8,128)(2,1)S(1)}, u32[]{:S(2)}, u32[]{:S(2)}) %all-to-all-start) | async-done | bytes 1310752 | tf_op jit(solution)/shard_map/dispatch/all_to_all | solution.py:533
  44.3 5.3 %project.1 = (bf16[128,768]{1,0:T(8,128)(2,1)}, bf16[128,1536]{1,0:T(8,128)(2,1)}, bf16[16,152,128]{2,1,0:T(8,128)(2,1)}, bf16[512,128]{1,0:T(8,128)(2,1)}) custom-call(s32[1]{0:T(128)} %bitcast.1.odd_ref, bf16[1024,640]{1,0:T(8,128)(2,1)S(1)} %bitcast.18, bf16[1536,768]{1,0:T(8,128)(2,1)} %embed_hbm_ref.1, bf16[768,2304]{1,0:T(8,128)(2,1)} %refs_0_.1), custom_call_target="tpu_custom_call" | custom-call | tf_op jit(solution)/shard_map/project/pallas_call | solution.py:45
  49.6 3.6 %all-to-all-start.1 = ((bf16[16,152,128]{2,1,0:T(8,128)(2,1)}), bf16[16,152,128]{2,1,0:T(8,128)(2,1)S(1)}, u32[]{:S(2)}, u32[]{:S(2)}) async-start(bf16[16,152,128]{2,1,0:T(8,128)(2,1)} %get-tuple-element.34), calls=%async_computation.1 | async-start | bytes 1245184 | tf_op jit(solution)/shard_map/project/all_to_all | solution.py:555
  54.4 13.0 %all-to-all-done.1.chunk_ref = bf16[16,152,128]{2,1,0:T(8,128)(2,1)S(1)} async-done(((bf16[16,152,128]{2,1,0:T(8,128)(2,1)}), bf16[16,152,128]{2,1,0:T(8,128)(2,1)S(1)}, u32[]{:S(2)}, u32[]{:S(2)}) %all-to-all-start.1) | async-done | bytes 622624 | tf_op jit(solution)/shard_map/project/all_to_all | solution.py:555
  68.7 3.6 %all-to-all-start.2 = ((bf16[8,96,256]{2,1,0:T(8,128)(2,1)}), bf16[8,96,256]{2,1,0:T(8,128)(2,1)S(1)}, u32[]{:S(2)}, u32[]{:S(2)}) async-start(bf16[8,96,256]{2,1,0:T(8,128)(2,1)} %get-tuple-element.39), calls=%async_computation.2 | async-start | bytes 786432 | tf_op jit(solution)/shard_map/dilated/all_to_all | solution.py:577
  72.4 7.0 %near.3 = (bf16[144,2048]{1,0:T(8,128)(2,1)S(1)}, f32[144,1024]{1,0:T(8,128)}, f32[2,128,1024]{2,1,0:T(8,128)S(1)}, f32[2,128,1024]{2,1,0:T(8,128)S(1)}) custom-call(s32[1]{0:T(128)} %bitcast.phase_ref, bf16[144,2048]{1,0:T(8,128)(2,1)} %get-tuple-element.37.rows_ref, s32[8,2048]{1,0:T(8,128)S(1)} %get-tuple-element.35.local_ref, ...), custom_call_target="tpu_custom_call" | custom-call | flops 8000000000 | bytes 8000000 | tf_op jit(solution)/shard_map/near/pallas_call | solution.py:45
  79.4 1.6 all-to-all-done.2.far_ref
  81.1 2.8 %far.1 = (bf16[8,96,256]{2,1,0:T(8,128)(2,1)}, bf16[2,128,2048]{2,1,0:T(8,128)(2,1)}, bf16[2,128,1024]{2,1,0:T(8,128)(2,1)}) custom-call(bf16[48,256]{1,0:T(8,128)(2,1)S(1)} %get-tuple-element.36.query_ref, bf16[48,256]{1,0:T(8,128)(2,1)S(1)} %near.2.dilated_grad_ref.grad_ref, f32[2,128,1024]{2,1,0:T(8,128)S(1)} %get-tuple-element.40.score_ref, ...), custom_call_target="tpu_custom_call" | custom-call | tf_op jit(solution)/shard_map/far/pallas_call | solution.py:45
  83.8 3.5 %all-to-all-start.3 = ((bf16[8,96,256]{2,1,0:T(8,128)(2,1)}), bf16[8,96,256]{2,1,0:T(8,128)(2,1)S(1)}, u32[]{:S(2)}, u32[]{:S(2)}) async-start(bf16[8,96,256]{2,1,0:T(8,128)(2,1)} %get-tuple-element.47), calls=%async_computation.3 | async-start | bytes 786432 | tf_op jit(solution)/shard_map/far/all_to_all | solution.py:601
  87.3 4.4 %unplace.3 = (bf16[48,256]{1,0:T(8,128)(2,1)S(1)}, bf16[144,2048]{1,0:T(8,128)(2,1)S(1)}) custom-call(s32[1]{0:T(128)} %bitcast.phase_ref, bf16[4,48,512]{2,1,0:T(8,128)(2,1)} %bitcast.23, bf16[48,256]{1,0:T(8,128)(2,1)S(1)} %get-tuple-element.36.query_ref, bf16[48,256]{1,0:T(8,128)(2,1)S(1)} %near.2.dilated_grad_ref.grad_ref, ...), custom_call_target="tpu_custom_call" | custom-call | tf_op jit(solution)/shard_map/unplace/pallas_call | solution.py:45
  91.6 1.5 unplace.4.main_ref
  93.1 3.0 %all-to-all-done.3.far_ref = bf16[8,96,256]{2,1,0:T(8,128)(2,1)S(1)} async-done(((bf16[8,96,256]{2,1,0:T(8,128)(2,1)}), bf16[8,96,256]{2,1,0:T(8,128)(2,1)S(1)}, u32[]{:S(2)}, u32[]{:S(2)}) %all-to-all-start.3) | async-done | bytes 393248 | tf_op jit(solution)/shard_map/far/all_to_all | solution.py:601
  96.1 1.4 unplace.5
  97.5 4.3 %all-to-all-start.4 = ((bf16[16,144,128]{2,1,0:T(8,128)(2,1)}), bf16[16,144,128]{2,1,0:T(8,128)(2,1)}, u32[]{:S(2)}, u32[]{:S(2)}) async-start(bf16[16,144,128]{2,1,0:T(8,128)(2,1)} %bitcast.5), calls=%async_computation.4 | async-start | bytes 1179648 | tf_op jit(solution)/shard_map/unplace/all_to_all | solution.py:630
  101.8 2.0 %tiles_grad.3.weight_ref = bf16[768,2304]{1,0:T(8,128)(2,1)S(1)} custom-call(bf16[144,2048]{1,0:T(8,128)(2,1)} %get-tuple-element.49._.grad_ref, bf16[768,2304]{1,0:T(8,128)(2,1)} %refs_0_.1), custom_call_target="tpu_custom_call" | custom-call | tf_op jit(solution)/shard_map/tiles_grad/pallas_call | solution.py:45
  103.8 10.3 %all-to-all-done.4 = bf16[16,144,128]{2,1,0:T(8,128)(2,1)} async-done(((bf16[16,144,128]{2,1,0:T(8,128)(2,1)}), bf16[16,144,128]{2,1,0:T(8,128)(2,1)}, u32[]{:S(2)}, u32[]{:S(2)}) %all-to-all-start.4) | async-done | bytes 589856 | tf_op jit(solution)/shard_map/unplace/all_to_all | solution.py:630
  114.1 3.9 %tiles_grad.4 = (bf16[768,128]{1,0:T(8,128)(2,1)}, bf16[1024,384]{1,0:T(8,128)(2,1)}) custom-call(bf16[2304,128]{1,0:T(8,128)(2,1)} %bitcast.6.rows_ref, bf16[768,2304]{1,0:T(8,128)(2,1)S(1)} %tiles_grad.3.weight_ref, bf16[512,128]{1,0:T(8,128)(2,1)} %get-tuple-element.50.pick_ref), custom_call_target="tpu_custom_call" | custom-call | tf_op jit(solution)/shard_map/tiles_grad/pallas_call | solution.py:45
  118.0 5.0 %all-to-all-start.5 = ((bf16[128,8,384]{2,1,0:T(8,128)(2,1)}), bf16[128,8,384]{2,1,0:T(8,128)(2,1)S(1)}, u32[]{:S(2)}, u32[]{:S(2)}) async-start(bf16[128,8,384]{2,1,0:T(8,128)(2,1)} %bitcast.24), calls=%async_computation.5 | async-start | bytes 1572864 | tf_op jit(solution)/shard_map/tiles_grad/all_to_all | solution.py:664
  126.6 2.7 %tiles_grad.5 = bf16[64,72,128]{2,1,0:T(8,128)(2,1)} custom-call(bf16[768,128]{1,0:T(8,128)(2,1)} %get-tuple-element.51.grad_ref, bf16[768,128]{1,0:T(8,128)(2,1)S(1)} %collective-permute-done.other_grad_ref, bf16[128,768]{1,0:T(8,128)(2,1)} %copy.12.keep_ref, bf16[128,768]{1,0:T(8,128)(2,1)} %copy-done.2), custom_call_target="tpu_custom_call" | custom-call | tf_op jit(solution)/shard_map/tiles_grad/pallas_call | solution.py:45
  129.3 9.8 %all-to-all-done.5 = bf16[128,8,384]{2,1,0:T(8,128)(2,1)S(1)} async-done(((bf16[128,8,384]{2,1,0:T(8,128)(2,1)}), bf16[128,8,384]{2,1,0:T(8,128)(2,1)S(1)}, u32[]{:S(2)}, u32[]{:S(2)}) %all-to-all-start.5) | async-done | bytes 786464 | tf_op jit(solution)/shard_map/tiles_grad/all_to_all | solution.py:664
  139.1 4.7 %all-to-all-start.6 = ((bf16[64,72,128]{2,1,0:T(8,128)(2,1)}), bf16[64,72,128]{2,1,0:T(8,128)(2,1)S(1)}, u32[]{:S(2)}, u32[]{:S(2)}) async-start(bf16[64,72,128]{2,1,0:T(8,128)(2,1)} %tiles_grad.5), calls=%async_computation.6 | async-start | bytes 2359296 | tf_op jit(solution)/shard_map/embed_grad/all_to_all | solution.py:681
  143.8 3.7 %qkv_grad.2 = (f32[4,96,256]{2,1,0:T(8,128)}, bf16[4,96,256]{2,1,0:T(8,128)(2,1)}) custom-call(s32[1]{0:T(128)} %bitcast.13.core_ref, bf16[144,2048]{1,0:T(8,128)(2,1)} %get-tuple-element.49._.grad_ref, bf16[2048,768]{1,0:T(8,128)(2,1)} %all-gather.2.cloned.1.call-done.rows_ref), custom_call_target="tpu_custom_call" | custom-call | tf_op jit(solution)/shard_map/qkv_grad/pallas_call | solution.py:45
  148.6 2.0 %collect.1 = bf16[384,768]{1,0:T(8,128)(2,1)} custom-call(bf16[1024,384]{1,0:T(8,128)(2,1)S(1)} %bitcast.19, s32[384,128]{1,0:T(8,128)S(1)} %dispatch.3.base_ref), custom_call_target="tpu_custom_call" | custom-call | tf_op jit(solution)/shard_map/collect/pallas_call | solution.py:45
  151.3 1.7 %qkv_grad.3 = (f32[96,256]{1,0:T(8,128)}, bf16[96,256]{1,0:T(8,128)(2,1)}, bf16[96,256]{1,0:T(8,128)(2,1)}, bf16[96,256]{1,0:T(8,128)(2,1)}) custom-call(s32[1]{0:T(128)} %bitcast.12.chip_ref, f32[4,96,256]{2,1,0:T(8,128)} %get-tuple-element.57.keep_ref, bf16[4,96,256]{2,1,0:T(8,128)(2,1)} %copy-done), custom_call_target="tpu_custom_call" | custom-call | tf_op jit(solution)/shard_map/qkv_grad/pallas_call | solution.py:45
  153.0 1.6 collective-permute-start.3
  154.6 2.9 %collective-permute-start.4 = (bf16[96,256]{1,0:T(8,128)(2,1)}, bf16[96,256]{1,0:T(8,128)(2,1)S(1)}, u32[]{:S(2)}, u32[]{:S(2)}) collective-permute-start(bf16[96,256]{1,0:T(8,128)(2,1)} %get-tuple-element.61), channel_id=1, source_target_pairs={{0,64},{16,80},{32,96},{48,112},{64,0},{80,16},{96,32},{112,48},{1... | collective-permute-start | bytes 147464 | tf_op jit(solution)/shard_map/qkv_grad/ppermute | solution.py:652
  157.5 1.4 collective-permute-start.5
  158.8 4.0 %convolution_convert_fusion = bf16[384,1536]{1,0:T(8,128)(2,1)} fusion(bf16[384,768]{1,0:T(8,128)(2,1)} %collect.1, bf16[1536,768]{1,0:T(8,128)(2,1)} %embed_hbm_ref.1), kind=kOutput, calls=%fused_computation | convolution fusion | flops 906559488 | bytes 4128768 | tf_op jit(solution)/shard_map/feature_grad/dot_general | solution.py:692
  162.8 1.6 all-to-all-done.6.parts_ref
  165.1 1.9 %embed_grad.1 = (f32[48,192]{1,0:T(8,128)}, f32[144,96]{1,0:T(8,128)}) custom-call(s32[1]{0:T(128)} %bitcast.12.chip_ref, bf16[64,72,128]{2,1,0:T(8,128)(2,1)S(1)} %all-to-all-done.6.parts_ref, f32[96,256]{1,0:T(8,128)} %get-tuple-element.59.own_ref, bf16[96,256]{1,0:T(8,128)(2,1)} %copy-done.3, bf16[96,256]{1,0:T(8,128)(2,1)} %copy-done.4, ...), custom_call_target="tpu_custom_call" | custom-call | tf_op jit(solution)/shard_map/embed_grad/pallas_call | solution.py:45
  (31 shorter events, 8.6 us)
Async XLA Ops:
  11.4 32.9 %all-to-all-start = ((bf16[128,8,640]{2,1,0:T(8,128)(2,1)}), bf16[128,8,640]{2,1,0:T(8,128)(2,1)S(1)}, u32[]{:S(2)}, u32[]{:S(2)}) async-start(bf16[128,8,640]{2,1,0:T(8,128)(2,1)} %bitcast.2), calls=%async_computation | async-start | bytes 2621440 | tf_op jit(solution)/shard_map/dispatch/all_to_all | solution.py:533
  22.5 121.3 %all-gather.2.cloned.1.call-start = ((), (), s32[]{:S(2)}) async-start(), calls=%async_computation.7 | async-start | bytes 3342336 | tf_op jit(solution)/shard_map/qkv_grad/all_gather | solution.py:634
  49.6 17.8 %all-to-all-start.1 = ((bf16[16,152,128]{2,1,0:T(8,128)(2,1)}), bf16[16,152,128]{2,1,0:T(8,128)(2,1)S(1)}, u32[]{:S(2)}, u32[]{:S(2)}) async-start(bf16[16,152,128]{2,1,0:T(8,128)(2,1)} %get-tuple-element.34), calls=%async_computation.1 | async-start | bytes 1245184 | tf_op jit(solution)/shard_map/project/all_to_all | solution.py:555
  68.7 12.3 %all-to-all-start.2 = ((bf16[8,96,256]{2,1,0:T(8,128)(2,1)}), bf16[8,96,256]{2,1,0:T(8,128)(2,1)S(1)}, u32[]{:S(2)}, u32[]{:S(2)}) async-start(bf16[8,96,256]{2,1,0:T(8,128)(2,1)} %get-tuple-element.39), calls=%async_computation.2 | async-start | bytes 786432 | tf_op jit(solution)/shard_map/dilated/all_to_all | solution.py:577
  83.8 12.3 %all-to-all-start.3 = ((bf16[8,96,256]{2,1,0:T(8,128)(2,1)}), bf16[8,96,256]{2,1,0:T(8,128)(2,1)S(1)}, u32[]{:S(2)}, u32[]{:S(2)}) async-start(bf16[8,96,256]{2,1,0:T(8,128)(2,1)} %get-tuple-element.47), calls=%async_computation.3 | async-start | bytes 786432 | tf_op jit(solution)/shard_map/far/all_to_all | solution.py:601
  97.5 16.6 %all-to-all-start.4 = ((bf16[16,144,128]{2,1,0:T(8,128)(2,1)}), bf16[16,144,128]{2,1,0:T(8,128)(2,1)}, u32[]{:S(2)}, u32[]{:S(2)}) async-start(bf16[16,144,128]{2,1,0:T(8,128)(2,1)} %bitcast.5), calls=%async_computation.4 | async-start | bytes 1179648 | tf_op jit(solution)/shard_map/unplace/all_to_all | solution.py:630
  118.0 6.5 %copy-start.1 = (bf16[768,128]{1,0:T(8,128)(2,1)S(1)}, bf16[768,128]{1,0:T(8,128)(2,1)}, u32[]{:S(2)}) copy-start(bf16[768,128]{1,0:T(8,128)(2,1)} %get-tuple-element.51.grad_ref) | copy-start | bytes 589828
  118.0 21.1 %all-to-all-start.5 = ((bf16[128,8,384]{2,1,0:T(8,128)(2,1)}), bf16[128,8,384]{2,1,0:T(8,128)(2,1)S(1)}, u32[]{:S(2)}, u32[]{:S(2)}) async-start(bf16[128,8,384]{2,1,0:T(8,128)(2,1)} %bitcast.24), calls=%async_computation.5 | async-start | bytes 1572864 | tf_op jit(solution)/shard_map/tiles_grad/all_to_all | solution.py:664
  124.4 1.5 collective-permute-start.1
  124.5 1.7 collective-permute-start
  126.0 0.7 copy-start.2
  139.1 25.3 %all-to-all-start.6 = ((bf16[64,72,128]{2,1,0:T(8,128)(2,1)}), bf16[64,72,128]{2,1,0:T(8,128)(2,1)S(1)}, u32[]{:S(2)}, u32[]{:S(2)}) async-start(bf16[64,72,128]{2,1,0:T(8,128)(2,1)} %tiles_grad.5), calls=%async_computation.6 | async-start | bytes 2359296 | tf_op jit(solution)/shard_map/embed_grad/all_to_all | solution.py:681
  147.6 3.0 %collective-permute-start.2 = (bf16[4,96,256]{2,1,0:T(8,128)(2,1)}, bf16[4,96,256]{2,1,0:T(8,128)(2,1)S(1)}, u32[]{:S(2)}, u32[]{:S(2)}) collective-permute-start(bf16[4,96,256]{2,1,0:T(8,128)(2,1)} %get-tuple-element.58), channel_id=1, source_target_pairs={{0,16},{16,0},{32,48},{48,32},{64,80},{80,64},{96,112},{112,96},{1... | collective-permute-start | bytes 589832 | tf_op jit(solution)/shard_map/qkv_grad/ppermute | solution.py:644
  150.6 0.7 copy-start
  153.0 11.3 %collective-permute-start.3 = (bf16[96,256]{1,0:T(8,128)(2,1)}, bf16[96,256]{1,0:T(8,128)(2,1)S(1)}, u32[]{:S(2)}, u32[]{:S(2)}) collective-permute-start(bf16[96,256]{1,0:T(8,128)(2,1)} %get-tuple-element.60), channel_id=1, source_target_pairs={{0,32},{16,48},{32,64},{48,80},{64,96},{80,112},{96,0},{112,16},{1... | collective-permute-start | bytes 147464 | tf_op jit(solution)/shard_map/qkv_grad/ppermute | solution.py:652
  154.6 9.9 %collective-permute-start.4 = (bf16[96,256]{1,0:T(8,128)(2,1)}, bf16[96,256]{1,0:T(8,128)(2,1)S(1)}, u32[]{:S(2)}, u32[]{:S(2)}) collective-permute-start(bf16[96,256]{1,0:T(8,128)(2,1)} %get-tuple-element.61), channel_id=1, source_target_pairs={{0,64},{16,80},{32,96},{48,112},{64,0},{80,16},{96,32},{112,48},{1... | collective-permute-start | bytes 147464 | tf_op jit(solution)/shard_map/qkv_grad/ppermute | solution.py:652
  157.5 7.0 %collective-permute-start.5 = (bf16[96,256]{1,0:T(8,128)(2,1)}, bf16[96,256]{1,0:T(8,128)(2,1)S(1)}, u32[]{:S(2)}, u32[]{:S(2)}) collective-permute-start(bf16[96,256]{1,0:T(8,128)(2,1)} %get-tuple-element.62), channel_id=1, source_target_pairs={{0,96},{16,112},{32,0},{48,16},{64,32},{80,48},{96,64},{112,80},{1... | collective-permute-start | bytes 147464 | tf_op jit(solution)/shard_map/qkv_grad/ppermute | solution.py:652
  164.4 0.6 copy-start.3
  164.5 0.6 copy-start.4
  164.5 0.6 copy-start.5
Sparse Core Ops, SparseCore 0:
  49.8 45.2 all-gather.1
